TPU v7x, 32 devices: a whole 2x2x4 slice. The times are simulated.
32 devices in a mesh: dp: 8 (over y, x, core), tensor: 4 (over z).
Axes of the slice: x: 2, y: 2, z: 4, core: 2. Of those that a mesh axis runs over, the one named last changes fastest.
Arguments:
- kv_part: bfloat16 [4, 2048, 12288], P('tensor', 'dp'), may hold values from -2 to 2
- queries: bfloat16 [4096, 6144], P('dp', 'tensor'), may hold values from -6 to 6
- w_out: bfloat16 [6144, 8192], P('tensor'), may hold values from -0.078125 to 0.078125
- d_out: bfloat16 [4096, 8192], P('dp', 'tensor'), may hold values from -48 to 48
- nbr_owner: int32 [64, 2], replicated, may hold values from 0 to 7, as said below
- nbr_slot: int32 [64, 2], replicated, may hold values from 0 to 1, as said below
Outputs:
- mixed: bfloat16 [4096, 8192], P('dp', 'tensor')
- d_kv: bfloat16 [2048, 12288], P('dp', 'tensor')
Inputs may be any that keep to these rules, and one draw needn't show every extreme that they name: `nbr_owner`: the two neighbours of one span have different owners. `nbr_slot`: all neighbours that the spans of one dp index r (spans r * 8 to (r + 1) * 8 - 1) take from one owner have the same slot.
All inputs are finite; a program needn't handle non-finite values.
Results may differ from a plain program's by a relative error of at most 0.025.
Values may be sent and summed in bfloat16 or wider, within the bound.
No kernel may reach another device: no remote copies, remote signals or barrier semaphores. Data moves between devices by JAX's collectives and lax.ppermute only.
A program may use at most 192 MiB of HBM per device.

v0:
```python
import jax
import jax.numpy as jnp
from jax import lax
from jax.sharding import PartitionSpec as P

HD = 128
SPAN = 64
NBR_LEN = 128
NB_DEV = 2


def local(kv_part, queries, w_out, d_out, nbr_owner, nbr_slot):
    dp_count = lax.axis_size("dp")
    reader = lax.axis_index("dp")
    head_width = w_out.shape[0]
    heads_here = head_width // HD
    share_width = 2 * head_width
    span_count = queries.shape[0] // SPAN
    read_count = 2 * span_count
    block_width = NBR_LEN * share_width
    local_partial = kv_part[0]
    summed = lax.psum(local_partial, "tensor").astype(jnp.float32)
    shares = lax.dynamic_slice_in_dim(
        summed, lax.axis_index("tensor") * share_width, share_width, 1
    ).astype(jnp.bfloat16)
    share_blocks = shares.reshape(NB_DEV, block_width)
    owner_ids = jnp.arange(dp_count, dtype=jnp.int32)
    slot_ids = jnp.arange(NB_DEV, dtype=jnp.int32)
    owner_hits = nbr_owner[:, :, None] == owner_ids[None, None, :]
    per_reader = owner_hits.reshape(dp_count, read_count, dp_count)
    reads_from = jnp.any(per_reader, axis=1)
    slot_from = jnp.max(jnp.where(per_reader, nbr_slot.reshape(dp_count, read_count, 1), 0), axis=1)
    my_owner = lax.dynamic_slice_in_dim(nbr_owner, reader * span_count, span_count, 0).reshape(
        read_count
    )
    my_slot = lax.dynamic_slice_in_dim(nbr_slot, reader * span_count, span_count, 0).reshape(
        read_count
    )
    read_table = (my_owner[:, None] == owner_ids[None, :]).astype(jnp.bfloat16)
    serving = lax.dynamic_index_in_dim(reads_from, reader, 1, False)
    serving_slot = lax.dynamic_index_in_dim(slot_from, reader, 1, False)
    owner_select = ((serving_slot[:, None] == slot_ids[None, :]) & serving[:, None]).astype(
        jnp.bfloat16
    )
    everyone = lax.all_gather(share_blocks, "dp", axis=0, tiled=True)
    wanted = (my_owner * NB_DEV + my_slot)[:, None] == jnp.arange(
        dp_count * NB_DEV, dtype=jnp.int32
    )[None, :]
    neighbours = jnp.dot(
        wanted.astype(jnp.bfloat16), everyone, preferred_element_type=jnp.float32
    ).astype(jnp.bfloat16)
    layout = neighbours.reshape(span_count, 2 * NBR_LEN, heads_here, 2, HD)
    keys = layout[:, :, :, 0]
    values = layout[:, :, :, 1]
    query_view = queries.reshape(span_count, SPAN, heads_here, HD)
    factor = HD ** (-0.5)
    scores = (
        jnp.einsum("cqhd,ckhd->chqk", query_view, keys, preferred_element_type=jnp.float32) * factor
    )
    highest = jnp.max(scores, axis=-1, keepdims=True)
    expo = jnp.exp(scores - highest)
    probs = expo / jnp.sum(expo, axis=-1, keepdims=True)
    probs_low = probs.astype(jnp.bfloat16)
    attended = jnp.einsum("chqk,ckhd->cqhd", probs_low, values, preferred_element_type=jnp.float32)
    attended = attended.astype(jnp.bfloat16).reshape(span_count * SPAN, head_width)
    partial_out = jnp.dot(attended, w_out, preferred_element_type=jnp.float32)
    mixed = lax.psum_scatter(
        partial_out.astype(jnp.bfloat16), "tensor", scatter_dimension=1, tiled=True
    )
    grad_attended = lax.dot_general(
        lax.all_gather(d_out, "tensor", axis=1, tiled=True),
        w_out,
        (((1,), (1,)), ((), ())),
        preferred_element_type=jnp.float32,
    ).astype(jnp.bfloat16)
    grad_view = grad_attended.reshape(span_count, SPAN, heads_here, HD)
    grad_values = jnp.einsum(
        "chqk,cqhd->ckhd", probs_low, grad_view, preferred_element_type=jnp.float32
    )
    grad_probs = jnp.einsum(
        "cqhd,ckhd->chqk", grad_view, values, preferred_element_type=jnp.float32
    )
    grad_scores = probs * (grad_probs - jnp.sum(probs * grad_probs, axis=-1, keepdims=True))
    grad_scores = grad_scores.astype(jnp.bfloat16)
    grad_keys = (
        jnp.einsum("chqk,cqhd->ckhd", grad_scores, query_view, preferred_element_type=jnp.float32)
        * factor
    )
    grad_blocks = jnp.stack([grad_keys, grad_values], axis=3).reshape(read_count, block_width)
    per_owner = lax.dot_general(
        read_table.astype(jnp.float32),
        grad_blocks,
        (((0,), (0,)), ((), ())),
        precision=lax.Precision.HIGHEST,
        preferred_element_type=jnp.float32,
    ).astype(jnp.bfloat16)
    returned = lax.all_to_all(per_owner, "dp", split_axis=0, concat_axis=0, tiled=True)
    owner_grad = lax.dot_general(
        owner_select, returned, (((0,), (0,)), ((), ())), preferred_element_type=jnp.float32
    )
    d_kv = owner_grad.astype(jnp.bfloat16).reshape(NB_DEV * NBR_LEN, share_width)
    return (mixed, d_kv)


def solution(mesh):
    placed = (
        P("tensor", "dp", None),
        P("dp", "tensor"),
        P("tensor", None),
        P("dp", "tensor"),
        P(),
        P(),
    )
    return jax.shard_map(
        local,
        mesh=mesh,
        in_specs=placed,
        out_specs=(P("dp", "tensor"), P("dp", "tensor")),
        check_vma=False,
    )
```

profile of v0, /device:TPU:0, one launch (start us, length us, event | category | flops | bytes accessed | tf_op | source)
XLA Modules:
  0.0 785.4 jit_solution(15067656395291653493)
XLA Ops:
  7.2 0.0 all-reduce.2.cloned.1.call-start
  7.2 0.7 all-reduce.2.cloned.1.call-update
  7.9 0.0 copy-start.4
  7.9 0.0 copy-start.6
  7.9 0.0 copy-start.3
  7.9 0.0 all-gather.6.cloned.1.call-start
  8.0 228.0 %all-reduce.2.cloned.1.call-done = bf16[256,12288]{1,0:T(8,128)(2,1)} async-done(((bf16[256,12288]{1,0:T(8,128)(2,1)}), bf16[256,12288]{1,0:T(8,128)(2,1)}) %all-reduce.2.cloned.1.call-update) | async-done | bytes 6291472 | tf_op jit(solution)/shard_map/psum | solution.py:22
  236.0 1.5 convert_convert_fusion
  237.5 2.3 reshape.62
  239.7 0.0 all-gather.6.cloned.1.call-update
  239.8 0.0 all-gather.4.cloned.1.call-start
  239.8 0.7 all-gather.4.cloned.1.call-update
  240.5 0.0 reduce-scatter.2.cloned.1.call-start
  240.6 0.0 copy-done.4
  240.6 0.0 copy-done.6
  240.6 0.1 constant_dynamic-slice_fusion
  240.7 0.1 copy.75
  240.7 0.1 reshape.54
  240.8 0.1 copy.74
  240.9 0.1 reshape.53
  241.0 0.0 copy-done.3
  241.0 2.1 reshape.57
  243.1 67.9 %all-gather.6.cloned.1.call-done = bf16[8,2,393216]{2,1,0:T(2,128)(2,1)} async-done(((bf16[1,2,393216]{2,1,0:T(2,128)(2,1)}), bf16[8,2,393216]{2,1,0:T(2,128)(2,1)}) %all-gather.6.cloned.1.call-update) | async-done | bytes 12582928 | tf_op jit(solution)/shard_map/all_gather | solution.py:45
  311.0 16.4 %reshape.63 = bf16[16,393216]{1,0:T(8,128)(2,1)} reshape(bf16[8,2,393216]{2,1,0:T(2,128)(2,1)} %all-gather.6.cloned.1.call-done) | data formatting | bytes 25165824
  327.4 0.0 copy-done.8
  327.4 12.6 %convolution_convert_fusion = bf16[16,393216]{1,0:T(8,128)(2,1)} fusion(bf16[16,393216]{1,0:T(8,128)(2,1)} %reshape.63, s32[16]{0:T(128)S(1)} %multiply_add_fusion), kind=kOutput, calls=%fused_computation.1 | convolution fusion | flops 207618304 | bytes 25165888 | tf_op jit(solution)/shard_map/dot_general | solution.py:49
  340.0 24.0 %reshape.56 = bf16[8,256,12,2,128]{4,3,2,1,0:T(2,128)(2,1)} reshape(bf16[16,393216]{1,0:T(8,128)(2,1)} %convolution_convert_fusion) | data formatting | bytes 25165824 | tf_op jit(solution)/shard_map/reshape | solution.py:52
  364.0 25.6 %fusion.46 = (bf16[8,256,12,1,128]{4,3,2,1,0:T(2,128)(2,1)}, bf16[8,256,12,1,128]{4,3,2,1,0:T(2,128)(2,1)}) fusion(bf16[8,256,12,2,128]{4,3,2,1,0:T(2,128)(2,1)} %reshape.56), kind=kLoop, calls=%fused_computation.55 | loop fusion | bytes 25165824 | tf_op jit(solution)/shard_map/slice | solution.py:53
  389.6 7.5 fusion.2
  397.1 4.3 fusion.47
  401.4 0.2 copy-done
  401.6 15.9 %fusion.19 = bf16[8,64,12,128]{3,1,2,0:T(8,128)(2,1)S(1)} fusion(bf16[8,256,12,1,128]{4,3,2,1,0:T(2,128)(2,1)} %get-tuple-element.3, f32[8,12,64]{2,1,0:T(8,128)S(1)} %get-tuple-element.4, f32[8,12,256,64]{2,3,1,0:T(8,128)} %copy-done), kind=kOutput, calls=%fused_computation.33 | convolution fusion | flops 411310336 | bytes 14180352 | tf_op jit(solution)/shard_map/chqk,ckhd->cqhd/dot_general | solution.py:64
  417.5 1.1 copy.79
  418.6 19.9 %convolution_convert_fusion.3 = bf16[512,8192]{1,0:T(8,128)(2,1)} fusion(bf16[1536,8192]{1,0:T(8,128)(2,1)} %param.8, bf16[64,8,12,128]{3,2,1,0:T(8,128)(2,1)S(1)} %bitcast.75), kind=kOutput, calls=%fused_computation.7 | convolution fusion | flops 12889096192 | bytes 35127296 | tf_op jit(solution)/shard_map/dot_general | solution.py:66
  438.5 0.0 reduce-scatter.2.cloned.1.call-update
  438.5 23.7 %all-gather.4.cloned.1.call-done = bf16[512,8192]{1,0:T(8,128)(2,1)} async-done(((bf16[512,2048]{1,0:T(8,128)(2,1)}), bf16[512,8192]{1,0:T(8,128)(2,1)}) %all-gather.4.cloned.1.call-update) | async-done | bytes 8388624 | tf_op jit(solution)/shard_map/all_gather | solution.py:71
  462.2 20.5 %convolution_convert_fusion.4 = bf16[512,1536]{1,0:T(8,128)(2,1)} fusion(bf16[512,8192]{1,0:T(8,128)(2,1)} %all-gather.4.cloned.1.call-done, bf16[1536,8192]{1,0:T(8,128)(2,1)} %param.8), kind=kOutput, calls=%fused_computation.25 | convolution fusion | flops 12885688320 | bytes 35127296 | tf_op jit(solution)/shard_map/dot_general | solution.py:70
  482.8 2.9 reshape.59
  485.7 0.0 copy-start.2
  485.7 20.2 %convolution_bitcast_fusion = f32[8,256,12,1,128]{4,1,2,0,3:T(8,128)} fusion(bf16[8,64,12,128]{3,2,1,0:T(8,128)(2,1)S(1)} %reshape.59, f32[8,12,64]{2,1,0:T(8,128)S(1)} %get-tuple-element.4, f32[8,12,256,64]{2,3,1,0:T(8,128)} %copy-done), kind=kOutput, calls=%fused_computation.20 | convolution fusion | flops 410523904 | bytes 20471808 | tf_op jit(solution)/shard_map/chqk,cqhd->ckhd/dot_general | solution.py:77
  505.9 12.8 %multiply_reduce_fusion = (f32[8,12,64]{2,1,0:T(8,128)S(1)}, f32[8,12,64,256]{3,2,1,0:T(8,128)}) fusion(f32[8,12,64,256]{3,2,1,0:T(8,128)} %get-tuple-element.5, f32[8,12,64]{2,1,0:T(8,128)S(1)} %get-tuple-element.4, bf16[8,256,12,1,128]{4,3,2,1,0:T(2,128)(2,1)} %get-tuple-element.3, bf16[8,64,12,128]{3,2,1,0:T(8,128)(2,1)} %copy-done.2), kind=kOutput, calls=%fused_computation.18 | convolution fusion | flops 407365632 | bytes 20496384 | tf_op jit(solution)/shard_map/cqhd,ckhd->chqk/dot_general | solution.py:80
  518.7 19.0 %multiply_bitcast_fusion = f32[8,256,12,1,128]{4,1,2,0,3:T(8,128)} fusion(f32[8,12,64,256]{3,2,1,0:T(8,128)} %get-tuple-element.7, f32[8,12,64]{2,1,0:T(8,128)S(1)} %get-tuple-element.6, bf16[8,64,12,128]{3,2,1,0:T(8,128)(2,1)S(1)} %copy-done.1, f32[8,12,64]{2,1,0:T(8,128)S(1)} %get-tuple-element.4, f32[8,12,256,64]{2,3,1,0:T(8,128)} %copy-done), kind=kOutput, calls=%fused_computation.6 | convolution fusion | flops 416815360 | bytes 26787840 | tf_op jit(solution)/shard_map/chqk,cqhd->ckhd/dot_general | solution.py:86
  537.7 17.5 %pad_maximum_fusion = f32[8,256,12,2,128]{4,1,2,0,3:T(8,128)} fusion(f32[8,256,12,1,128]{4,1,2,0,3:T(8,128)} %convolution_bitcast_fusion, f32[8,256,12,1,128]{4,1,2,0,3:T(8,128)} %multiply_bitcast_fusion), kind=kLoop, calls=%fused_computation.5 | loop fusion | flops 6291456 | bytes 50331648 | tf_op jit(solution)/shard_map/stack | solution.py:89
  555.3 42.1 %copy.86 = f32[8,256,12,2,128]{4,3,2,1,0:T(2,128)} copy(f32[8,256,12,2,128]{4,1,2,0,3:T(8,128)} %pad_maximum_fusion) | data formatting | bytes 50331648 | tf_op jit(solution)/shard_map/stack | solution.py:89
  597.3 42.0 %reshape.60 = f32[16,393216]{1,0:T(8,128)} reshape(f32[8,256,12,2,128]{4,3,2,1,0:T(2,128)} %copy.86) | data formatting | bytes 50331648 | tf_op jit(solution)/shard_map/reshape | solution.py:89
  639.3 15.0 %fusion.1 = bf16[8,1,393216]{2,0,1:T(8,128)(2,1)} fusion(f32[16,393216]{1,0:T(8,128)} %reshape.60, s32[16]{0:T(128)S(1)} %copy-done.9), kind=kOutput, calls=%fused_computation.3 | convolution fusion | flops 607125632 | bytes 31457344 | tf_op jit(solution)/shard_map/dot_general | solution.py:90
  654.3 0.5 broadcast.20
  654.8 9.2 %reduce.4 = bf16[8,393216]{1,0:T(8,128)(2,1)} reduce(bf16[8,1,393216]{2,0,1:T(8,128)(2,1)} %fusion.1, bf16[]{:T(256)} %broadcast.20), dimensions={1}, to_apply=%copy.87.reduce_sub_computation | reduce | bytes 12582914 | tf_op jit(solution)/shard_map/all_to_all | solution.py:97
  664.0 11.4 %reshape.67 = bf16[8,2,196608]{2,1,0:T(2,128)(2,1)} reshape(bf16[8,393216]{1,0:T(8,128)(2,1)} %reduce.4) | data formatting | bytes 12582912
  675.4 5.2 all-to-all-start
  680.7 0.0 copy-done.5
  680.7 0.1 copy.81
  680.8 0.0 copy-done.7
  680.8 0.1 copy.80
  680.9 0.1 broadcast_in_dim.14
  680.9 0.1 eq.60
  681.0 0.2 select_reduce_fusion
  681.2 0.2 dynamic-slice_reduce_fusion
  681.4 0.2 fusion.26
  681.6 0.2 dynamic-slice_reduce_fusion.1
  681.8 70.4 %all-to-all-done = bf16[8,2,196608]{2,1,0:T(2,128)(2,1)} async-done(((bf16[8,2,196608]{2,1,0:T(2,128)(2,1)}), bf16[8,2,196608]{2,1,0:T(2,128)(2,1)}, u32[]{:S(2)}, u32[]{:S(2)}) %all-to-all-start) | async-done | bytes 6291488 | tf_op jit(solution)/shard_map/all_to_all | solution.py:97
  752.3 10.9 %reshape.68 = bf16[8,1,393216]{2,1,0:T(2,128)(2,1)} reshape(bf16[8,2,196608]{2,1,0:T(2,128)(2,1)} %all-to-all-done) | data formatting | bytes 12582912
  763.2 12.5 %convolution_convert_fusion.2 = bf16[2,393216]{1,0:T(2,128)(2,1)S(1)} fusion(bf16[8,1,393216]{2,1,0:T(2,128)(2,1)} %reshape.68, s32[8]{0:T(128)S(1)} %dynamic-slice_reduce_fusion, pred[8]{0:T(512)(128)(4,1)S(1)} %dynamic-slice_reduce_fusion.1), kind=kOutput, calls=%fused_computation.4 | convolution fusion | flops 13369376 | bytes 7864360 | tf_op jit(solution)/shard_map/dot_general | solution.py:98
  775.7 2.6 reshape.61
  (11 shorter events, 0.0 us)
Async XLA Ops:
  7.2 228.8 %all-reduce.2.cloned.1.call-start = ((), (), s32[]{:S(2)}) async-start(), calls=%async_computation.2 | async-start | bytes 12582912 | tf_op jit(solution)/shard_map/psum | solution.py:22
  7.9 232.7 %copy-start.4 = (s32[64,2]{0,1:T(2,128)S(1)}, s32[64,2]{0,1:T(2,128)}, u32[]{:S(2)}) copy-start(s32[64,2]{0,1:T(2,128)} %param.11) | copy-start | bytes 1540
  7.9 232.7 %copy-start.6 = (s32[64,2]{0,1:T(2,128)S(1)}, s32[64,2]{0,1:T(2,128)}, u32[]{:S(2)}) copy-start(s32[64,2]{0,1:T(2,128)} %param.10) | copy-start | bytes 1540
  7.9 233.1 %copy-start.3 = (bf16[512,1536]{1,0:T(8,128)(2,1)S(1)}, bf16[512,1536]{1,0:T(8,128)(2,1)}, u32[]{:S(2)}) copy-start(bf16[512,1536]{1,0:T(8,128)(2,1)} %param.7) | copy-start | bytes 4718596
  7.9 303.1 %all-gather.6.cloned.1.call-start = ((), (), s32[]{:S(2)}) async-start(), calls=%async_computation.5 | async-start | bytes 14155776 | tf_op jit(solution)/shard_map/all_gather | solution.py:45
  239.8 222.5 %all-gather.4.cloned.1.call-start = ((), (), s32[]{:S(2)}) async-start(), calls=%async_computation.4 | async-start | bytes 10485760 | tf_op jit(solution)/shard_map/all_gather | solution.py:71
  240.5 537.9 %reduce-scatter.2.cloned.1.call-start = ((), (), s32[]{:S(2)}) async-start(), calls=%async_computation.3 | async-start | bytes 10485760 | tf_op jit(solution)/shard_map/reduce_scatter | solution.py:67
  241.0 86.4 %copy-start.8 = (s32[16]{0:T(128)}, s32[16]{0:T(128)S(1)}, u32[]{:S(2)}) copy-start(s32[16]{0:T(128)S(1)} %reshape.53) | copy-start | bytes 196
  397.1 4.5 copy-start
  485.7 20.2 %copy-start.2 = (bf16[8,64,12,128]{3,2,1,0:T(8,128)(2,1)}, bf16[8,64,12,128]{3,2,1,0:T(8,128)(2,1)S(1)}, u32[]{:S(2)}) copy-start(bf16[8,64,12,128]{3,2,1,0:T(8,128)(2,1)S(1)} %reshape.59) | copy-start | bytes 4718596
  505.9 12.9 %copy-start.1 = (bf16[8,64,12,128]{3,2,1,0:T(8,128)(2,1)S(1)}, bf16[8,64,12,128]{3,2,1,0:T(8,128)(2,1)}, u32[]{:S(2)}) copy-start(bf16[8,64,12,128]{3,2,1,0:T(8,128)(2,1)} %reshape.57) | copy-start | bytes 4718596
  597.3 42.0 %copy-start.9 = (s32[16]{0:T(128)S(1)}, s32[16]{0:T(128)}, u32[]{:S(2)}) copy-start(s32[16]{0:T(128)} %copy-done.8) | copy-start | bytes 196
  675.4 5.2 copy-start.5
  675.4 5.3 copy-start.7
  675.4 76.8 %all-to-all-start = ((bf16[8,2,196608]{2,1,0:T(2,128)(2,1)}), bf16[8,2,196608]{2,1,0:T(2,128)(2,1)}, u32[]{:S(2)}, u32[]{:S(2)}) async-start(bf16[8,2,196608]{2,1,0:T(2,128)(2,1)} %reshape.67), calls=%async_computation.1 | async-start | bytes 12582912 | tf_op jit(solution)/shard_map/all_to_all | solution.py:97
Sparse Core Ops, SparseCore 0:
  10.4 225.5 all-reduce.1
  239.9 71.0 all-gather.5
  312.6 149.6 all-gather.3
  465.0 142.6 reduce-scatter.1
where the time goes:
time: 792 us; the launch traced here: 785 us
  waiting for transfers between devices  391 us (49%)
  local copies, waits for them, and re-layouts  185 us (23%)
  matrix products  156 us (20%)
  other arithmetic  33 us (4%)
  between operations  14.4 us (2%)
    psum x1, waiting for transfers between devices, local(): summed = lax.psum(local_partial, 'tensor').astype(jnp.float32)  228 us
    all_to_all x1, waiting for transfers between devices, local(): lax.all_to_all(per_owner, 'dp', split_axis=0, concat_axis=0, tiled=True)  70.4 us
    all_gather x1, waiting for transfers between devices, local(): everyone = lax.all_gather(share_blocks, 'dp', axis=0, tiled=True)  67.9 us
    another operation x1, local copies, waits for them, and re-layouts, local(): jnp.stack([grad_keys, grad_values], axis=3).reshape(read_count, block_width)  42.1 us
    reshape x1, local copies, waits for them, and re-layouts, local(): jnp.stack([grad_keys, grad_values], axis=3).reshape(read_count, block_width)  42 us
    unnamed x26, local copies, waits for them, and re-layouts  41.4 us
    slice x1, local copies, waits for them, and re-layouts, local(): keys = layout[:, :, :, 0]  25.6 us
    reshape x1, local copies, waits for them, and re-layouts, local(): layout = neighbours.reshape(span_count, 2 * NBR_LEN, heads_here, 2, HD)  24 us
  transfers between devices with their start and end apart: 5, of which 4 were waited for; matrix products, arithmetic and copies ran while one was open for 47% of the time, Pallas kernels for 0%

commit v1 on v0

v1 whole, which is shorter than its diff:
```python
import functools

import jax
import jax.numpy as jnp
from jax import lax
from jax.experimental import pallas as pl
from jax.experimental.pallas import tpu as pltpu
from jax.sharding import PartitionSpec as P

HD = 128
SPAN = 64
NBR_LEN = 128
NB_DEV = 2
NT = (((1,), (1,)), ((), ()))
BIG_VMEM = 56 * 1024 * 1024


def pair_of(first, second, column):
    return jnp.concatenate(
        [first[0, :, column : column + HD], second[0, :, column : column + HD]], axis=0
    )


def attend_kernel(heads, ids_ref, q_ref, first_ref, second_ref, out_ref):
    del ids_ref
    for head in range(heads):
        at = head * HD
        keys = pair_of(first_ref, second_ref, 2 * at)
        values = pair_of(first_ref, second_ref, 2 * at + HD)
        scores = lax.dot_general(
            q_ref[:, at : at + HD], keys, NT, preferred_element_type=jnp.float32
        ) * (HD**-0.5)
        expo = jnp.exp(scores - jnp.max(scores, axis=1, keepdims=True))
        probs = expo / jnp.sum(expo, axis=1, keepdims=True)
        out = jnp.dot(probs.astype(jnp.bfloat16), values, preferred_element_type=jnp.float32)
        out_ref[:, at : at + HD] = out.astype(jnp.bfloat16)


def attend(ids, queries, blocks):
    tokens, width = queries.shape
    spans = tokens // SPAN
    share = blocks.shape[2]
    return pl.pallas_call(
        functools.partial(attend_kernel, width // HD),
        grid_spec=pltpu.PrefetchScalarGridSpec(
            num_scalar_prefetch=1,
            grid=(spans,),
            in_specs=[
                pl.BlockSpec((SPAN, width), lambda c, ids: (c, 0)),
                pl.BlockSpec((1, NBR_LEN, share), lambda c, ids: (ids[2 * c], 0, 0)),
                pl.BlockSpec((1, NBR_LEN, share), lambda c, ids: (ids[2 * c + 1], 0, 0)),
            ],
            out_specs=pl.BlockSpec((SPAN, width), lambda c, ids: (c, 0)),
        ),
        out_shape=jax.ShapeDtypeStruct((tokens, width), jnp.bfloat16),
        compiler_params=pltpu.CompilerParams(vmem_limit_bytes=BIG_VMEM),
        cost_estimate=pl.CostEstimate(
            flops=8 * tokens * NBR_LEN * width,
            bytes_accessed=4 * tokens * width + 4 * spans * NBR_LEN * share,
            transcendentals=2 * tokens * NBR_LEN * width // HD,
        ),
        name="attend",
    )(ids, queries, blocks, blocks)


def attend_grad_kernel(
    heads, ids_ref, own_ref, q_ref, g_ref, first_ref, second_ref, out_ref, total_ref
):
    del ids_ref
    span = pl.program_id(1)

    @pl.when(span == 0)
    def _():
        total_ref[...] = jnp.zeros_like(total_ref)

    owner_a = own_ref[2 * span]
    owner_b = own_ref[2 * span + 1]
    factor = HD**-0.5
    for head in range(heads):
        at = head * HD
        query = q_ref[:, at : at + HD]
        grad = g_ref[:, at : at + HD]
        keys = pair_of(first_ref, second_ref, 2 * at)
        values = pair_of(first_ref, second_ref, 2 * at + HD)
        scores = lax.dot_general(keys, query, NT, preferred_element_type=jnp.float32) * factor
        expo = jnp.exp(scores - jnp.max(scores, axis=0, keepdims=True))
        probs = expo / jnp.sum(expo, axis=0, keepdims=True)
        grad_probs = lax.dot_general(values, grad, NT, preferred_element_type=jnp.float32)
        inner = jnp.sum(probs * grad_probs, axis=0, keepdims=True)
        grad_scores = (probs * (grad_probs - inner)).astype(jnp.bfloat16)
        grad_keys = jnp.dot(grad_scores, query, preferred_element_type=jnp.float32) * factor
        grad_values = jnp.dot(
            probs.astype(jnp.bfloat16), grad, preferred_element_type=jnp.float32
        )
        key_at = slice(2 * at, 2 * at + HD)
        value_at = slice(2 * at + HD, 2 * at + 2 * HD)
        total_ref[owner_a, :, key_at] += grad_keys[:NBR_LEN]
        total_ref[owner_b, :, key_at] += grad_keys[NBR_LEN:]
        total_ref[owner_a, :, value_at] += grad_values[:NBR_LEN]
        total_ref[owner_b, :, value_at] += grad_values[NBR_LEN:]

    @pl.when(span == pl.num_programs(1) - 1)
    def _():
        out_ref[...] = total_ref[...].astype(jnp.bfloat16)


def attend_grad(ids, owners, owner_count, queries, grads, blocks, groups):
    tokens, width = queries.shape
    spans = tokens // SPAN
    share = blocks.shape[2]
    part, share_part = width // groups, share // groups
    return pl.pallas_call(
        functools.partial(attend_grad_kernel, part // HD),
        grid_spec=pltpu.PrefetchScalarGridSpec(
            num_scalar_prefetch=2,
            grid=(groups, spans),
            in_specs=[
                pl.BlockSpec((SPAN, part), lambda g, c, ids, own: (c, g)),
                pl.BlockSpec((SPAN, part), lambda g, c, ids, own: (c, g)),
                pl.BlockSpec(
                    (1, NBR_LEN, share_part), lambda g, c, ids, own: (ids[2 * c], 0, g)
                ),
                pl.BlockSpec(
                    (1, NBR_LEN, share_part), lambda g, c, ids, own: (ids[2 * c + 1], 0, g)
                ),
            ],
            out_specs=pl.BlockSpec(
                (owner_count, NBR_LEN, share_part), lambda g, c, ids, own: (0, 0, g)
            ),
            scratch_shapes=[pltpu.VMEM((owner_count, NBR_LEN, share_part), jnp.float32)],
        ),
        out_shape=jax.ShapeDtypeStruct((owner_count, NBR_LEN, share), jnp.bfloat16),
        compiler_params=pltpu.CompilerParams(vmem_limit_bytes=BIG_VMEM),
        cost_estimate=pl.CostEstimate(
            flops=20 * tokens * NBR_LEN * width,
            bytes_accessed=4 * tokens * width
            + 4 * spans * NBR_LEN * share
            + 2 * owner_count * NBR_LEN * share,
            transcendentals=2 * tokens * NBR_LEN * width // HD,
        ),
        name="attend_grad",
    )(ids, owners, queries, grads, blocks, blocks)


def line_reduce_scatter(term, me, count, chunks):
    right = [None] * chunks
    left = [None] * chunks
    for step in range(1, count):
        rightward = [(i, i + 1) for i in range(step)]
        leftward = [(i, i - 1) for i in range(count - step, count)]
        to_right = me + count - step
        to_left = me - count + step
        for c in range(chunks):
            if 2 * step <= count:
                total = term(c, jnp.where(me < step, to_right, jnp.maximum(to_left, 0)))
                if step > 1:
                    total = total + right[c].astype(jnp.float32) + left[c].astype(jnp.float32)
                total = total.astype(jnp.bfloat16)
                right_total, left_total = total, total
            else:
                right_total = term(c, jnp.minimum(to_right, count - 1))
                right_total = (right_total + right[c].astype(jnp.float32)).astype(jnp.bfloat16)
                left_total = term(c, jnp.maximum(to_left, 0))
                left_total = (left_total + left[c].astype(jnp.float32)).astype(jnp.bfloat16)
            right[c] = lax.ppermute(right_total, "tensor", rightward)
            left[c] = lax.ppermute(left_total, "tensor", leftward)
    return [
        term(c, me) + right[c].astype(jnp.float32) + left[c].astype(jnp.float32)
        for c in range(chunks)
    ]


def line_all_gather(block, count):
    right, left = [block], [block]
    for step in range(1, count):
        rightward = [(i, i + 1) for i in range(step - 1, count - 1)]
        leftward = [(i, i - 1) for i in range(1, count - step + 1)]
        right.append(lax.ppermute(right[-1], "tensor", rightward))
        left.append(lax.ppermute(left[-1], "tensor", leftward))
    return [block] + [left[s] + right[count - s] for s in range(1, count)]


def local(kv_part, queries, w_out, d_out, nbr_owner, nbr_slot):
    dp_count = lax.axis_size("dp")
    tensor_count = lax.axis_size("tensor")
    reader = lax.axis_index("dp")
    me = lax.axis_index("tensor")
    tokens, head_width = queries.shape
    share_width = 2 * head_width
    span_count = tokens // SPAN
    read_count = 2 * span_count
    out_width = d_out.shape[1]

    owner_ids = jnp.arange(dp_count, dtype=jnp.int32)
    per_reader = (nbr_owner[:, :, None] == owner_ids[None, None, :]).reshape(
        dp_count, read_count, dp_count
    )
    slot_from = jnp.max(
        jnp.where(per_reader, nbr_slot.reshape(dp_count, read_count, 1), 0), axis=1
    )
    serving_slot = lax.dynamic_index_in_dim(slot_from, reader, 1, False)
    owners = lax.dynamic_slice_in_dim(nbr_owner, reader * span_count, span_count, 0).reshape(
        read_count
    )
    slots = lax.dynamic_slice_in_dim(nbr_slot, reader * span_count, span_count, 0).reshape(
        read_count
    )
    ids = owners * NB_DEV + slots

    def kv_term(chunk, shard):
        rows = kv_part[0, chunk * NBR_LEN : (chunk + 1) * NBR_LEN]
        return lax.dynamic_slice_in_dim(rows, shard * share_width, share_width, 1).astype(
            jnp.float32
        )

    summed = line_reduce_scatter(kv_term, me, tensor_count, NB_DEV)
    share = jnp.stack([part.astype(jnp.bfloat16) for part in summed])
    blocks = lax.all_gather(share, "dp", axis=0, tiled=True)

    attended = attend(ids, queries, blocks)
    row_chunks = 2
    rows = tokens // row_chunks

    def mixed_term(chunk, shard):
        weights = lax.dynamic_slice_in_dim(w_out, shard * out_width, out_width, 1)
        return jnp.dot(
            attended[chunk * rows : (chunk + 1) * rows],
            weights,
            preferred_element_type=jnp.float32,
        )

    mixed = line_reduce_scatter(mixed_term, me, tensor_count, row_chunks)
    mixed = jnp.concatenate([part.astype(jnp.bfloat16) for part in mixed])

    grads = []
    for chunk in range(row_chunks):
        pieces = line_all_gather(d_out[chunk * rows : (chunk + 1) * rows], tensor_count)
        total = jnp.zeros((rows, head_width), jnp.float32)
        for s in [0] + sorted(range(1, tensor_count), key=lambda s: abs(2 * s - tensor_count)):
            weights = lax.dynamic_slice_in_dim(
                w_out, lax.rem(me + s, tensor_count) * out_width, out_width, 1
            )
            total = total + lax.dot_general(
                pieces[s], weights, NT, preferred_element_type=jnp.float32
            )
        grads.append(total.astype(jnp.bfloat16))
    grad_attended = jnp.concatenate(grads)
    per_owner = attend_grad(ids, owners, dp_count, queries, grad_attended, blocks, 2)
    returned = lax.all_to_all(per_owner, "dp", split_axis=0, concat_axis=0, tiled=True)
    picked = [
        jnp.sum(
            jnp.where((serving_slot == slot)[:, None, None], returned.astype(jnp.float32), 0.0),
            axis=0,
        )
        for slot in range(NB_DEV)
    ]
    d_kv = jnp.concatenate(picked).astype(jnp.bfloat16)
    return (mixed, d_kv)


def solution(mesh):
    placed = (
        P("tensor", "dp", None),
        P("dp", "tensor"),
        P("tensor", None),
        P("dp", "tensor"),
        P(),
        P(),
    )
    return jax.shard_map(
        local,
        mesh=mesh,
        in_specs=placed,
        out_specs=(P("dp", "tensor"), P("dp", "tensor")),
        check_vma=False,
    )
```

time: 792 us -> 503 us (0.64)
  waiting for transfers between devices: 391 us -> 176 us
  local copies, waits for them, and re-layouts: 185 us -> 12.5 us
  starting transfers between devices: 5.37 us -> 101 us
  Pallas kernels: 0 us -> 73 us
  matrix products: 156 us -> 87.8 us
    psum x1 -> x0, waiting for transfers between devices: 228 us -> none  [local(): summed = lax.psum(local_partial, 'tensor').astype(jnp.float32)]
    ppermute x0 -> x36, waiting for transfers between devices: none -> 176 us  [the longest x6 86.3 us: line_all_gather(): left.append(lax.ppermute(left[-1], 'tensor', leftward))]
    ppermute x0 -> x36, starting transfers between devices: none -> 96.5 us  [the longest x12 54.6 us: line_reduce_scatter(): right[c] = lax.ppermute(right_total, 'tensor', rightward)]
    all_gather x2 -> x1, waiting for transfers between devices: 91.6 us -> 0.02 us  [local(): blocks = lax.all_gather(share, 'dp', axis=0, tiled=True)]
    reshape x5 -> x0, local copies, waits for them, and re-layouts: 73.7 us -> none  [the longest x1 42 us: local(): jnp.stack([grad_keys, grad_values], axis=3).reshape(read_count, block_width)]
    pallas_call x0 -> x2, Pallas kernels: none -> 73 us  [the longest x1 38.1 us: attend_grad(): pl.pallas_call(functools.partial(attend_grad_kernel, part // HD), grid_sp...]
    all_to_all x1, waiting for transfers between devices: 70.4 us -> 0.01 us  [local(): lax.all_to_all(per_owner, 'dp', split_axis=0, concat_axis=0, tiled=True)]
    dot_general x10 -> x18, matrix products: 156 us -> 87.8 us  [the longest x10 46.8 us: mixed_term(): jnp.dot(attended[chunk * rows:(chunk + 1) * rows], weights, preferred_ele...]
  transfers between devices with their start and end apart: 5 -> 38, of which waited for: 4 -> 18; matrix products, arithmetic and copies ran while one was open for 47% -> 22% of each run, Pallas kernels for 0% -> 15%
where the time goes in v1:
time: 503 us; the launch traced here: 494 us
  waiting for transfers between devices  176 us (35%)
  starting transfers between devices  101 us (20%)
  matrix products  87.8 us (17%)
  Pallas kernels  73 us (15%)
  other arithmetic  28.1 us (6%)
  between operations  15 us (3%)
  local copies, waits for them, and re-layouts  12.5 us (2%)
    ppermute x6, waiting for transfers between devices, line_all_gather(): left.append(lax.ppermute(left[-1], 'tensor', leftward))  86.3 us
    ppermute x12, waiting for transfers between devices, line_reduce_scatter(): right[c] = lax.ppermute(right_total, 'tensor', rightward)  83.3 us
    ppermute x12, starting transfers between devices, line_reduce_scatter(): right[c] = lax.ppermute(right_total, 'tensor', rightward)  54.6 us
    dot_general x10, matrix products, mixed_term(): jnp.dot(attended[chunk * rows:(chunk + 1) * rows], weights, preferred_ele...  46.8 us
    dot_general x8, matrix products, local(): lax.dot_general(pieces[s], weights, NT, preferred_element_type=jnp.float32)  41 us
    pallas_call x1, Pallas kernels, attend_grad(): pl.pallas_call(functools.partial(attend_grad_kernel, part // HD), grid_sp...  38.1 us
    pallas_call x1, Pallas kernels, attend(): pl.pallas_call(functools.partial(attend_kernel, width // HD), grid_spec=p...  34.9 us
    ppermute x12, starting transfers between devices, line_reduce_scatter(): left[c] = lax.ppermute(left_total, 'tensor', leftward)  17.8 us
  transfers between devices with their start and end apart: 38, of which 18 were waited for; matrix products, arithmetic and copies ran while one was open for 22% of the time, Pallas kernels for 15%

profile of v1, /device:TPU:0, one launch (start us, length us, event | category | flops | bytes accessed | tf_op | source)
XLA Modules:
  0.0 494.2 jit_solution(469897725218573234)
XLA Ops:
  7.2 5.0 %fusion.148 = (bf16[1,128,12288]{2,1,0:T(8,128)(2,1)S(1)}, bf16[1,128,12288]{2,1,0:T(8,128)(2,1)}) fusion(bf16[1,256,12288]{2,1,0:T(8,128)(2,1)} %param.6), kind=kLoop, calls=%fused_computation.132 | loop fusion | bytes 12582912 | tf_op jit(solution)/shard_map/slice | solution.py:211
  12.2 2.1 dynamic-slice_bitcast_fusion
  15.8 5.8 %collective-permute-start.6 = (bf16[128,3072]{1,0:T(8,128)(2,1)}, bf16[128,3072]{1,0:T(8,128)(2,1)}, u32[]{:S(2)}, u32[]{:S(2)}) collective-permute-start(bf16[128,3072]{1,0:T(8,128)(2,1)} %dynamic-slice_bitcast_fusion), channel_id=1, source_target_pairs={{0,1},{4,5},{8,9},{12,13},{16,17},{20,21},{24,25},{28,29}} | collective-permute-start | bytes 2359304 | tf_op jit(solution)/shard_map/ppermute | solution.py:165
  24.2 2.2 collective-permute-start
  26.4 12.7 %collective-permute-done.6 = bf16[128,3072]{1,0:T(8,128)(2,1)} collective-permute-done((bf16[128,3072]{1,0:T(8,128)(2,1)}, bf16[128,3072]{1,0:T(8,128)(2,1)}, u32[]{:S(2)}, u32[]{:S(2)}) %collective-permute-start.6) | collective-permute-done | bytes 786464 | tf_op jit(solution)/shard_map/ppermute | solution.py:165
  39.0 2.8 fusion.76
  43.4 5.0 %collective-permute-start.8 = (bf16[128,3072]{1,0:T(8,128)(2,1)}, bf16[128,3072]{1,0:T(8,128)(2,1)}, u32[]{:S(2)}, u32[]{:S(2)}) collective-permute-start(bf16[128,3072]{1,0:T(8,128)(2,1)} %fusion.76), channel_id=1, source_target_pairs={{0,1},{1,2},{4,5},{5,6},{8,9},{9,10},{12,13},{13,14},{16,17},{17,1... | collective-permute-start | bytes 2359304 | tf_op jit(solution)/shard_map/ppermute | solution.py:165
  48.4 7.4 %collective-permute-done = bf16[128,3072]{1,0:T(8,128)(2,1)} collective-permute-done((bf16[128,3072]{1,0:T(8,128)(2,1)}, bf16[128,3072]{1,0:T(8,128)(2,1)}, u32[]{:S(2)}, u32[]{:S(2)}) %collective-permute-start) | collective-permute-done | bytes 786464 | tf_op jit(solution)/shard_map/ppermute | solution.py:165
  55.9 2.6 fusion.82
  60.0 5.1 %collective-permute-start.2 = (bf16[128,3072]{1,0:T(8,128)(2,1)}, bf16[128,3072]{1,0:T(8,128)(2,1)}, u32[]{:S(2)}, u32[]{:S(2)}) collective-permute-start(bf16[128,3072]{1,0:T(8,128)(2,1)} %fusion.82), channel_id=1, source_target_pairs={{0,1},{1,2},{4,5},{5,6},{8,9},{9,10},{12,13},{13,14},{16,17},{17,1... | collective-permute-start | bytes 2359304 | tf_op jit(solution)/shard_map/ppermute | solution.py:165
  65.1 7.6 %collective-permute-done.8 = bf16[128,3072]{1,0:T(8,128)(2,1)} collective-permute-done((bf16[128,3072]{1,0:T(8,128)(2,1)}, bf16[128,3072]{1,0:T(8,128)(2,1)}, u32[]{:S(2)}, u32[]{:S(2)}) %collective-permute-start.8) | collective-permute-done | bytes 786464 | tf_op jit(solution)/shard_map/ppermute | solution.py:165
  72.7 3.6 fusion.77
  76.3 5.3 %collective-permute-start.9 = (bf16[128,3072]{1,0:T(8,128)(2,1)}, bf16[128,3072]{1,0:T(8,128)(2,1)}, u32[]{:S(2)}, u32[]{:S(2)}) collective-permute-start(bf16[128,3072]{1,0:T(8,128)(2,1)} %get-tuple-element.10), channel_id=1, source_target_pairs={{0,1},{1,2},{2,3},{4,5},{5,6},{6,7},{8,9},{9,10},{10,11},{12,13},{... | collective-permute-start | bytes 2359304 | tf_op jit(solution)/shard_map/ppermute | solution.py:165
  82.9 6.7 %collective-permute-done.2 = bf16[128,3072]{1,0:T(8,128)(2,1)} collective-permute-done((bf16[128,3072]{1,0:T(8,128)(2,1)}, bf16[128,3072]{1,0:T(8,128)(2,1)}, u32[]{:S(2)}, u32[]{:S(2)}) %collective-permute-start.2) | collective-permute-done | bytes 786464 | tf_op jit(solution)/shard_map/ppermute | solution.py:165
  89.6 3.2 fusion.83
  92.7 5.3 %collective-permute-start.3 = (bf16[128,3072]{1,0:T(8,128)(2,1)}, bf16[128,3072]{1,0:T(8,128)(2,1)}, u32[]{:S(2)}, u32[]{:S(2)}) collective-permute-start(bf16[128,3072]{1,0:T(8,128)(2,1)} %get-tuple-element.8), channel_id=1, source_target_pairs={{0,1},{1,2},{2,3},{4,5},{5,6},{6,7},{8,9},{9,10},{10,11},{12,13},{... | collective-permute-start | bytes 2359304 | tf_op jit(solution)/shard_map/ppermute | solution.py:165
  99.3 7.1 %collective-permute-done.9 = bf16[128,3072]{1,0:T(8,128)(2,1)} collective-permute-done((bf16[128,3072]{1,0:T(8,128)(2,1)}, bf16[128,3072]{1,0:T(8,128)(2,1)}, u32[]{:S(2)}, u32[]{:S(2)}) %collective-permute-start.9) | collective-permute-done | bytes 786464 | tf_op jit(solution)/shard_map/ppermute | solution.py:165
  106.4 2.0 fusion.93
  108.4 13.7 %collective-permute-done.3 = bf16[128,3072]{1,0:T(8,128)(2,1)} collective-permute-done((bf16[128,3072]{1,0:T(8,128)(2,1)}, bf16[128,3072]{1,0:T(8,128)(2,1)}, u32[]{:S(2)}, u32[]{:S(2)}) %collective-permute-start.3) | collective-permute-done | bytes 786464 | tf_op jit(solution)/shard_map/ppermute | solution.py:165
  122.1 1.7 fusion.92
  128.5 6.0 %collective-permute-start.26 = (bf16[256,2048]{1,0:T(8,128)(2,1)}, bf16[256,2048]{1,0:T(8,128)(2,1)}, u32[]{:S(2)}, u32[]{:S(2)}) collective-permute-start(bf16[256,2048]{1,0:T(8,128)(2,1)} %get-tuple-element.12), channel_id=1, source_target_pairs={{0,1},{1,2},{2,3},{4,5},{5,6},{6,7},{8,9},{9,10},{10,11},{12,13},{... | collective-permute-start | bytes 3145736 | tf_op jit(solution)/shard_map/ppermute | solution.py:178
  135.8 5.6 %collective-permute-start.32 = (bf16[256,2048]{1,0:T(8,128)(2,1)S(1)}, bf16[256,2048]{1,0:T(8,128)(2,1)}, u32[]{:S(2)}, u32[]{:S(2)}) collective-permute-start(bf16[256,2048]{1,0:T(8,128)(2,1)S(1)} %get-tuple-element.13), channel_id=1, source_target_pairs={{0,1},{1,2},{2,3},{4,5},{5,6},{6,7},{8,9},{9,10},{10,11},{12,13},{... | collective-permute-start | bytes 3145736 | tf_op jit(solution)/shard_map/ppermute | solution.py:178
  141.7 14.2 %collective-permute-done.24 = bf16[256,2048]{1,0:T(8,128)(2,1)} collective-permute-done((bf16[256,2048]{1,0:T(8,128)(2,1)}, bf16[256,2048]{1,0:T(8,128)(2,1)}, u32[]{:S(2)}, u32[]{:S(2)}) %collective-permute-start.24) | collective-permute-done | bytes 1048608 | tf_op jit(solution)/shard_map/ppermute | solution.py:179
  158.1 20.3 %collective-permute-done.30 = bf16[256,2048]{1,0:T(8,128)(2,1)} collective-permute-done((bf16[256,2048]{1,0:T(8,128)(2,1)S(1)}, bf16[256,2048]{1,0:T(8,128)(2,1)}, u32[]{:S(2)}, u32[]{:S(2)}) %collective-permute-start.30) | collective-permute-done | bytes 1048608 | tf_op jit(solution)/shard_map/ppermute | solution.py:179
  179.7 1.7 collective-permute-start.33
  181.9 6.0 %fusion.41 = f32[256,1536]{1,0:T(8,128)} fusion(bf16[1536,8192]{1,0:T(8,128)(2,1)} %param.8, s32[]{:T(128)S(6)} %select_n.103, bf16[512,2048]{1,0:T(8,128)(2,1)S(1)} %copy-done), kind=kOutput, calls=%fused_computation.41 | convolution fusion | flops 1610612736 | bytes 8912900 | tf_op jit(solution)/shard_map/dot_general | solution.py:243
  187.9 4.8 fusion.38
  192.7 8.1 %collective-permute-done.25 = bf16[256,2048]{1,0:T(8,128)(2,1)S(1)} collective-permute-done((bf16[256,2048]{1,0:T(8,128)(2,1)}, bf16[256,2048]{1,0:T(8,128)(2,1)S(1)}, u32[]{:S(2)}, u32[]{:S(2)}) %collective-permute-start.25) | collective-permute-done | bytes 1048608 | tf_op jit(solution)/shard_map/ppermute | solution.py:179
  202.1 1.7 collective-permute-start.28
  203.8 19.5 %collective-permute-done.31 = bf16[256,2048]{1,0:T(8,128)(2,1)S(1)} collective-permute-done((bf16[256,2048]{1,0:T(8,128)(2,1)}, bf16[256,2048]{1,0:T(8,128)(2,1)S(1)}, u32[]{:S(2)}, u32[]{:S(2)}) %collective-permute-start.31) | collective-permute-done | bytes 1048608 | tf_op jit(solution)/shard_map/ppermute | solution.py:179
  225.5 5.8 %fusion.44 = f32[256,1536]{1,0:T(8,128)} fusion(f32[256,1536]{1,0:T(8,128)S(1)} %fusion.38, bf16[1536,8192]{1,0:T(8,128)(2,1)} %param.8, s32[]{:T(128)S(6)} %select_n.104, bf16[256,2048]{1,0:T(8,128)(2,1)S(1)} %collective-permute-done.25, bf16[256,2048]{1,0:T(8,128)(2,1)S(1)} %collective-permute-done.27), kind=kOutput, calls=%fused_computation.42 | convolution fusion | flops 1611530240 | bytes 11534340 | tf_op jit(solution)/shard_map/dot_general | solution.py:243
  231.3 6.7 %fusion.47 = f32[256,1536]{1,0:T(8,128)} fusion(f32[256,1536]{1,0:T(8,128)} %fusion.41, bf16[1536,8192]{1,0:T(8,128)(2,1)} %param.8, s32[]{:T(128)S(6)} %select_n.104, bf16[256,2048]{1,0:T(8,128)(2,1)S(1)} %collective-permute-done.31, bf16[256,2048]{1,0:T(8,128)(2,1)} %collective-permute-done.33), kind=kOutput, calls=%fused_computation.43 | convolution fusion | flops 1611530240 | bytes 11534340 | tf_op jit(solution)/shard_map/dot_general | solution.py:243
  238.0 7.8 %collective-permute-done.29 = bf16[256,2048]{1,0:T(8,128)(2,1)S(1)} collective-permute-done((bf16[256,2048]{1,0:T(8,128)(2,1)S(1)}, bf16[256,2048]{1,0:T(8,128)(2,1)S(1)}, u32[]{:S(2)}, u32[]{:S(2)}) %collective-permute-start.29) | collective-permute-done | bytes 1048608 | tf_op jit(solution)/shard_map/ppermute | solution.py:179
  245.8 4.2 fusion.4
  250.0 16.4 %collective-permute-done.35 = bf16[256,2048]{1,0:T(8,128)(2,1)S(1)} collective-permute-done((bf16[256,2048]{1,0:T(8,128)(2,1)S(1)}, bf16[256,2048]{1,0:T(8,128)(2,1)S(1)}, u32[]{:S(2)}, u32[]{:S(2)}) %collective-permute-start.35) | collective-permute-done | bytes 1048608 | tf_op jit(solution)/shard_map/ppermute | solution.py:179
  266.4 4.2 fusion.2
  270.6 4.4 fusion.62
  275.1 34.9 %attend.1 = bf16[512,1536]{1,0:T(8,128)(2,1)} custom-call(s32[16]{0:T(128)} %multiply_add_fusion.ids_ref, bf16[512,1536]{1,0:T(8,128)(2,1)} %q_ref.3, bf16[16,128,3072]{2,1,0:T(8,128)(2,1)} %all-gather.2.cloned.1.call-done.first_ref.second_ref, bf16[16,128,3072]{2,1,0:T(8,128)(2,1)} %all-gather.2.cloned.1.call-done.first_ref.second_ref), custom_call_target="tpu_custom_call" | custom-call | flops 805306368 | bytes 15728640 | tf_op jit(solution)/shard_map/attend/pallas_call | solution.py:43
  309.9 6.0 %fusion.71 = bf16[256,2048]{1,0:T(8,128)(2,1)} fusion(bf16[1536,8192]{1,0:T(8,128)(2,1)} %param.8, s32[]{:T(128)S(6)} %select_n.99, bf16[512,1536]{1,0:T(8,128)(2,1)} %attend.1), kind=kOutput, calls=%fused_computation.51 | convolution fusion | flops 1611137024 | bytes 8126468 | tf_op jit(solution)/shard_map/dot_general | solution.py:226
  317.5 2.6 collective-permute-start.18
  320.2 5.0 %fusion.65 = bf16[256,1536]{1,0:T(8,128)(2,1)S(1)} fusion(f32[256,1536]{1,0:T(8,128)S(1)} %copy-done.7, f32[256,1536]{1,0:T(8,128)S(1)} %copy-done.6, bf16[1536,8192]{1,0:T(8,128)(2,1)} %param.8, s32[]{:T(128)S(6)} %select_n.105, bf16[256,2048]{1,0:T(8,128)(2,1)} %collective-permute-done.30, bf16[256,2048]{1,0:T(8,128)(2,1)S(1)} %collective-permute-done.34), kind=kOutput, calls=%fused_computation.49 | convolution fusion | flops 1612316672 | bytes 12320772 | tf_op jit(solution)/shard_map/dot_general | solution.py:243
  327.2 5.6 %fusion.68 = bf16[256,2048]{1,0:T(8,128)(2,1)} fusion(bf16[1536,8192]{1,0:T(8,128)(2,1)} %param.8, s32[]{:T(128)S(6)} %select_n.99, bf16[512,1536]{1,0:T(8,128)(2,1)S(1)} %copy-done.1), kind=kOutput, calls=%fused_computation.50 | convolution fusion | flops 1611137024 | bytes 8126468 | tf_op jit(solution)/shard_map/dot_general | solution.py:226
  333.5 2.3 collective-permute-start.12
  335.8 38.1 %attend_grad.1 = bf16[8,128,3072]{2,1,0:T(8,128)(2,1)} custom-call(s32[16]{0:T(128)} %multiply_add_fusion.ids_ref, s32[16]{0:T(128)} %copy-done.4, bf16[512,1536]{1,0:T(8,128)(2,1)} %q_ref.3, bf16[512,1536]{1,0:T(8,128)(2,1)} %pad_maximum_fusion.2.g_ref, bf16[16,128,3072]{2,1,0:T(8,128)(2,1)} %all-gather.2.cloned.1.call-done.first_ref.second_ref, ...), custom_call_target="tpu_custom_call" | custom-call | flops 2013265920 | bytes 22020096 | tf_op jit(solution)/shard_map/attend_grad/pallas_call | solution.py:112
  373.9 4.8 all-to-all-start
  378.7 6.2 %add_convert_fusion.3 = bf16[256,2048]{1,0:T(8,128)(2,1)} fusion(bf16[256,2048]{1,0:T(8,128)(2,1)} %collective-permute-done.19, bf16[256,2048]{1,0:T(8,128)(2,1)} %collective-permute-done.18, bf16[1536,8192]{1,0:T(8,128)(2,1)} %param.8, s32[]{:T(128)S(6)} %select_n.98, bf16[512,1536]{1,0:T(8,128)(2,1)S(1)} %copy-done.1), kind=kOutput, calls=%fused_computation.56 | convolution fusion | flops 1613234176 | bytes 10223620 | tf_op jit(solution)/shard_map/dot_general | solution.py:226
  384.9 1.6 collective-permute-start.22
  386.5 2.3 collective-permute-start.20
  389.8 5.2 %add_convert_fusion.7 = bf16[256,2048]{1,0:T(8,128)(2,1)S(1)} fusion(bf16[256,2048]{1,0:T(8,128)(2,1)} %copy-done.5, bf16[256,2048]{1,0:T(8,128)(2,1)} %collective-permute-done.12, bf16[1536,8192]{1,0:T(8,128)(2,1)} %param.8, s32[]{:T(128)S(6)} %select_n.98, bf16[512,1536]{1,0:T(8,128)(2,1)S(1)} %copy-done.1), kind=kOutput, calls=%fused_computation.60 | convolution fusion | flops 1613234176 | bytes 10223620 | tf_op jit(solution)/shard_map/dot_general | solution.py:226
  395.0 1.7 collective-permute-start.16
  398.8 5.0 %add_convert_fusion.1 = bf16[256,2048]{1,0:T(8,128)(2,1)S(1)} fusion(bf16[256,2048]{1,0:T(8,128)(2,1)} %collective-permute-done.22, bf16[1536,8192]{1,0:T(8,128)(2,1)} %param.8, s32[]{:T(128)S(6)} %select_n.100, bf16[512,1536]{1,0:T(8,128)(2,1)S(1)} %copy-done.1), kind=kOutput, calls=%fused_computation.54 | convolution fusion | flops 1612185600 | bytes 9175044 | tf_op jit(solution)/shard_map/dot_general | solution.py:226
  403.8 1.8 collective-permute-start.23
  405.6 6.0 %collective-permute-done.20 = bf16[256,2048]{1,0:T(8,128)(2,1)} collective-permute-done((bf16[256,2048]{1,0:T(8,128)(2,1)}, bf16[256,2048]{1,0:T(8,128)(2,1)}, u32[]{:S(2)}, u32[]{:S(2)}) %collective-permute-start.20) | collective-permute-done | bytes 1048608 | tf_op jit(solution)/shard_map/ppermute | solution.py:165
  411.7 4.8 add_convert_fusion.2
  416.5 8.5 %collective-permute-start.21 = (bf16[256,2048]{1,0:T(8,128)(2,1)S(1)}, bf16[256,2048]{1,0:T(8,128)(2,1)S(1)}, u32[]{:S(2)}, u32[]{:S(2)}) collective-permute-start(bf16[256,2048]{1,0:T(8,128)(2,1)S(1)} %add_convert_fusion.2), channel_id=1, source_target_pairs={{0,1},{1,2},{2,3},{4,5},{5,6},{6,7},{8,9},{9,10},{10,11},{12,13},{... | collective-permute-start | bytes 3145736 | tf_op jit(solution)/shard_map/ppermute | solution.py:165
  425.1 5.8 %add_convert_fusion.5 = bf16[256,2048]{1,0:T(8,128)(2,1)} fusion(bf16[256,2048]{1,0:T(8,128)(2,1)} %collective-permute-done.16, bf16[1536,8192]{1,0:T(8,128)(2,1)} %param.8, s32[]{:T(128)S(6)} %select_n.100, bf16[512,1536]{1,0:T(8,128)(2,1)S(1)} %copy-done.1), kind=kOutput, calls=%fused_computation.58 | convolution fusion | flops 1612185600 | bytes 9175044 | tf_op jit(solution)/shard_map/dot_general | solution.py:226
  434.0 4.6 add_convert_fusion.6
  438.6 8.9 %collective-permute-start.15 = (bf16[256,2048]{1,0:T(8,128)(2,1)S(1)}, bf16[256,2048]{1,0:T(8,128)(2,1)S(1)}, u32[]{:S(2)}, u32[]{:S(2)}) collective-permute-start(bf16[256,2048]{1,0:T(8,128)(2,1)S(1)} %add_convert_fusion.6), channel_id=1, source_target_pairs={{0,1},{1,2},{2,3},{4,5},{5,6},{6,7},{8,9},{9,10},{10,11},{12,13},{... | collective-permute-start | bytes 3145736 | tf_op jit(solution)/shard_map/ppermute | solution.py:165
  447.6 1.8 fusion.34
  449.4 1.8 fusion.36
  451.2 5.3 %collective-permute-done.21 = bf16[256,2048]{1,0:T(8,128)(2,1)S(1)} collective-permute-done((bf16[256,2048]{1,0:T(8,128)(2,1)S(1)}, bf16[256,2048]{1,0:T(8,128)(2,1)S(1)}, u32[]{:S(2)}, u32[]{:S(2)}) %collective-permute-start.21) | collective-permute-done | bytes 1048608 | tf_op jit(solution)/shard_map/ppermute | solution.py:165
  457.0 6.5 %collective-permute-done.17 = bf16[256,2048]{1,0:T(8,128)(2,1)S(1)} collective-permute-done((bf16[256,2048]{1,0:T(8,128)(2,1)}, bf16[256,2048]{1,0:T(8,128)(2,1)S(1)}, u32[]{:S(2)}, u32[]{:S(2)}) %collective-permute-start.17) | collective-permute-done | bytes 1048608 | tf_op jit(solution)/shard_map/ppermute | solution.py:166
  463.5 15.2 %collective-permute-done.15 = bf16[256,2048]{1,0:T(8,128)(2,1)S(1)} collective-permute-done((bf16[256,2048]{1,0:T(8,128)(2,1)S(1)}, bf16[256,2048]{1,0:T(8,128)(2,1)S(1)}, u32[]{:S(2)}, u32[]{:S(2)}) %collective-permute-start.15) | collective-permute-done | bytes 1048608 | tf_op jit(solution)/shard_map/ppermute | solution.py:165
  480.7 5.0 %fusion = (bf16[128,3072]{1,0:T(8,128)(2,1)S(1)}, bf16[128,3072]{1,0:T(8,128)(2,1)S(1)}) fusion(bf16[8,128,3072]{2,1,0:T(8,128)(2,1)} %all-to-all-done, pred[8]{0:T(512)(128)(4,1)S(1)} %get-tuple-element.4, pred[8]{0:T(512)(128)(4,1)S(1)} %get-tuple-element.5), kind=kLoop, calls=%fused_computation.2 | loop fusion | flops 14942208 | bytes 7864336 | tf_op jit(solution)/shard_map/reduce_sum | solution.py:251
  (104 shorter events, 37.8 us)
Async XLA Ops:
  7.2 267.9 %all-gather.2.cloned.1.call-start = ((), (), s32[]{:S(2)}) async-start(), calls=%async_computation.1 | async-start | bytes 14155776 | tf_op jit(solution)/shard_map/all_gather | solution.py:218
  14.3 12.1 %collective-permute-start.7 = (bf16[128,3072]{1,0:T(8,128)(2,1)}, bf16[128,3072]{1,0:T(8,128)(2,1)}, u32[]{:S(2)}, u32[]{:S(2)}) collective-permute-start(bf16[128,3072]{1,0:T(8,128)(2,1)} %dynamic-slice_bitcast_fusion), channel_id=1, source_target_pairs={{3,2},{7,6},{11,10},{15,14},{19,18},{23,22},{27,26},{31,30}} | collective-permute-start | bytes 2359304 | tf_op jit(solution)/shard_map/ppermute | solution.py:166
  15.8 23.2 %collective-permute-start.6 = (bf16[128,3072]{1,0:T(8,128)(2,1)}, bf16[128,3072]{1,0:T(8,128)(2,1)}, u32[]{:S(2)}, u32[]{:S(2)}) collective-permute-start(bf16[128,3072]{1,0:T(8,128)(2,1)} %dynamic-slice_bitcast_fusion), channel_id=1, source_target_pairs={{0,1},{4,5},{8,9},{12,13},{16,17},{20,21},{24,25},{28,29}} | collective-permute-start | bytes 2359304 | tf_op jit(solution)/shard_map/ppermute | solution.py:165
  22.6 25.8 %collective-permute-start.1 = (bf16[128,3072]{1,0:T(8,128)(2,1)}, bf16[128,3072]{1,0:T(8,128)(2,1)}, u32[]{:S(2)}, u32[]{:S(2)}) collective-permute-start(bf16[128,3072]{1,0:T(8,128)(2,1)} %dynamic-slice_bitcast_fusion.1), channel_id=1, source_target_pairs={{3,2},{7,6},{11,10},{15,14},{19,18},{23,22},{27,26},{31,30}} | collective-permute-start | bytes 2359304 | tf_op jit(solution)/shard_map/ppermute | solution.py:166
  24.2 31.7 %collective-permute-start = (bf16[128,3072]{1,0:T(8,128)(2,1)}, bf16[128,3072]{1,0:T(8,128)(2,1)}, u32[]{:S(2)}, u32[]{:S(2)}) collective-permute-start(bf16[128,3072]{1,0:T(8,128)(2,1)} %dynamic-slice_bitcast_fusion.1), channel_id=1, source_target_pairs={{0,1},{4,5},{8,9},{12,13},{16,17},{20,21},{24,25},{28,29}} | collective-permute-start | bytes 2359304 | tf_op jit(solution)/shard_map/ppermute | solution.py:165
  41.9 23.2 %collective-permute-start.10 = (bf16[128,3072]{1,0:T(8,128)(2,1)}, bf16[128,3072]{1,0:T(8,128)(2,1)}, u32[]{:S(2)}, u32[]{:S(2)}) collective-permute-start(bf16[128,3072]{1,0:T(8,128)(2,1)} %fusion.76), channel_id=1, source_target_pairs={{2,1},{3,2},{6,5},{7,6},{10,9},{11,10},{14,13},{15,14},{18,17},{19... | collective-permute-start | bytes 2359304 | tf_op jit(solution)/shard_map/ppermute | solution.py:166
  43.4 29.3 %collective-permute-start.8 = (bf16[128,3072]{1,0:T(8,128)(2,1)}, bf16[128,3072]{1,0:T(8,128)(2,1)}, u32[]{:S(2)}, u32[]{:S(2)}) collective-permute-start(bf16[128,3072]{1,0:T(8,128)(2,1)} %fusion.76), channel_id=1, source_target_pairs={{0,1},{1,2},{4,5},{5,6},{8,9},{9,10},{12,13},{13,14},{16,17},{17,1... | collective-permute-start | bytes 2359304 | tf_op jit(solution)/shard_map/ppermute | solution.py:165
  58.5 24.4 %collective-permute-start.4 = (bf16[128,3072]{1,0:T(8,128)(2,1)}, bf16[128,3072]{1,0:T(8,128)(2,1)}, u32[]{:S(2)}, u32[]{:S(2)}) collective-permute-start(bf16[128,3072]{1,0:T(8,128)(2,1)} %fusion.82), channel_id=1, source_target_pairs={{2,1},{3,2},{6,5},{7,6},{10,9},{11,10},{14,13},{15,14},{18,17},{19... | collective-permute-start | bytes 2359304 | tf_op jit(solution)/shard_map/ppermute | solution.py:166
  60.0 29.6 %collective-permute-start.2 = (bf16[128,3072]{1,0:T(8,128)(2,1)}, bf16[128,3072]{1,0:T(8,128)(2,1)}, u32[]{:S(2)}, u32[]{:S(2)}) collective-permute-start(bf16[128,3072]{1,0:T(8,128)(2,1)} %fusion.82), channel_id=1, source_target_pairs={{0,1},{1,2},{4,5},{5,6},{8,9},{9,10},{12,13},{13,14},{16,17},{17,1... | collective-permute-start | bytes 2359304 | tf_op jit(solution)/shard_map/ppermute | solution.py:165
  76.3 30.1 %collective-permute-start.9 = (bf16[128,3072]{1,0:T(8,128)(2,1)}, bf16[128,3072]{1,0:T(8,128)(2,1)}, u32[]{:S(2)}, u32[]{:S(2)}) collective-permute-start(bf16[128,3072]{1,0:T(8,128)(2,1)} %get-tuple-element.10), channel_id=1, source_target_pairs={{0,1},{1,2},{2,3},{4,5},{5,6},{6,7},{8,9},{9,10},{10,11},{12,13},{... | collective-permute-start | bytes 2359304 | tf_op jit(solution)/shard_map/ppermute | solution.py:165
  81.6 24.9 %collective-permute-start.11 = (bf16[128,3072]{1,0:T(8,128)(2,1)}, bf16[128,3072]{1,0:T(8,128)(2,1)}, u32[]{:S(2)}, u32[]{:S(2)}) collective-permute-start(bf16[128,3072]{1,0:T(8,128)(2,1)} %get-tuple-element.11), channel_id=1, source_target_pairs={{1,0},{2,1},{3,2},{5,4},{6,5},{7,6},{9,8},{10,9},{11,10},{13,12},{... | collective-permute-start | bytes 2359304 | tf_op jit(solution)/shard_map/ppermute | solution.py:166
  92.7 29.4 %collective-permute-start.3 = (bf16[128,3072]{1,0:T(8,128)(2,1)}, bf16[128,3072]{1,0:T(8,128)(2,1)}, u32[]{:S(2)}, u32[]{:S(2)}) collective-permute-start(bf16[128,3072]{1,0:T(8,128)(2,1)} %get-tuple-element.8), channel_id=1, source_target_pairs={{0,1},{1,2},{2,3},{4,5},{5,6},{6,7},{8,9},{9,10},{10,11},{12,13},{... | collective-permute-start | bytes 2359304 | tf_op jit(solution)/shard_map/ppermute | solution.py:165
  98.0 24.1 %collective-permute-start.5 = (bf16[128,3072]{1,0:T(8,128)(2,1)}, bf16[128,3072]{1,0:T(8,128)(2,1)}, u32[]{:S(2)}, u32[]{:S(2)}) collective-permute-start(bf16[128,3072]{1,0:T(8,128)(2,1)} %get-tuple-element.9), channel_id=1, source_target_pairs={{1,0},{2,1},{3,2},{5,4},{6,5},{7,6},{9,8},{10,9},{11,10},{13,12},{... | collective-permute-start | bytes 2359304 | tf_op jit(solution)/shard_map/ppermute | solution.py:166
  123.9 2.2 copy-start
  126.0 15.3 %copy-start.2 = (s32[64,2]{0,1:T(2,128)S(1)}, s32[64,2]{0,1:T(2,128)}, u32[]{:S(2)}) copy-start(s32[64,2]{0,1:T(2,128)} %param.10) | copy-start | bytes 1540
  126.0 15.3 %copy-start.3 = (s32[64,2]{0,1:T(2,128)S(1)}, s32[64,2]{0,1:T(2,128)}, u32[]{:S(2)}) copy-start(s32[64,2]{0,1:T(2,128)} %param.11) | copy-start | bytes 1540
  127.2 28.8 %collective-permute-start.24 = (bf16[256,2048]{1,0:T(8,128)(2,1)}, bf16[256,2048]{1,0:T(8,128)(2,1)}, u32[]{:S(2)}, u32[]{:S(2)}) collective-permute-start(bf16[256,2048]{1,0:T(8,128)(2,1)} %get-tuple-element.12), channel_id=1, source_target_pairs={{1,0},{2,1},{3,2},{5,4},{6,5},{7,6},{9,8},{10,9},{11,10},{13,12},{... | collective-permute-start | bytes 3145736 | tf_op jit(solution)/shard_map/ppermute | solution.py:179
  128.5 28.9 %collective-permute-start.26 = (bf16[256,2048]{1,0:T(8,128)(2,1)}, bf16[256,2048]{1,0:T(8,128)(2,1)}, u32[]{:S(2)}, u32[]{:S(2)}) collective-permute-start(bf16[256,2048]{1,0:T(8,128)(2,1)} %get-tuple-element.12), channel_id=1, source_target_pairs={{0,1},{1,2},{2,3},{4,5},{5,6},{6,7},{8,9},{9,10},{10,11},{12,13},{... | collective-permute-start | bytes 3145736 | tf_op jit(solution)/shard_map/ppermute | solution.py:178
  134.5 44.0 %collective-permute-start.30 = (bf16[256,2048]{1,0:T(8,128)(2,1)S(1)}, bf16[256,2048]{1,0:T(8,128)(2,1)}, u32[]{:S(2)}, u32[]{:S(2)}) collective-permute-start(bf16[256,2048]{1,0:T(8,128)(2,1)S(1)} %get-tuple-element.13), channel_id=1, source_target_pairs={{1,0},{2,1},{3,2},{5,4},{6,5},{7,6},{9,8},{10,9},{11,10},{13,12},{... | collective-permute-start | bytes 3145736 | tf_op jit(solution)/shard_map/ppermute | solution.py:179
  135.8 44.0 %collective-permute-start.32 = (bf16[256,2048]{1,0:T(8,128)(2,1)S(1)}, bf16[256,2048]{1,0:T(8,128)(2,1)}, u32[]{:S(2)}, u32[]{:S(2)}) collective-permute-start(bf16[256,2048]{1,0:T(8,128)(2,1)S(1)} %get-tuple-element.13), channel_id=1, source_target_pairs={{0,1},{1,2},{2,3},{4,5},{5,6},{6,7},{8,9},{9,10},{10,11},{12,13},{... | collective-permute-start | bytes 3145736 | tf_op jit(solution)/shard_map/ppermute | solution.py:178
  141.7 46.2 %copy-start.4 = (s32[16]{0:T(128)}, s32[16]{0:T(128)S(1)}, u32[]{:S(2)}) copy-start(s32[16]{0:T(128)S(1)} %reshape.56.own_ref) | copy-start | bytes 196
  156.0 44.8 %collective-permute-start.25 = (bf16[256,2048]{1,0:T(8,128)(2,1)}, bf16[256,2048]{1,0:T(8,128)(2,1)S(1)}, u32[]{:S(2)}, u32[]{:S(2)}) collective-permute-start(bf16[256,2048]{1,0:T(8,128)(2,1)} %collective-permute-done.24), channel_id=1, source_target_pairs={{1,0},{2,1},{5,4},{6,5},{9,8},{10,9},{13,12},{14,13},{17,16},{18,1... | collective-permute-start | bytes 3145736 | tf_op jit(solution)/shard_map/ppermute | solution.py:179
  157.4 44.7 %collective-permute-start.27 = (bf16[256,2048]{1,0:T(8,128)(2,1)}, bf16[256,2048]{1,0:T(8,128)(2,1)S(1)}, u32[]{:S(2)}, u32[]{:S(2)}) collective-permute-start(bf16[256,2048]{1,0:T(8,128)(2,1)} %collective-permute-done.26), channel_id=1, source_target_pairs={{1,2},{2,3},{5,6},{6,7},{9,10},{10,11},{13,14},{14,15},{17,18},{18... | collective-permute-start | bytes 3145736 | tf_op jit(solution)/shard_map/ppermute | solution.py:178
  178.4 44.8 %collective-permute-start.31 = (bf16[256,2048]{1,0:T(8,128)(2,1)}, bf16[256,2048]{1,0:T(8,128)(2,1)S(1)}, u32[]{:S(2)}, u32[]{:S(2)}) collective-permute-start(bf16[256,2048]{1,0:T(8,128)(2,1)} %collective-permute-done.30), channel_id=1, source_target_pairs={{1,0},{2,1},{5,4},{6,5},{9,8},{10,9},{13,12},{14,13},{17,16},{18,1... | collective-permute-start | bytes 3145736 | tf_op jit(solution)/shard_map/ppermute | solution.py:179
  179.7 44.8 %collective-permute-start.33 = (bf16[256,2048]{1,0:T(8,128)(2,1)}, bf16[256,2048]{1,0:T(8,128)(2,1)}, u32[]{:S(2)}, u32[]{:S(2)}) collective-permute-start(bf16[256,2048]{1,0:T(8,128)(2,1)} %collective-permute-done.32), channel_id=1, source_target_pairs={{1,2},{2,3},{5,6},{6,7},{9,10},{10,11},{13,14},{14,15},{17,18},{18... | collective-permute-start | bytes 3145736 | tf_op jit(solution)/shard_map/ppermute | solution.py:178
  181.9 63.8 %slice-start = ((s8[25165824]{0:T(1024)(128)(4,1)}), s8[4194304]{0:T(1024)(128)(4,1)S(1)}, s32[]{:S(2)}) async-start(s8[25165824]{0:T(1024)(128)(4,1)} %bitcast.36), calls=%async_computation.2 | async-start | bytes 8388608
  181.9 63.8 %slice-start.1 = ((s8[25165824]{0:T(1024)(128)(4,1)}), s8[4194304]{0:T(1024)(128)(4,1)S(1)}, s32[]{:S(2)}) async-start(s8[25165824]{0:T(1024)(128)(4,1)} %bitcast.36), calls=%async_computation.3 | async-start | bytes 8388608
  187.9 57.8 %slice-start.2 = ((s8[25165824]{0:T(1024)(128)(4,1)}), s8[4194304]{0:T(1024)(128)(4,1)S(1)}, s32[]{:S(2)}) async-start(s8[25165824]{0:T(1024)(128)(4,1)} %bitcast.36), calls=%async_computation.4 | async-start | bytes 8388608
  187.9 57.8 %slice-start.3 = ((s8[25165824]{0:T(1024)(128)(4,1)}), s8[4194304]{0:T(1024)(128)(4,1)S(1)}, s32[]{:S(2)}) async-start(s8[25165824]{0:T(1024)(128)(4,1)} %bitcast.36), calls=%async_computation.5 | async-start | bytes 8388608
  192.7 53.1 %slice-start.4 = ((s8[25165824]{0:T(1024)(128)(4,1)}), s8[4194304]{0:T(1024)(128)(4,1)S(1)}, s32[]{:S(2)}) async-start(s8[25165824]{0:T(1024)(128)(4,1)} %bitcast.36), calls=%async_computation.6 | async-start | bytes 8388608
  200.8 44.9 %collective-permute-start.29 = (bf16[256,2048]{1,0:T(8,128)(2,1)S(1)}, bf16[256,2048]{1,0:T(8,128)(2,1)S(1)}, u32[]{:S(2)}, u32[]{:S(2)}) collective-permute-start(bf16[256,2048]{1,0:T(8,128)(2,1)S(1)} %collective-permute-done.25), channel_id=1, source_target_pairs={{1,0},{5,4},{9,8},{13,12},{17,16},{21,20},{25,24},{29,28}} | collective-permute-start | bytes 3145736 | tf_op jit(solution)/shard_map/ppermute | solution.py:179
  202.1 68.5 %collective-permute-start.28 = (bf16[256,2048]{1,0:T(8,128)(2,1)S(1)}, bf16[256,2048]{1,0:T(8,128)(2,1)}, u32[]{:S(2)}, u32[]{:S(2)}) collective-permute-start(bf16[256,2048]{1,0:T(8,128)(2,1)S(1)} %collective-permute-done.27), channel_id=1, source_target_pairs={{2,3},{6,7},{10,11},{14,15},{18,19},{22,23},{26,27},{30,31}} | collective-permute-start | bytes 3145736 | tf_op jit(solution)/shard_map/ppermute | solution.py:178
  223.3 43.2 %collective-permute-start.35 = (bf16[256,2048]{1,0:T(8,128)(2,1)S(1)}, bf16[256,2048]{1,0:T(8,128)(2,1)S(1)}, u32[]{:S(2)}, u32[]{:S(2)}) collective-permute-start(bf16[256,2048]{1,0:T(8,128)(2,1)S(1)} %collective-permute-done.31), channel_id=1, source_target_pairs={{1,0},{5,4},{9,8},{13,12},{17,16},{21,20},{25,24},{29,28}} | collective-permute-start | bytes 3145736 | tf_op jit(solution)/shard_map/ppermute | solution.py:179
  224.6 95.6 %collective-permute-start.34 = (bf16[256,2048]{1,0:T(8,128)(2,1)}, bf16[256,2048]{1,0:T(8,128)(2,1)S(1)}, u32[]{:S(2)}, u32[]{:S(2)}) collective-permute-start(bf16[256,2048]{1,0:T(8,128)(2,1)} %collective-permute-done.33), channel_id=1, source_target_pairs={{2,3},{6,7},{10,11},{14,15},{18,19},{22,23},{26,27},{30,31}} | collective-permute-start | bytes 3145736 | tf_op jit(solution)/shard_map/ppermute | solution.py:178
  231.3 14.5 %slice-start.5 = ((s8[25165824]{0:T(1024)(128)(4,1)}), s8[4194304]{0:T(1024)(128)(4,1)S(1)}, s32[]{:S(2)}) async-start(s8[25165824]{0:T(1024)(128)(4,1)} %bitcast.36), calls=%async_computation.7 | async-start | bytes 8388608
  309.9 10.2 %copy-start.6 = (f32[256,1536]{1,0:T(8,128)S(1)}, f32[256,1536]{1,0:T(8,128)}, u32[]{:S(2)}) copy-start(f32[256,1536]{1,0:T(8,128)} %fusion.47) | copy-start | bytes 4718596
  309.9 10.2 %copy-start.7 = (f32[256,1536]{1,0:T(8,128)S(1)}, f32[256,1536]{1,0:T(8,128)}, u32[]{:S(2)}) copy-start(f32[256,1536]{1,0:T(8,128)} %fusion.2) | copy-start | bytes 4718596
  315.9 62.8 %collective-permute-start.19 = (bf16[256,2048]{1,0:T(8,128)(2,1)}, bf16[256,2048]{1,0:T(8,128)(2,1)}, u32[]{:S(2)}, u32[]{:S(2)}) collective-permute-start(bf16[256,2048]{1,0:T(8,128)(2,1)} %fusion.71), channel_id=1, source_target_pairs={{3,2},{7,6},{11,10},{15,14},{19,18},{23,22},{27,26},{31,30}} | collective-permute-start | bytes 3145736 | tf_op jit(solution)/shard_map/ppermute | solution.py:166
  317.5 61.1 %collective-permute-start.18 = (bf16[256,2048]{1,0:T(8,128)(2,1)}, bf16[256,2048]{1,0:T(8,128)(2,1)}, u32[]{:S(2)}, u32[]{:S(2)}) collective-permute-start(bf16[256,2048]{1,0:T(8,128)(2,1)} %fusion.71), channel_id=1, source_target_pairs={{0,1},{4,5},{8,9},{12,13},{16,17},{20,21},{24,25},{28,29}} | collective-permute-start | bytes 3145736 | tf_op jit(solution)/shard_map/ppermute | solution.py:165
  325.2 2.0 copy-start.1
  332.7 56.1 %collective-permute-start.13 = (bf16[256,2048]{1,0:T(8,128)(2,1)}, bf16[256,2048]{1,0:T(8,128)(2,1)S(1)}, u32[]{:S(2)}, u32[]{:S(2)}) collective-permute-start(bf16[256,2048]{1,0:T(8,128)(2,1)} %fusion.68), channel_id=1, source_target_pairs={{3,2},{7,6},{11,10},{15,14},{19,18},{23,22},{27,26},{31,30}} | collective-permute-start | bytes 3145736 | tf_op jit(solution)/shard_map/ppermute | solution.py:166
  333.5 56.3 %collective-permute-start.12 = (bf16[256,2048]{1,0:T(8,128)(2,1)}, bf16[256,2048]{1,0:T(8,128)(2,1)}, u32[]{:S(2)}, u32[]{:S(2)}) collective-permute-start(bf16[256,2048]{1,0:T(8,128)(2,1)} %fusion.68), channel_id=1, source_target_pairs={{0,1},{4,5},{8,9},{12,13},{16,17},{20,21},{24,25},{28,29}} | collective-permute-start | bytes 3145736 | tf_op jit(solution)/shard_map/ppermute | solution.py:165
  373.9 106.8 %all-to-all-start = ((bf16[8,128,3072]{2,1,0:T(8,128)(2,1)}), bf16[8,128,3072]{2,1,0:T(8,128)(2,1)}, u32[]{:S(2)}, u32[]{:S(2)}) async-start(bf16[8,128,3072]{2,1,0:T(8,128)(2,1)} %attend_grad.1), calls=%async_computation | async-start | bytes 12582912 | tf_op jit(solution)/shard_map/all_to_all | solution.py:249
  384.9 13.9 %collective-permute-start.22 = (bf16[256,2048]{1,0:T(8,128)(2,1)}, bf16[256,2048]{1,0:T(8,128)(2,1)}, u32[]{:S(2)}, u32[]{:S(2)}) collective-permute-start(bf16[256,2048]{1,0:T(8,128)(2,1)} %add_convert_fusion.3), channel_id=1, source_target_pairs={{2,1},{3,2},{6,5},{7,6},{10,9},{11,10},{14,13},{15,14},{18,17},{19... | collective-permute-start | bytes 3145736 | tf_op jit(solution)/shard_map/ppermute | solution.py:166
  386.5 25.1 %collective-permute-start.20 = (bf16[256,2048]{1,0:T(8,128)(2,1)}, bf16[256,2048]{1,0:T(8,128)(2,1)}, u32[]{:S(2)}, u32[]{:S(2)}) collective-permute-start(bf16[256,2048]{1,0:T(8,128)(2,1)} %add_convert_fusion.3), channel_id=1, source_target_pairs={{0,1},{1,2},{4,5},{5,6},{8,9},{9,10},{12,13},{13,14},{16,17},{17,1... | collective-permute-start | bytes 3145736 | tf_op jit(solution)/shard_map/ppermute | solution.py:165
  388.8 1.0 copy-start.5
  395.0 30.1 %collective-permute-start.16 = (bf16[256,2048]{1,0:T(8,128)(2,1)S(1)}, bf16[256,2048]{1,0:T(8,128)(2,1)}, u32[]{:S(2)}, u32[]{:S(2)}) collective-permute-start(bf16[256,2048]{1,0:T(8,128)(2,1)S(1)} %add_convert_fusion.7), channel_id=1, source_target_pairs={{2,1},{3,2},{6,5},{7,6},{10,9},{11,10},{14,13},{15,14},{18,17},{19... | collective-permute-start | bytes 3145736 | tf_op jit(solution)/shard_map/ppermute | solution.py:166
  397.4 36.6 %collective-permute-start.14 = (bf16[256,2048]{1,0:T(8,128)(2,1)S(1)}, bf16[256,2048]{1,0:T(8,128)(2,1)S(1)}, u32[]{:S(2)}, u32[]{:S(2)}) collective-permute-start(bf16[256,2048]{1,0:T(8,128)(2,1)S(1)} %add_convert_fusion.7), channel_id=1, source_target_pairs={{0,1},{1,2},{4,5},{5,6},{8,9},{9,10},{12,13},{13,14},{16,17},{17,1... | collective-permute-start | bytes 3145736 | tf_op jit(solution)/shard_map/ppermute | solution.py:165
  398.8 48.8 %slice-start.6 = ((s8[25165824]{0:T(1024)(128)(4,1)}), s8[4194304]{0:T(1024)(128)(4,1)S(1)}, s32[]{:S(2)}) async-start(s8[25165824]{0:T(1024)(128)(4,1)} %bitcast.38), calls=%async_computation.8 | async-start | bytes 8388608
  398.8 48.8 %slice-start.7 = ((s8[25165824]{0:T(1024)(128)(4,1)}), s8[4194304]{0:T(1024)(128)(4,1)S(1)}, s32[]{:S(2)}) async-start(s8[25165824]{0:T(1024)(128)(4,1)} %bitcast.38), calls=%async_computation.9 | async-start | bytes 8388608
  403.8 43.7 %slice-start.8 = ((s8[25165824]{0:T(1024)(128)(4,1)}), s8[4194304]{0:T(1024)(128)(4,1)S(1)}, s32[]{:S(2)}) async-start(s8[25165824]{0:T(1024)(128)(4,1)} %bitcast.38), calls=%async_computation.10 | async-start | bytes 8388608
  403.8 47.4 %collective-permute-start.23 = (bf16[256,2048]{1,0:T(8,128)(2,1)S(1)}, bf16[256,2048]{1,0:T(8,128)(2,1)S(1)}, u32[]{:S(2)}, u32[]{:S(2)}) collective-permute-start(bf16[256,2048]{1,0:T(8,128)(2,1)S(1)} %add_convert_fusion.1), channel_id=1, source_target_pairs={{1,0},{2,1},{3,2},{5,4},{6,5},{7,6},{9,8},{10,9},{11,10},{13,12},{... | collective-permute-start | bytes 3145736 | tf_op jit(solution)/shard_map/ppermute | solution.py:166
  416.5 31.1 %slice-start.9 = ((s8[25165824]{0:T(1024)(128)(4,1)}), s8[4194304]{0:T(1024)(128)(4,1)S(1)}, s32[]{:S(2)}) async-start(s8[25165824]{0:T(1024)(128)(4,1)} %bitcast.38), calls=%async_computation.11 | async-start | bytes 8388608
  416.5 31.1 %slice-start.10 = ((s8[25165824]{0:T(1024)(128)(4,1)}), s8[4194304]{0:T(1024)(128)(4,1)S(1)}, s32[]{:S(2)}) async-start(s8[25165824]{0:T(1024)(128)(4,1)} %bitcast.38), calls=%async_computation.12 | async-start | bytes 8388608
  416.5 40.0 %collective-permute-start.21 = (bf16[256,2048]{1,0:T(8,128)(2,1)S(1)}, bf16[256,2048]{1,0:T(8,128)(2,1)S(1)}, u32[]{:S(2)}, u32[]{:S(2)}) collective-permute-start(bf16[256,2048]{1,0:T(8,128)(2,1)S(1)} %add_convert_fusion.2), channel_id=1, source_target_pairs={{0,1},{1,2},{2,3},{4,5},{5,6},{6,7},{8,9},{9,10},{10,11},{12,13},{... | collective-permute-start | bytes 3145736 | tf_op jit(solution)/shard_map/ppermute | solution.py:165
  430.9 16.7 %slice-start.11 = ((s8[25165824]{0:T(1024)(128)(4,1)}), s8[4194304]{0:T(1024)(128)(4,1)S(1)}, s32[]{:S(2)}) async-start(s8[25165824]{0:T(1024)(128)(4,1)} %bitcast.38), calls=%async_computation.13 | async-start | bytes 8388608
  430.9 32.5 %collective-permute-start.17 = (bf16[256,2048]{1,0:T(8,128)(2,1)}, bf16[256,2048]{1,0:T(8,128)(2,1)S(1)}, u32[]{:S(2)}, u32[]{:S(2)}) collective-permute-start(bf16[256,2048]{1,0:T(8,128)(2,1)} %add_convert_fusion.5), channel_id=1, source_target_pairs={{1,0},{2,1},{3,2},{5,4},{6,5},{7,6},{9,8},{10,9},{11,10},{13,12},{... | collective-permute-start | bytes 3145736 | tf_op jit(solution)/shard_map/ppermute | solution.py:166
  438.6 40.0 %collective-permute-start.15 = (bf16[256,2048]{1,0:T(8,128)(2,1)S(1)}, bf16[256,2048]{1,0:T(8,128)(2,1)S(1)}, u32[]{:S(2)}, u32[]{:S(2)}) collective-permute-start(bf16[256,2048]{1,0:T(8,128)(2,1)S(1)} %add_convert_fusion.6), channel_id=1, source_target_pairs={{0,1},{1,2},{2,3},{4,5},{5,6},{6,7},{8,9},{9,10},{10,11},{12,13},{... | collective-permute-start | bytes 3145736 | tf_op jit(solution)/shard_map/ppermute | solution.py:165
Sparse Core Ops, SparseCore 0:
  125.3 72.2 all-gather.1

commit v2 on v0

v2 whole, which is shorter than its diff:
```python
import functools

import jax
import jax.numpy as jnp
from jax import lax
from jax.experimental import pallas as pl
from jax.experimental.pallas import tpu as pltpu
from jax.sharding import PartitionSpec as P

HD = 128
SPAN = 64
NBR_LEN = 128
NB_DEV = 2
NT = (((1,), (1,)), ((), ()))
MIB = 1024 * 1024
SMALL = pl.CostEstimate(flops=1, bytes_accessed=1, transcendentals=0)


def pair_of(first, second, column):
    return jnp.concatenate(
        [first[0, :, column : column + HD], second[0, :, column : column + HD]], axis=0
    )


def two_heads_of(first, second, head, offset):
    left, right = 2 * head * HD + offset, 2 * (head + 1) * HD + offset
    rows = [
        jnp.concatenate([ref[0, :, left : left + HD], ref[0, :, right : right + HD]], axis=1)
        for ref in (first, second)
    ]
    return jnp.concatenate(rows, axis=0)


def block_diagonal(ref, rows, head):
    left = ref[rows, head * HD : (head + 1) * HD]
    right = ref[rows, (head + 1) * HD : (head + 2) * HD]
    blank = jnp.zeros_like(left)
    return jnp.concatenate(
        [jnp.concatenate([left, blank], axis=1), jnp.concatenate([blank, right], axis=1)], axis=0
    )


def attend_kernel(heads, ids_ref, q_ref, *refs):
    del ids_ref
    out_ref = refs[-1]
    every = [(c, h) for c in range(len(refs) // 2) for h in range(heads)]
    rows = [slice(c * SPAN, (c + 1) * SPAN) for c, _ in every]
    scores = [
        lax.dot_general(
            q_ref[r, h * HD : (h + 1) * HD],
            pair_of(refs[2 * c], refs[2 * c + 1], 2 * h * HD),
            NT,
            preferred_element_type=jnp.float32,
        )
        for r, (c, h) in zip(rows, every)
    ]
    highest = [jnp.max(s, axis=1, keepdims=True) for s in scores]
    expo = [jnp.exp((s - m) * (HD**-0.5)) for s, m in zip(scores, highest)]
    inverse = [1.0 / jnp.sum(e, axis=1, keepdims=True) for e in expo]
    probs = [(e * r).astype(jnp.bfloat16) for e, r in zip(expo, inverse)]
    for p, r, (c, h) in zip(probs, rows, every):
        values = pair_of(refs[2 * c], refs[2 * c + 1], 2 * h * HD + HD)
        out = jnp.dot(p, values, preferred_element_type=jnp.float32)
        out_ref[r, h * HD : (h + 1) * HD] = out.astype(jnp.bfloat16)


def neighbour_specs(group, share):
    def spec(place):
        return pl.BlockSpec(
            (1, NBR_LEN, share), lambda c, ids, *_: (ids[2 * group * c + place], 0, 0)
        )

    return [spec(place) for place in range(2 * group)]


def attend(ids, queries, blocks, part):
    tokens = queries.shape[0]
    spans = tokens // SPAN
    share = blocks.shape[2]
    width = share // 2
    group = 2 if spans % 2 == 0 else 1
    return pl.pallas_call(
        functools.partial(attend_kernel, width // HD),
        grid_spec=pltpu.PrefetchScalarGridSpec(
            num_scalar_prefetch=1,
            grid=(spans // group,),
            in_specs=[pl.BlockSpec((group * SPAN, width), lambda c, ids: (c, part))]
            + neighbour_specs(group, share),
            out_specs=pl.BlockSpec((group * SPAN, width), lambda c, ids: (c, 0)),
        ),
        out_shape=jax.ShapeDtypeStruct((tokens, width), jnp.bfloat16),
        compiler_params=pltpu.CompilerParams(vmem_limit_bytes=42 * MIB),
        cost_estimate=SMALL,
        name="attend",
    )(ids, queries, *([blocks] * (2 * group)))


def attend_grad_kernel(group, parts, ids_ref, own_ref, q_ref, g_ref, *refs):
    del ids_ref
    out_ref, total_ref = refs[-2:]
    step = pl.program_id(0)

    @pl.when(step == 0)
    def _():
        total_ref[...] = jnp.zeros_like(total_ref)

    factor = HD**-0.5
    heads = q_ref.shape[1] // HD
    part_heads = heads // parts
    for c in range(group):
        tokens = slice(c * SPAN, (c + 1) * SPAN)
        places = (
            (own_ref[2 * (group * step + c)], slice(0, NBR_LEN)),
            (own_ref[2 * (group * step + c) + 1], slice(NBR_LEN, 2 * NBR_LEN)),
        )
        for part in range(parts):
            first_ref, second_ref = refs[2 * (group * part + c) : 2 * (group * part + c) + 2]
            pairs = range(0, part_heads, 2)
            query = [block_diagonal(q_ref, tokens, part * part_heads + h) for h in pairs]
            grad = [block_diagonal(g_ref, tokens, part * part_heads + h) for h in pairs]
            scores = [
                lax.dot_general(
                    two_heads_of(first_ref, second_ref, h, 0),
                    x,
                    NT,
                    preferred_element_type=jnp.float32,
                )
                for h, x in zip(pairs, query)
            ]
            grad_probs = [
                lax.dot_general(
                    two_heads_of(first_ref, second_ref, h, HD),
                    x,
                    NT,
                    preferred_element_type=jnp.float32,
                )
                for h, x in zip(pairs, grad)
            ]
            highest = [jnp.max(s, axis=0, keepdims=True) for s in scores]
            expo = [jnp.exp((s - m) * factor) for s, m in zip(scores, highest)]
            inverse = [1.0 / jnp.sum(e, axis=0, keepdims=True) for e in expo]
            probs = [e * r for e, r in zip(expo, inverse)]
            inner = [jnp.sum(p * d, axis=0, keepdims=True) for p, d in zip(probs, grad_probs)]
            grad_scores = [
                (p * (d - i)).astype(jnp.bfloat16) for p, d, i in zip(probs, grad_probs, inner)
            ]
            grad_keys = [
                jnp.dot(d, x, preferred_element_type=jnp.float32)
                for d, x in zip(grad_scores, query)
            ]
            grad_values = [
                jnp.dot(p.astype(jnp.bfloat16), x, preferred_element_type=jnp.float32)
                for p, x in zip(probs, grad)
            ]
            for h, keys, values in zip(pairs, grad_keys, grad_values):
                for i in range(2):
                    at = 2 * (part * part_heads + h + i) * HD
                    lanes = slice(i * HD, (i + 1) * HD)
                    for owner, rows in places:
                        total_ref[owner, :, at : at + HD] += keys[rows, lanes]
                        total_ref[owner, :, at + HD : at + 2 * HD] += values[rows, lanes]

    @pl.when(step == pl.num_programs(0) - 1)
    def _():
        for h in range(heads):
            at = 2 * h * HD
            out_ref[:, :, at : at + HD] = (total_ref[:, :, at : at + HD] * factor).astype(
                jnp.bfloat16
            )
            out_ref[:, :, at + HD : at + 2 * HD] = total_ref[
                :, :, at + HD : at + 2 * HD
            ].astype(jnp.bfloat16)


def attend_grad(ids, owners, owner_count, queries, grads, blocks):
    tokens, width = queries.shape
    spans = tokens // SPAN
    parts = len(blocks)
    part_share = blocks[0].shape[2]
    share = parts * part_share
    group = 2 if spans % 2 == 0 else 1
    return pl.pallas_call(
        functools.partial(attend_grad_kernel, group, parts),
        grid_spec=pltpu.PrefetchScalarGridSpec(
            num_scalar_prefetch=2,
            grid=(spans // group,),
            in_specs=[pl.BlockSpec((group * SPAN, width), lambda c, ids, own: (c, 0))] * 2
            + neighbour_specs(group, part_share) * parts,
            out_specs=pl.BlockSpec(
                (owner_count, NBR_LEN, share), lambda c, ids, own: (0, 0, 0)
            ),
            scratch_shapes=[pltpu.VMEM((owner_count, NBR_LEN, share), jnp.float32)],
        ),
        out_shape=jax.ShapeDtypeStruct((owner_count, NBR_LEN, share), jnp.bfloat16),
        compiler_params=pltpu.CompilerParams(vmem_limit_bytes=50 * MIB),
        cost_estimate=SMALL,
        name="attend_grad",
    )(ids, owners, queries, grads, *[b for b in blocks for _ in range(2 * group)])


def tile_of(width):
    return next(tile for tile in (512, 384, 256, HD) if width % tile == 0)


def project_kernel(parts, received, shard_ref, *refs):
    del shard_ref
    inputs, weights = refs[:parts], refs[parts : 2 * parts]
    total = jnp.dot(inputs[0][...], weights[0][...], preferred_element_type=jnp.float32)
    for x, w in zip(inputs[1:], weights[1:]):
        total = total + jnp.dot(x[...], w[...], preferred_element_type=jnp.float32)
    for r in refs[2 * parts : 2 * parts + received]:
        total = total + r[...].astype(jnp.float32)
    refs[-1][...] = total.astype(jnp.bfloat16)


def project(shard, inputs, w_out, width, received):
    parts = len(inputs)
    tokens, depth = inputs[0].shape
    tile = tile_of(width)
    steps = width // tile

    def weights_of(part):
        return pl.BlockSpec((depth, tile), lambda j, s: (part, s[0] * steps + j))

    return pl.pallas_call(
        functools.partial(project_kernel, parts, len(received)),
        grid_spec=pltpu.PrefetchScalarGridSpec(
            num_scalar_prefetch=1,
            grid=(steps,),
            in_specs=[pl.BlockSpec((tokens, depth), lambda j, s: (0, 0))] * parts
            + [weights_of(part) for part in range(parts)]
            + [pl.BlockSpec((tokens, tile), lambda j, s: (0, j))] * len(received),
            out_specs=pl.BlockSpec((tokens, tile), lambda j, s: (0, j)),
        ),
        out_shape=jax.ShapeDtypeStruct((tokens, width), jnp.bfloat16),
        compiler_params=pltpu.CompilerParams(vmem_limit_bytes=42 * MIB),
        cost_estimate=SMALL,
        name="project",
    )(shard.reshape(1), *inputs, *([w_out] * parts), *received)


def back_project_kernel(counts, carried, shards_ref, *refs):
    del shards_ref
    weights, out_ref = refs[: len(counts)], refs[-1]
    total = refs[-2][...] if carried else None
    at = len(counts)
    for count, weight in zip(counts, weights):
        block = refs[at][...]
        for other in refs[at + 1 : at + count]:
            block = block + other[...]
        at += count
        term = lax.dot_general(block, weight[...], NT, preferred_element_type=jnp.float32)
        total = term if total is None else total + term
    out_ref[...] = total.astype(out_ref.dtype)


def back_project(groups, w_out, carry, out_type):
    tokens, depth = groups[0][1][0].shape
    head_width = w_out.shape[0]
    tile = tile_of(head_width)
    blocks = [block for _, sources in groups for block in sources]
    extra = [] if carry is None else [carry]

    def weights_of(group):
        return pl.BlockSpec((tile, depth), lambda j, s: (j, s[group]))

    return pl.pallas_call(
        functools.partial(
            back_project_kernel, [len(sources) for _, sources in groups], carry is not None
        ),
        grid_spec=pltpu.PrefetchScalarGridSpec(
            num_scalar_prefetch=1,
            grid=(head_width // tile,),
            in_specs=[weights_of(group) for group in range(len(groups))]
            + [pl.BlockSpec((tokens, depth), lambda j, s: (0, 0), pipeline_mode=pl.Buffered(1))]
            * len(blocks)
            + [pl.BlockSpec((tokens, tile), lambda j, s: (0, j))] * len(extra),
            out_specs=pl.BlockSpec((tokens, tile), lambda j, s: (0, j)),
        ),
        out_shape=jax.ShapeDtypeStruct((tokens, head_width), out_type),
        compiler_params=pltpu.CompilerParams(vmem_limit_bytes=48 * MIB),
        cost_estimate=SMALL,
        name="back_project",
    )(jnp.stack([shard for shard, _ in groups]), *([w_out] * len(groups)), *blocks, *extra)


def after(x, *others):
    return lax.optimization_barrier((x, *others))[0]


FAR, NEAR, BESIDE = (3, 3, 0, 0), (2, 2, 1, 1), (1, 0, 3, 2)
INWARDS = [(0, 1), (3, 2)]
OUTWARDS = [(1, 0), (2, 3)]
SWAP = [(0, 1), (1, 0), (2, 3), (3, 2)]
ACROSS = [(1, 2), (2, 1)]
TWO_ON = [(1, 3), (2, 0)]
TWO_IN = [(3, 1), (0, 2)]


def send(x, hops):
    return lax.ppermute(x, "tensor", hops)


def entry(table, me):
    return jnp.take(jnp.array(table, jnp.int32), me)


class LineSum:
    def __init__(self, term, me):
        self.term, self.me = term, me
        self.far = term(entry(FAR, me), [])
        self.far_in = send(self.far, INWARDS)
        self.near = term(after(entry(NEAR, me), self.far), [])
        self.near_in = send(self.near, INWARDS)
        self.beside = term(after(entry(BESIDE, me), self.near), [])
        self.beside_in = send(self.beside, SWAP)

    def add_far(self, *others):
        self.far_sum = self.far + after(self.far_in, *others)
        self.far_in = send(self.far_sum, TWO_ON)

    def add_near(self, *others):
        self.near_sum = self.near + after(self.near_in, *others)
        self.near_in = send(self.near_sum, ACROSS)

    def finish(self):
        return self.term(self.me, [self.beside_in, self.far_in, self.near_in])


def settle_kernel(slot_ref, returned_ref, out_ref):
    totals = [jnp.zeros(returned_ref.shape[1:], jnp.float32) for _ in range(NB_DEV)]
    for r in range(returned_ref.shape[0]):
        block = returned_ref[r].astype(jnp.float32)
        for slot in range(NB_DEV):
            totals[slot] = totals[slot] + jnp.where(slot_ref[r] == slot, block, 0.0)
    for slot in range(NB_DEV):
        out_ref[slot * NBR_LEN : (slot + 1) * NBR_LEN] = totals[slot].astype(jnp.bfloat16)


def settle(slots, returned):
    readers, _, width = returned.shape
    tile = next(tile for tile in (1024, 768, 512, 256, HD) if width % tile == 0)
    return pl.pallas_call(
        settle_kernel,
        grid_spec=pltpu.PrefetchScalarGridSpec(
            num_scalar_prefetch=1,
            grid=(width // tile,),
            in_specs=[pl.BlockSpec((readers, NBR_LEN, tile), lambda j, s: (0, 0, j))],
            out_specs=pl.BlockSpec((NB_DEV * NBR_LEN, tile), lambda j, s: (0, j)),
        ),
        out_shape=jax.ShapeDtypeStruct((NB_DEV * NBR_LEN, width), jnp.bfloat16),
        compiler_params=pltpu.CompilerParams(vmem_limit_bytes=42 * MIB),
        cost_estimate=SMALL,
        name="settle",
    )(slots, returned)


def local(kv_part, queries, w_out, d_out, nbr_owner, nbr_slot):
    dp_count = lax.axis_size("dp")
    count = lax.axis_size("tensor")
    reader = lax.axis_index("dp")
    me = lax.axis_index("tensor")
    tokens, head_width = queries.shape
    share_width = 2 * head_width
    span_count = tokens // SPAN
    read_count = 2 * span_count
    out_width = d_out.shape[1]

    owner_ids = jnp.arange(dp_count, dtype=jnp.int32)
    per_reader = (nbr_owner[:, :, None] == owner_ids[None, None, :]).reshape(
        dp_count, read_count, dp_count
    )
    slot_from = jnp.max(
        jnp.where(per_reader, nbr_slot.reshape(dp_count, read_count, 1), 0), axis=1
    )
    owners = lax.dynamic_slice_in_dim(nbr_owner, reader * span_count, span_count, 0).reshape(
        read_count
    )
    slots = lax.dynamic_slice_in_dim(nbr_slot, reader * span_count, span_count, 0).reshape(
        read_count
    )
    ids = owners * NB_DEV + slots
    serving_slot = lax.dynamic_index_in_dim(slot_from, reader, 1, False)

    def kv_term(shard, received):
        total = lax.dynamic_slice_in_dim(
            kv_part[0], shard * share_width, share_width, 1
        ).astype(jnp.float32)
        for r in received:
            total = total + r.astype(jnp.float32)
        return total.astype(jnp.bfloat16)

    if count == 4:
        across = send(d_out, ACROSS)
        outwards = send(d_out, OUTWARDS)
        line = LineSum(kv_term, me)
        line.add_far(across, outwards)
        line.add_near(line.far_in)
        share = line.finish()
        two_in = send(after(d_out, line.near_sum), TWO_IN)
        inwards = send(after(d_out, two_in), INWARDS)
        groups = [
            (entry(range(4), me), [d_out]),
            (entry(NEAR, me), [across, send(after(across, line.near_sum), OUTWARDS)]),
            (entry(BESIDE, me), [inwards, outwards]),
            (entry(FAR, me), [two_in, send(two_in, OUTWARDS)]),
        ]
    else:
        share = lax.psum_scatter(kv_part[0], "tensor", scatter_dimension=1, tiled=True)
        gathered = lax.all_gather(d_out, "tensor", axis=0)
        groups = [(jnp.int32(s), [gathered[s]]) for s in range(count)]
    blocks = lax.all_gather(
        share.reshape(NB_DEV, NBR_LEN, share_width), "dp", axis=0, tiled=True
    )

    def mixed_term(shard, received):
        return project(shard, [attended], w_out, out_width, received)

    if count == 4:
        grads = back_project(groups[:1], w_out, None, jnp.float32)
        attended = attend(after(ids, grads), queries, blocks, 0)
        line = LineSum(mixed_term, me)
        first = (after(groups[1][0], line.beside), groups[1][1])
        grads = back_project([first] + groups[2:], w_out, grads, jnp.bfloat16)
        own_sums = attend_grad(ids, owners, dp_count, queries, grads, [blocks])
        line.add_far(own_sums)
        line.add_near(line.far_in)
        mixed = line.finish()
    else:
        attended = attend(ids, queries, blocks, 0)
        partial = jnp.concatenate(
            [mixed_term(jnp.int32(s), []) for s in range(count)], axis=1
        )
        mixed = lax.psum_scatter(partial, "tensor", scatter_dimension=1, tiled=True)
        grads = None
        for at in range(count):
            last = at == count - 1
            grads = back_project(
                groups[at : at + 1], w_out, grads, jnp.bfloat16 if last else jnp.float32
            )
        own_sums = attend_grad(ids, owners, dp_count, queries, grads, [blocks])
    returned = lax.all_to_all(own_sums, "dp", split_axis=0, concat_axis=0, tiled=True)
    return (mixed, settle(serving_slot, returned))


def solution(mesh):
    placed = (
        P("tensor", "dp", None),
        P("dp", "tensor"),
        P("tensor", None),
        P("dp", "tensor"),
        P(),
        P(),
    )
    return jax.shard_map(
        local,
        mesh=mesh,
        in_specs=placed,
        out_specs=(P("dp", "tensor"), P("dp", "tensor")),
        check_vma=False,
    )
```

time: 792 us -> 414 us (0.52)
  waiting for transfers between devices: 391 us -> 214 us
  local copies, waits for them, and re-layouts: 185 us -> 14.6 us
  matrix products: 156 us -> 0 us
  Pallas kernels: 0 us -> 86.2 us
  starting transfers between devices: 5.37 us -> 59 us
  other arithmetic: 33 us -> 17.2 us
    psum x1 -> x0, waiting for transfers between devices: 228 us -> none  [local(): summed = lax.psum(local_partial, 'tensor').astype(jnp.float32)]
    ppermute x0 -> x16, waiting for transfers between devices: none -> 195 us  [send(): return lax.ppermute(x, 'tensor', hops)]
    dot_general x10 -> x0, matrix products: 156 us -> none  [the longest x1 20.5 us: local(): lax.dot_general(lax.all_gather(d_out, 'tensor', axis=1, tiled=True), w_ou...]
    pallas_call x0 -> x9, Pallas kernels: none -> 86.2 us  [the longest x4 27.6 us: project(): pl.pallas_call(functools.partial(project_kernel, parts, len(received)), g...]
    all_gather x2 -> x1, waiting for transfers between devices: 91.6 us -> 9.15 us  [local(): lax.all_gather(share.reshape(NB_DEV, NBR_LEN, share_width), 'dp', axis=0,...]
    reshape x5 -> x0, local copies, waits for them, and re-layouts: 73.7 us -> none  [the longest x1 42 us: local(): jnp.stack([grad_keys, grad_values], axis=3).reshape(read_count, block_width)]
    all_to_all x1, waiting for transfers between devices: 70.4 us -> 9.84 us  [local(): lax.all_to_all(own_sums, 'dp', split_axis=0, concat_axis=0, tiled=True)]
    ppermute x0 -> x16, starting transfers between devices: none -> 54.2 us  [send(): return lax.ppermute(x, 'tensor', hops)]
  transfers between devices with their start and end apart: 5 -> 18, of which waited for: 4 -> 10; matrix products, arithmetic and copies ran while one was open for 47% -> 5% of each run, Pallas kernels for 0% -> 19%
where the time goes in v2:
time: 414 us; the launch traced here: 407 us
  waiting for transfers between devices  214 us (52%)
  Pallas kernels  86.2 us (21%)
  starting transfers between devices  59 us (14%)
  other arithmetic  17.2 us (4%)
  between operations  16.2 us (4%)
  local copies, waits for them, and re-layouts  14.6 us (4%)
    ppermute x16, waiting for transfers between devices, send(): return lax.ppermute(x, 'tensor', hops)  195 us
    ppermute x16, starting transfers between devices, send(): return lax.ppermute(x, 'tensor', hops)  54.2 us
    pallas_call x4, Pallas kernels, project(): pl.pallas_call(functools.partial(project_kernel, parts, len(received)), g...  27.6 us
    pallas_call x2, Pallas kernels, back_project(): pl.pallas_call(functools.partial(back_project_kernel, [len(sources) for _...  25.2 us
    pallas_call x1, Pallas kernels, attend_grad(): pl.pallas_call(functools.partial(attend_grad_kernel, group, parts), grid_...  18.9 us
    all_to_all x1, waiting for transfers between devices, local(): lax.all_to_all(own_sums, 'dp', split_axis=0, concat_axis=0, tiled=True)  9.84 us
    all_gather x1, waiting for transfers between devices, local(): lax.all_gather(share.reshape(NB_DEV, NBR_LEN, share_width), 'dp', axis=0,...  9.15 us
  transfers between devices with their start and end apart: 18, of which 10 were waited for; matrix products, arithmetic and copies ran while one was open for 5% of the time, Pallas kernels for 19%

profile of v2, /device:TPU:0, one launch (start us, length us, event | category | flops | bytes accessed | tf_op | source)
XLA Modules:
  0.0 407.3 jit_solution(1764642011772366729)
XLA Ops:
  7.2 0.0 all-gather.2.cloned.1.call-start
  7.2 1.3 collective-permute-start.3
  8.5 2.0 collective-permute-start.2
  10.5 1.2 dynamic-slice.21
  12.4 2.7 dynamic-slice_bitcast_fusion.2
  15.1 9.9 %collective-permute-start.1 = (bf16[256,3072]{1,0:T(8,128)(2,1)}, bf16[256,3072]{1,0:T(8,128)(2,1)}, u32[]{:S(2)}, u32[]{:S(2)}) collective-permute-start(bf16[256,3072]{1,0:T(8,128)(2,1)} %dynamic-slice_bitcast_fusion.2), channel_id=1, source_target_pairs={{0,1},{3,2},{4,5},{7,6},{8,9},{11,10},{12,13},{15,14},{16,17},{19,... | collective-permute-start | bytes 4718600 | tf_op jit(solution)/shard_map/ppermute | solution.py:301
  25.0 0.6 dynamic-slice.20
  26.2 2.7 dynamic-slice_bitcast_fusion.1
  28.9 2.6 collective-permute-start.5
  31.5 27.5 %collective-permute-done.1 = bf16[256,3072]{1,0:T(8,128)(2,1)} collective-permute-done((bf16[256,3072]{1,0:T(8,128)(2,1)}, bf16[256,3072]{1,0:T(8,128)(2,1)}, u32[]{:S(2)}, u32[]{:S(2)}) %collective-permute-start.1) | collective-permute-done | bytes 1572896 | tf_op jit(solution)/shard_map/ppermute | solution.py:301
  59.0 4.4 %fusion.4 = bf16[256,3072]{1,0:T(8,128)(2,1)} fusion(bf16[256,3072]{1,0:T(8,128)(2,1)} %collective-permute-done.1, bf16[1,256,12288]{2,1,0:T(8,128)(2,1)} %param.16, s32[]{:T(128)S(6)} %select_n.76), kind=kLoop, calls=%fused_computation.15 | loop fusion | flops 3145728 | bytes 4718596 | tf_op jit(solution)/shard_map/add | solution.py:319
  63.4 1.3 collective-permute-start.4
  64.7 0.6 dynamic-slice.19
  65.9 1.5 dynamic-slice_bitcast_fusion
  67.4 5.1 %collective-permute-start = (bf16[256,3072]{1,0:T(8,128)(2,1)S(1)}, bf16[256,3072]{1,0:T(8,128)(2,1)}, u32[]{:S(2)}, u32[]{:S(2)}) collective-permute-start(bf16[256,3072]{1,0:T(8,128)(2,1)S(1)} %dynamic-slice_bitcast_fusion), channel_id=1, source_target_pairs={{0,1},{1,0},{2,3},{3,2},{4,5},{5,4},{6,7},{7,6},{8,9},{9,8},{10,11... | collective-permute-start | bytes 4718600 | tf_op jit(solution)/shard_map/ppermute | solution.py:301
  72.5 20.2 %collective-permute-done.5 = bf16[256,3072]{1,0:T(8,128)(2,1)} collective-permute-done((bf16[256,3072]{1,0:T(8,128)(2,1)}, bf16[256,3072]{1,0:T(8,128)(2,1)}, u32[]{:S(2)}, u32[]{:S(2)}) %collective-permute-start.5) | collective-permute-done | bytes 1572896 | tf_op jit(solution)/shard_map/ppermute | solution.py:301
  92.7 10.0 %collective-permute-done.4 = bf16[256,3072]{1,0:T(8,128)(2,1)} collective-permute-done((bf16[256,3072]{1,0:T(8,128)(2,1)}, bf16[256,3072]{1,0:T(8,128)(2,1)}, u32[]{:S(2)}, u32[]{:S(2)}) %collective-permute-start.4) | collective-permute-done | bytes 1572896 | tf_op jit(solution)/shard_map/ppermute | solution.py:301
  102.7 2.5 fusion.3
  105.2 1.8 collective-permute-start.6
  107.0 29.3 %collective-permute-done = bf16[256,3072]{1,0:T(8,128)(2,1)} collective-permute-done((bf16[256,3072]{1,0:T(8,128)(2,1)S(1)}, bf16[256,3072]{1,0:T(8,128)(2,1)}, u32[]{:S(2)}, u32[]{:S(2)}) %collective-permute-start) | collective-permute-done | bytes 1572896 | tf_op jit(solution)/shard_map/ppermute | solution.py:301
  136.3 5.0 %fusion.2 = bf16[256,3072]{1,0:T(8,128)(2,1)} fusion(bf16[256,3072]{1,0:T(8,128)(2,1)} %collective-permute-done.6, bf16[256,3072]{1,0:T(8,128)(2,1)} %collective-permute-done.4, bf16[256,3072]{1,0:T(8,128)(2,1)} %collective-permute-done, bf16[1,256,12288]{2,1,0:T(8,128)(2,1)} %param.16, s32[]{:T(128)S(6)} %select_n.72), kind=kLoop, calls=%fused_computation.3 | loop fusion | flops 6291456 | bytes 7864324 | tf_op jit(solution)/shard_map/convert_element_type | solution.py:391
  141.3 0.0 all-gather.2.cloned.1.call-update
  141.3 7.9 %collective-permute-start.10 = (bf16[512,2048]{1,0:T(8,128)(2,1)}, bf16[512,2048]{1,0:T(8,128)(2,1)}, u32[]{:S(2)}, u32[]{:S(2)}) collective-permute-start(bf16[512,2048]{1,0:T(8,128)(2,1)} %refs_1_.6), channel_id=1, source_target_pairs={{3,1},{0,2},{7,5},{4,6},{11,9},{8,10},{15,13},{12,14},{19,17},{16,... | collective-permute-start | bytes 6291464 | tf_op jit(solution)/shard_map/ppermute | solution.py:301
  149.2 1.3 collective-permute-start.9
  150.5 39.8 %collective-permute-done.10.refs_7_ = bf16[512,2048]{1,0:T(8,128)(2,1)} collective-permute-done((bf16[512,2048]{1,0:T(8,128)(2,1)}, bf16[512,2048]{1,0:T(8,128)(2,1)}, u32[]{:S(2)}, u32[]{:S(2)}) %collective-permute-start.10) | collective-permute-done | bytes 2097184 | tf_op jit(solution)/shard_map/ppermute | solution.py:301
  190.3 6.3 %collective-permute-start.11 = (bf16[512,2048]{1,0:T(8,128)(2,1)}, bf16[512,2048]{1,0:T(8,128)(2,1)}, u32[]{:S(2)}, u32[]{:S(2)}) collective-permute-start(bf16[512,2048]{1,0:T(8,128)(2,1)} %refs_1_.6), channel_id=1, source_target_pairs={{0,1},{3,2},{4,5},{7,6},{8,9},{11,10},{12,13},{15,14},{16,17},{19,... | collective-permute-start | bytes 6291464 | tf_op jit(solution)/shard_map/ppermute | solution.py:301
  196.6 1.3 collective-permute-start.12
  198.0 6.7 %back_project.2.refs_9_ = f32[512,1536]{1,0:T(8,128)S(1)} custom-call(s32[1]{0:T(128)S(6)} %select_n.87.shards_ref, bf16[1536,8192]{1,0:T(8,128)(2,1)} %refs_1_.11, bf16[512,2048]{1,0:T(8,128)(2,1)} %refs_1_.6), custom_call_target="tpu_custom_call" | custom-call | flops 1 | bytes 1 | tf_op jit(solution)/shard_map/back_project/pallas_call | solution.py:267
  204.7 1.6 copy-done
  206.3 0.1 constant_dynamic-slice_fusion
  206.4 0.1 copy.35
  206.5 0.1 reshape.40
  206.6 0.1 copy.34
  206.7 0.1 reshape.39.own_ref
  206.7 9.1 %all-gather.2.cloned.1.call-done.refs_0_.refs_1_.refs_2_.refs_3_ = bf16[16,128,3072]{2,1,0:T(8,128)(2,1)} async-done(((bf16[2,128,3072]{2,1,0:T(8,128)(2,1)}), bf16[16,128,3072]{2,1,0:T(8,128)(2,1)}) %all-gather.2.cloned.1.call-update) | async-done | bytes 12582928 | tf_op jit(solution)/shard_map/all_gather | solution.py:412
  215.9 8.0 %attend.1.refs_0_ = bf16[512,1536]{1,0:T(8,128)(2,1)S(1)} custom-call(s32[16]{0:T(128)S(1)} %multiply_add_fusion.ids_ref, bf16[512,1536]{1,0:T(8,128)(2,1)S(1)} %copy-done.3, bf16[16,128,3072]{2,1,0:T(8,128)(2,1)} %all-gather.2.cloned.1.call-done.refs_0_.refs_1_.refs_2_.refs_3_, ...), custom_call_target="tpu_custom_call" | custom-call | flops 1 | bytes 1 | tf_op jit(solution)/shard_map/attend/pallas_call | solution.py:82
  223.9 6.9 %project.4 = bf16[512,2048]{1,0:T(8,128)(2,1)} custom-call(s32[1]{0:T(128)S(6)} %select_n.90.shard_ref, bf16[512,1536]{1,0:T(8,128)(2,1)S(1)} %attend.1.refs_0_, bf16[1536,8192]{1,0:T(8,128)(2,1)} %refs_1_.11), custom_call_target="tpu_custom_call" | custom-call | flops 1 | bytes 1 | tf_op jit(solution)/shard_map/project/pallas_call | solution.py:225
  230.8 4.8 %collective-permute-start.8 = (bf16[512,2048]{1,0:T(8,128)(2,1)}, bf16[512,2048]{1,0:T(8,128)(2,1)}, u32[]{:S(2)}, u32[]{:S(2)}) collective-permute-start(bf16[512,2048]{1,0:T(8,128)(2,1)} %project.4), channel_id=1, source_target_pairs={{0,1},{3,2},{4,5},{7,6},{8,9},{11,10},{12,13},{15,14},{16,17},{19,... | collective-permute-start | bytes 6291464 | tf_op jit(solution)/shard_map/ppermute | solution.py:301
  235.6 6.0 %project.5 = bf16[512,2048]{1,0:T(8,128)(2,1)S(1)} custom-call(s32[1]{0:T(128)} %bitcast.11.shard_ref, bf16[512,1536]{1,0:T(8,128)(2,1)S(1)} %attend.1.refs_0_, bf16[1536,8192]{1,0:T(8,128)(2,1)} %refs_1_.11), custom_call_target="tpu_custom_call" | custom-call | flops 1 | bytes 1 | tf_op jit(solution)/shard_map/project/pallas_call | solution.py:225
  241.6 1.4 copy-done.1
  243.0 6.9 %project.6 = bf16[512,2048]{1,0:T(8,128)(2,1)} custom-call(s32[1]{0:T(128)} %bitcast.12.shard_ref, bf16[512,1536]{1,0:T(8,128)(2,1)S(1)} %attend.1.refs_0_, bf16[1536,8192]{1,0:T(8,128)(2,1)} %refs_1_.11), custom_call_target="tpu_custom_call" | custom-call | flops 1 | bytes 1 | tf_op jit(solution)/shard_map/project/pallas_call | solution.py:225
  249.9 0.1 pad_add_fusion.shards_ref
  249.9 18.5 %back_project.3.g_ref = bf16[512,1536]{1,0:T(8,128)(2,1)S(1)} custom-call(s32[3]{0:T(128)S(1)} %pad_add_fusion.shards_ref, bf16[1536,8192]{1,0:T(8,128)(2,1)} %refs_1_.11, bf16[1536,8192]{1,0:T(8,128)(2,1)} %refs_1_.11, bf16[1536,8192]{1,0:T(8,128)(2,1)} %refs_1_.11, bf16[512,2048]{1,0:T(8,128)(2,1)} %collective-permute-done.2.refs_3_, ...), custom_call_target="tpu_custom_call" | custom-call | flops 1 | bytes 1 | tf_op jit(solution)/shard_map/back_project/pallas_call | solution.py:267
  268.5 18.9 %attend_grad.1 = bf16[8,128,3072]{2,1,0:T(8,128)(2,1)} custom-call(s32[16]{0:T(128)S(1)} %multiply_add_fusion.ids_ref, s32[16]{0:T(128)S(1)} %reshape.39.own_ref, bf16[512,1536]{1,0:T(8,128)(2,1)S(1)} %copy-done.3, bf16[512,1536]{1,0:T(8,128)(2,1)S(1)} %back_project.3.g_ref, ...), custom_call_target="tpu_custom_call" | custom-call | flops 1 | bytes 1 | tf_op jit(solution)/shard_map/attend_grad/pallas_call | solution.py:182
  287.4 4.7 %all-to-all-start = ((bf16[8,128,3072]{2,1,0:T(8,128)(2,1)}), bf16[8,128,3072]{2,1,0:T(8,128)(2,1)}, u32[]{:S(2)}, u32[]{:S(2)}) async-start(bf16[8,128,3072]{2,1,0:T(8,128)(2,1)} %attend_grad.1), calls=%async_computation | async-start | bytes 12582912 | tf_op jit(solution)/shard_map/all_to_all | solution.py:442
  292.2 1.6 collective-permute-start.14
  293.8 3.0 add.69
  296.8 1.3 collective-permute-start.13
  298.1 3.8 collective-permute-start.7
  301.8 38.1 %collective-permute-done.14 = bf16[512,2048]{1,0:T(8,128)(2,1)S(1)} collective-permute-done((bf16[512,2048]{1,0:T(8,128)(2,1)}, bf16[512,2048]{1,0:T(8,128)(2,1)S(1)}, u32[]{:S(2)}, u32[]{:S(2)}) %collective-permute-start.14) | collective-permute-done | bytes 2097184 | tf_op jit(solution)/shard_map/ppermute | solution.py:301
  339.9 7.8 %collective-permute-done.13.refs_3_ = bf16[512,2048]{1,0:T(8,128)(2,1)S(1)} collective-permute-done((bf16[512,2048]{1,0:T(8,128)(2,1)S(1)}, bf16[512,2048]{1,0:T(8,128)(2,1)S(1)}, u32[]{:S(2)}, u32[]{:S(2)}) %collective-permute-start.13) | collective-permute-done | bytes 2097184 | tf_op jit(solution)/shard_map/ppermute | solution.py:301
  347.7 1.4 copy-done.4
  349.1 2.1 add.70
  351.2 2.0 collective-permute-start.15
  353.2 0.1 copy.36
  353.3 0.1 copy.37
  353.4 0.1 eq.16
  353.4 0.1 broadcast_in_dim.30
  353.5 0.2 select_reduce_fusion
  353.7 0.2 dynamic-slice_reduce_fusion.slot_ref
  353.9 9.8 %all-to-all-done.returned_ref = bf16[8,128,3072]{2,1,0:T(8,128)(2,1)} async-done(((bf16[8,128,3072]{2,1,0:T(8,128)(2,1)}), bf16[8,128,3072]{2,1,0:T(8,128)(2,1)}, u32[]{:S(2)}, u32[]{:S(2)}) %all-to-all-start) | async-done | bytes 6291488 | tf_op jit(solution)/shard_map/all_to_all | solution.py:442
  363.8 6.4 %settle.1 = bf16[256,3072]{1,0:T(8,128)(2,1)} custom-call(s32[8]{0:T(128)S(1)} %dynamic-slice_reduce_fusion.slot_ref, bf16[8,128,3072]{2,1,0:T(8,128)(2,1)} %all-to-all-done.returned_ref), custom_call_target="tpu_custom_call" | custom-call | flops 1 | bytes 1 | tf_op jit(solution)/shard_map/settle/pallas_call | solution.py:343
  370.2 22.5 %collective-permute-done.7.refs_2_ = bf16[512,2048]{1,0:T(8,128)(2,1)} collective-permute-done((bf16[512,2048]{1,0:T(8,128)(2,1)}, bf16[512,2048]{1,0:T(8,128)(2,1)}, u32[]{:S(2)}, u32[]{:S(2)}) %collective-permute-start.7) | collective-permute-done | bytes 2097184 | tf_op jit(solution)/shard_map/ppermute | solution.py:301
  392.6 7.8 %project.7 = bf16[512,2048]{1,0:T(8,128)(2,1)} custom-call(s32[1]{0:T(128)} %bitcast.shard_ref, bf16[512,1536]{1,0:T(8,128)(2,1)S(1)} %attend.1.refs_0_, bf16[1536,8192]{1,0:T(8,128)(2,1)} %refs_1_.11, bf16[512,2048]{1,0:T(8,128)(2,1)} %collective-permute-done.7.refs_2_, bf16[512,2048]{1,0:T(8,128)(2,1)S(1)} %copy-done.5, ...), custom_call_target="tpu_custom_call" | custom-call | flops 1 | bytes 1 | tf_op jit(solution)/shard_map/project/pallas_call | solution.py:225
  (28 shorter events, 0.1 us)
Async XLA Ops:
  7.2 17.8 %copy-start.10 = (s32[4]{0:T(128)S(1)}, s32[4]{0:T(128)}, u32[]{:S(2)}) copy-start(s32[4]{0:T(128)} %constant.109.clone..sunk.2) | copy-start | bytes 52
  7.2 208.7 %all-gather.2.cloned.1.call-start = ((), (), s32[]{:S(2)}) async-start(), calls=%async_computation.1 | async-start | bytes 14155776 | tf_op jit(solution)/shard_map/all_gather | solution.py:412
  7.2 51.8 %collective-permute-start.3 = (bf16[512,2048]{1,0:T(8,128)(2,1)}, bf16[512,2048]{1,0:T(8,128)(2,1)S(1)}, u32[]{:S(2)}, u32[]{:S(2)}) collective-permute-start(bf16[512,2048]{1,0:T(8,128)(2,1)} %refs_1_.6), channel_id=1, source_target_pairs={{1,0},{2,3},{5,4},{6,7},{9,8},{10,11},{13,12},{14,15},{17,16},{18,... | collective-permute-start | bytes 6291464 | tf_op jit(solution)/shard_map/ppermute | solution.py:301
  8.5 50.5 %collective-permute-start.2 = (bf16[512,2048]{1,0:T(8,128)(2,1)}, bf16[512,2048]{1,0:T(8,128)(2,1)}, u32[]{:S(2)}, u32[]{:S(2)}) collective-permute-start(bf16[512,2048]{1,0:T(8,128)(2,1)} %refs_1_.6), channel_id=1, source_target_pairs={{1,2},{2,1},{5,6},{6,5},{9,10},{10,9},{13,14},{14,13},{17,18},{18,... | collective-permute-start | bytes 6291464 | tf_op jit(solution)/shard_map/ppermute | solution.py:301
  15.1 43.9 %collective-permute-start.1 = (bf16[256,3072]{1,0:T(8,128)(2,1)}, bf16[256,3072]{1,0:T(8,128)(2,1)}, u32[]{:S(2)}, u32[]{:S(2)}) collective-permute-start(bf16[256,3072]{1,0:T(8,128)(2,1)} %dynamic-slice_bitcast_fusion.2), channel_id=1, source_target_pairs={{0,1},{3,2},{4,5},{7,6},{8,9},{11,10},{12,13},{15,14},{16,17},{19,... | collective-permute-start | bytes 4718600 | tf_op jit(solution)/shard_map/ppermute | solution.py:301
  28.9 35.8 %copy-start.9 = (s32[4]{0:T(128)S(1)}, s32[4]{0:T(128)}, u32[]{:S(2)}) copy-start(s32[4]{0:T(128)} %constant.110.clone..sunk.2) | copy-start | bytes 52
  28.9 63.8 %collective-permute-start.5 = (bf16[256,3072]{1,0:T(8,128)(2,1)}, bf16[256,3072]{1,0:T(8,128)(2,1)}, u32[]{:S(2)}, u32[]{:S(2)}) collective-permute-start(bf16[256,3072]{1,0:T(8,128)(2,1)} %dynamic-slice_bitcast_fusion.1), channel_id=1, source_target_pairs={{0,1},{3,2},{4,5},{7,6},{8,9},{11,10},{12,13},{15,14},{16,17},{19,... | collective-permute-start | bytes 4718600 | tf_op jit(solution)/shard_map/ppermute | solution.py:301
  59.0 4.4 %copy-start.6 = (bf16[512,2048]{1,0:T(8,128)(2,1)}, bf16[512,2048]{1,0:T(8,128)(2,1)S(1)}, u32[]{:S(2)}) copy-start(bf16[512,2048]{1,0:T(8,128)(2,1)S(1)} %collective-permute-done.3.refs_6_) | copy-start | bytes 6291460
  63.4 39.3 %collective-permute-start.4 = (bf16[256,3072]{1,0:T(8,128)(2,1)}, bf16[256,3072]{1,0:T(8,128)(2,1)}, u32[]{:S(2)}, u32[]{:S(2)}) collective-permute-start(bf16[256,3072]{1,0:T(8,128)(2,1)} %fusion.4), channel_id=1, source_target_pairs={{1,3},{2,0},{5,7},{6,4},{9,11},{10,8},{13,15},{14,12},{17,19},{18,... | collective-permute-start | bytes 4718600 | tf_op jit(solution)/shard_map/ppermute | solution.py:301
  67.4 68.9 %collective-permute-start = (bf16[256,3072]{1,0:T(8,128)(2,1)S(1)}, bf16[256,3072]{1,0:T(8,128)(2,1)}, u32[]{:S(2)}, u32[]{:S(2)}) collective-permute-start(bf16[256,3072]{1,0:T(8,128)(2,1)S(1)} %dynamic-slice_bitcast_fusion), channel_id=1, source_target_pairs={{0,1},{1,0},{2,3},{3,2},{4,5},{5,4},{6,7},{7,6},{8,9},{9,8},{10,11... | collective-permute-start | bytes 4718600 | tf_op jit(solution)/shard_map/ppermute | solution.py:301
  105.2 31.1 %collective-permute-start.6 = (bf16[256,3072]{1,0:T(8,128)(2,1)S(1)}, bf16[256,3072]{1,0:T(8,128)(2,1)}, u32[]{:S(2)}, u32[]{:S(2)}) collective-permute-start(bf16[256,3072]{1,0:T(8,128)(2,1)S(1)} %fusion.3), channel_id=1, source_target_pairs={{1,2},{2,1},{5,6},{6,5},{9,10},{10,9},{13,14},{14,13},{17,18},{18,... | collective-permute-start | bytes 4718600 | tf_op jit(solution)/shard_map/ppermute | solution.py:301
  141.3 49.0 %collective-permute-start.10 = (bf16[512,2048]{1,0:T(8,128)(2,1)}, bf16[512,2048]{1,0:T(8,128)(2,1)}, u32[]{:S(2)}, u32[]{:S(2)}) collective-permute-start(bf16[512,2048]{1,0:T(8,128)(2,1)} %refs_1_.6), channel_id=1, source_target_pairs={{3,1},{0,2},{7,5},{4,6},{11,9},{8,10},{15,13},{12,14},{19,17},{16,... | collective-permute-start | bytes 6291464 | tf_op jit(solution)/shard_map/ppermute | solution.py:301
  149.2 100.7 %collective-permute-start.9 = (bf16[512,2048]{1,0:T(8,128)(2,1)}, bf16[512,2048]{1,0:T(8,128)(2,1)}, u32[]{:S(2)}, u32[]{:S(2)}) collective-permute-start(bf16[512,2048]{1,0:T(8,128)(2,1)} %collective-permute-done.2.refs_3_), channel_id=1, source_target_pairs={{1,0},{2,3},{5,4},{6,7},{9,8},{10,11},{13,12},{14,15},{17,16},{18,... | collective-permute-start | bytes 6291464 | tf_op jit(solution)/shard_map/ppermute | solution.py:301
  190.3 59.6 %collective-permute-start.11 = (bf16[512,2048]{1,0:T(8,128)(2,1)}, bf16[512,2048]{1,0:T(8,128)(2,1)}, u32[]{:S(2)}, u32[]{:S(2)}) collective-permute-start(bf16[512,2048]{1,0:T(8,128)(2,1)} %refs_1_.6), channel_id=1, source_target_pairs={{0,1},{3,2},{4,5},{7,6},{8,9},{11,10},{12,13},{15,14},{16,17},{19,... | collective-permute-start | bytes 6291464 | tf_op jit(solution)/shard_map/ppermute | solution.py:301
  196.6 53.3 %collective-permute-start.12 = (bf16[512,2048]{1,0:T(8,128)(2,1)}, bf16[512,2048]{1,0:T(8,128)(2,1)}, u32[]{:S(2)}, u32[]{:S(2)}) collective-permute-start(bf16[512,2048]{1,0:T(8,128)(2,1)} %collective-permute-done.10.refs_7_), channel_id=1, source_target_pairs={{1,0},{2,3},{5,4},{6,7},{9,8},{10,11},{13,12},{14,15},{17,16},{18,... | collective-permute-start | bytes 6291464 | tf_op jit(solution)/shard_map/ppermute | solution.py:301
  197.9 8.4 %copy-start.7 = (s32[64,2]{0,1:T(2,128)S(1)}, s32[64,2]{0,1:T(2,128)}, u32[]{:S(2)}) copy-start(s32[64,2]{0,1:T(2,128)} %param.20) | copy-start | bytes 1540
  198.0 8.4 %copy-start.8 = (s32[64,2]{0,1:T(2,128)S(1)}, s32[64,2]{0,1:T(2,128)}, u32[]{:S(2)}) copy-start(s32[64,2]{0,1:T(2,128)} %param.21) | copy-start | bytes 1540
  198.0 17.9 %copy-start.3 = (bf16[512,1536]{1,0:T(8,128)(2,1)S(1)}, bf16[512,1536]{1,0:T(8,128)(2,1)}, u32[]{:S(2)}) copy-start(bf16[512,1536]{1,0:T(8,128)(2,1)} %q_ref.3) | copy-start | bytes 4718596
  204.7 1.7 copy-start
  230.8 62.9 %collective-permute-start.8 = (bf16[512,2048]{1,0:T(8,128)(2,1)}, bf16[512,2048]{1,0:T(8,128)(2,1)}, u32[]{:S(2)}, u32[]{:S(2)}) collective-permute-start(bf16[512,2048]{1,0:T(8,128)(2,1)} %project.4), channel_id=1, source_target_pairs={{0,1},{3,2},{4,5},{7,6},{8,9},{11,10},{12,13},{15,14},{16,17},{19,... | collective-permute-start | bytes 6291464 | tf_op jit(solution)/shard_map/ppermute | solution.py:301
  241.6 1.4 copy-start.1
  287.4 76.3 %all-to-all-start = ((bf16[8,128,3072]{2,1,0:T(8,128)(2,1)}), bf16[8,128,3072]{2,1,0:T(8,128)(2,1)}, u32[]{:S(2)}, u32[]{:S(2)}) async-start(bf16[8,128,3072]{2,1,0:T(8,128)(2,1)} %attend_grad.1), calls=%async_computation | async-start | bytes 12582912 | tf_op jit(solution)/shard_map/all_to_all | solution.py:442
  292.2 56.9 %copy-start.2 = (bf16[512,2048]{1,0:T(8,128)(2,1)S(1)}, bf16[512,2048]{1,0:T(8,128)(2,1)}, u32[]{:S(2)}) copy-start(bf16[512,2048]{1,0:T(8,128)(2,1)} %copy-done.1) | copy-start | bytes 6291460
  292.2 47.7 %collective-permute-start.14 = (bf16[512,2048]{1,0:T(8,128)(2,1)}, bf16[512,2048]{1,0:T(8,128)(2,1)S(1)}, u32[]{:S(2)}, u32[]{:S(2)}) collective-permute-start(bf16[512,2048]{1,0:T(8,128)(2,1)} %copy-done.1), channel_id=1, source_target_pairs={{0,1},{3,2},{4,5},{7,6},{8,9},{11,10},{12,13},{15,14},{16,17},{19,... | collective-permute-start | bytes 6291464 | tf_op jit(solution)/shard_map/ppermute | solution.py:301
  296.8 50.9 %collective-permute-start.13 = (bf16[512,2048]{1,0:T(8,128)(2,1)S(1)}, bf16[512,2048]{1,0:T(8,128)(2,1)S(1)}, u32[]{:S(2)}, u32[]{:S(2)}) collective-permute-start(bf16[512,2048]{1,0:T(8,128)(2,1)S(1)} %add.69), channel_id=1, source_target_pairs={{1,3},{2,0},{5,7},{6,4},{9,11},{10,8},{13,15},{14,12},{17,19},{18,... | collective-permute-start | bytes 6291464 | tf_op jit(solution)/shard_map/ppermute | solution.py:301
  298.1 94.6 %collective-permute-start.7 = (bf16[512,2048]{1,0:T(8,128)(2,1)}, bf16[512,2048]{1,0:T(8,128)(2,1)}, u32[]{:S(2)}, u32[]{:S(2)}) collective-permute-start(bf16[512,2048]{1,0:T(8,128)(2,1)} %project.6), channel_id=1, source_target_pairs={{0,1},{1,0},{2,3},{3,2},{4,5},{5,4},{6,7},{7,6},{8,9},{9,8},{10,11... | collective-permute-start | bytes 6291464 | tf_op jit(solution)/shard_map/ppermute | solution.py:301
  347.7 1.4 copy-start.4
  351.2 41.5 %collective-permute-start.15 = (bf16[512,2048]{1,0:T(8,128)(2,1)}, bf16[512,2048]{1,0:T(8,128)(2,1)}, u32[]{:S(2)}, u32[]{:S(2)}) collective-permute-start(bf16[512,2048]{1,0:T(8,128)(2,1)} %add.70), channel_id=1, source_target_pairs={{1,2},{2,1},{5,6},{6,5},{9,10},{10,9},{13,14},{14,13},{17,18},{18,... | collective-permute-start | bytes 6291464 | tf_op jit(solution)/shard_map/ppermute | solution.py:301
  363.8 28.9 %copy-start.5 = (bf16[512,2048]{1,0:T(8,128)(2,1)S(1)}, bf16[512,2048]{1,0:T(8,128)(2,1)}, u32[]{:S(2)}) copy-start(bf16[512,2048]{1,0:T(8,128)(2,1)} %copy-done.4) | copy-start | bytes 6291460
Sparse Core Ops, SparseCore 0:
  141.4 74.4 all-gather.1

commit v3 on v2

--- a/solution.py
+++ b/solution.py
@@ -288,7 +288,6 @@
     return lax.optimization_barrier((x, *others))[0]
 
 
-FAR, NEAR, BESIDE = (3, 3, 0, 0), (2, 2, 1, 1), (1, 0, 3, 2)
 INWARDS = [(0, 1), (3, 2)]
 OUTWARDS = [(1, 0), (2, 3)]
 SWAP = [(0, 1), (1, 0), (2, 3), (3, 2)]
@@ -301,30 +300,66 @@
     return lax.ppermute(x, "tensor", hops)
 
 
-def entry(table, me):
-    return jnp.take(jnp.array(table, jnp.int32), me)
+def far_of(me):
+    return jnp.where(me < 2, 3, 0)
+
+
+def near_of(me):
+    return jnp.where(me < 2, 2, 1)
+
+
+def beside_of(me):
+    return me ^ 1
+
+
+def sum_kernel(*refs):
+    total = refs[0][...].astype(jnp.float32)
+    for ref in refs[1:-1]:
+        total = total + ref[...].astype(jnp.float32)
+    refs[-1][...] = total.astype(jnp.bfloat16)
+
+
+def sum_of(arrays):
+    rows, width = arrays[0].shape
+    steps = 2 if rows % 32 == 0 else 1
+    block = pl.BlockSpec((rows // steps, width), lambda j: (j, 0))
+    return pl.pallas_call(
+        sum_kernel,
+        grid=(steps,),
+        in_specs=[block] * len(arrays),
+        out_specs=block,
+        out_shape=jax.ShapeDtypeStruct((rows, width), jnp.bfloat16),
+        compiler_params=pltpu.CompilerParams(vmem_limit_bytes=42 * MIB),
+        cost_estimate=SMALL,
+        name="sum_of",
+    )(*arrays)
 
 
 class LineSum:
     def __init__(self, term, me):
         self.term, self.me = term, me
-        self.far = term(entry(FAR, me), [])
+        self.far = term(far_of(me), [])
         self.far_in = send(self.far, INWARDS)
-        self.near = term(after(entry(NEAR, me), self.far), [])
+        self.near = term(after(near_of(me), self.far), [])
         self.near_in = send(self.near, INWARDS)
-        self.beside = term(after(entry(BESIDE, me), self.near), [])
+
+    def add_beside(self, *others):
+        self.beside = self.term(after(beside_of(self.me), self.near, *others), [])
         self.beside_in = send(self.beside, SWAP)
 
     def add_far(self, *others):
-        self.far_sum = self.far + after(self.far_in, *others)
+        self.far_sum = sum_of([self.far, after(self.far_in, *others)])
         self.far_in = send(self.far_sum, TWO_ON)
 
     def add_near(self, *others):
-        self.near_sum = self.near + after(self.near_in, *others)
+        self.near_sum = sum_of([self.near, after(self.near_in, *others)])
         self.near_in = send(self.near_sum, ACROSS)
 
-    def finish(self):
-        return self.term(self.me, [self.beside_in, self.far_in, self.near_in])
+    def received(self):
+        return [self.beside_in, self.far_in, self.near_in]
+
+    def finish(self, *others):
+        return self.term(after(self.me, *others), self.received())
 
 
 def settle_kernel(slot_ref, returned_ref, out_ref):
@@ -383,27 +418,24 @@
     serving_slot = lax.dynamic_index_in_dim(slot_from, reader, 1, False)
 
     def kv_term(shard, received):
-        total = lax.dynamic_slice_in_dim(
-            kv_part[0], shard * share_width, share_width, 1
-        ).astype(jnp.float32)
-        for r in received:
-            total = total + r.astype(jnp.float32)
-        return total.astype(jnp.bfloat16)
+        term = lax.dynamic_slice_in_dim(kv_part[0], shard * share_width, share_width, 1)
+        return sum_of([term, *received]) if received else term
 
     if count == 4:
         across = send(d_out, ACROSS)
         outwards = send(d_out, OUTWARDS)
         line = LineSum(kv_term, me)
+        line.add_beside()
         line.add_far(across, outwards)
         line.add_near(line.far_in)
         share = line.finish()
         two_in = send(after(d_out, line.near_sum), TWO_IN)
         inwards = send(after(d_out, two_in), INWARDS)
         groups = [
-            (entry(range(4), me), [d_out]),
-            (entry(NEAR, me), [across, send(after(across, line.near_sum), OUTWARDS)]),
-            (entry(BESIDE, me), [inwards, outwards]),
-            (entry(FAR, me), [two_in, send(two_in, OUTWARDS)]),
+            (me, [d_out]),
+            (near_of(me), [across, send(after(across, line.near_sum), OUTWARDS)]),
+            (beside_of(me), [inwards, outwards]),
+            (far_of(me), [two_in, send(two_in, OUTWARDS)]),
         ]
     else:
         share = lax.psum_scatter(kv_part[0], "tensor", scatter_dimension=1, tiled=True)
@@ -420,12 +452,13 @@
         grads = back_project(groups[:1], w_out, None, jnp.float32)
         attended = attend(after(ids, grads), queries, blocks, 0)
         line = LineSum(mixed_term, me)
-        first = (after(groups[1][0], line.beside), groups[1][1])
+        first = (after(groups[1][0], line.near), groups[1][1])
         grads = back_project([first] + groups[2:], w_out, grads, jnp.bfloat16)
         own_sums = attend_grad(ids, owners, dp_count, queries, grads, [blocks])
         line.add_far(own_sums)
-        line.add_near(line.far_in)
-        mixed = line.finish()
+        line.add_beside(line.far_sum)
+        mine = mixed_term(after(me, line.beside), [])
+        line.add_near(line.far_in, mine)
     else:
         attended = attend(ids, queries, blocks, 0)
         partial = jnp.concatenate(
@@ -440,7 +473,10 @@
             )
         own_sums = attend_grad(ids, owners, dp_count, queries, grads, [blocks])
     returned = lax.all_to_all(own_sums, "dp", split_axis=0, concat_axis=0, tiled=True)
-    return (mixed, settle(serving_slot, returned))
+    d_kv = settle(serving_slot, returned)
+    if count == 4:
+        mixed = sum_of([after(mine, d_kv), *line.received()])
+    return (mixed, d_kv)
 
 
 def solution(mesh):

time: 414 us -> 396 us (0.957)
  other arithmetic: 17.2 us -> 0.3 us
  Pallas kernels: 86.2 us -> 98.9 us
  waiting for transfers between devices: 214 us -> 208 us
    pallas_call x0 -> x6, Pallas kernels: none -> 13.6 us  [sum_of(): pl.pallas_call(sum_kernel, grid=(steps,), in_specs=[block] * len(arrays),...]
    add x4 -> x0, other arithmetic: 11.9 us -> none  [the longest x2 7.38 us: add_far(): self.far_sum = self.far + after(self.far_in, *others)]
    ppermute x16, waiting for transfers between devices: 195 us -> 187 us  [send(): return lax.ppermute(x, 'tensor', hops)]
    convert_element_type x1 -> x0, other arithmetic: 5 us -> none  [kv_term(): return total.astype(jnp.bfloat16)]
  transfers between devices with their start and end apart: 18 -> 18, of which waited for: 10 -> 11; matrix products, arithmetic and copies ran while one was open for 5% -> 2% of each run, Pallas kernels for 19% -> 24%
where the time goes in v3:
time: 396 us; the launch traced here: 392 us
  waiting for transfers between devices  208 us (53%)
  Pallas kernels  98.9 us (25%)
  starting transfers between devices  59.7 us (15%)
  between operations  14.3 us (4%)
  local copies, waits for them, and re-layouts  10.6 us (3%)
    ppermute x16, waiting for transfers between devices, send(): return lax.ppermute(x, 'tensor', hops)  187 us
    ppermute x16, starting transfers between devices, send(): return lax.ppermute(x, 'tensor', hops)  54.9 us
    pallas_call x4, Pallas kernels, project(): pl.pallas_call(functools.partial(project_kernel, parts, len(received)), g...  25.9 us
    pallas_call x2, Pallas kernels, back_project(): pl.pallas_call(functools.partial(back_project_kernel, [len(sources) for _...  25.2 us
    pallas_call x1, Pallas kernels, attend_grad(): pl.pallas_call(functools.partial(attend_grad_kernel, group, parts), grid_...  19.2 us
    pallas_call x6, Pallas kernels, sum_of(): pl.pallas_call(sum_kernel, grid=(steps,), in_specs=[block] * len(arrays),...  13.6 us
    all_to_all x1, waiting for transfers between devices, local(): lax.all_to_all(own_sums, 'dp', split_axis=0, concat_axis=0, tiled=True)  12 us
    all_gather x1, waiting for transfers between devices, local(): lax.all_gather(share.reshape(NB_DEV, NBR_LEN, share_width), 'dp', axis=0,...  9.12 us
  transfers between devices with their start and end apart: 18, of which 11 were waited for; matrix products, arithmetic and copies ran while one was open for 2% of the time, Pallas kernels for 24%

profile of v3, /device:TPU:0, one launch (start us, length us, event | category | flops | bytes accessed | tf_op | source)
XLA Modules:
  0.0 391.9 jit_solution(16692486095156213284)
XLA Ops:
  7.2 0.0 all-gather.2.cloned.1.call-start
  7.2 1.3 collective-permute-start.3
  8.5 2.0 collective-permute-start.2
  10.5 1.5 dynamic-slice_bitcast_fusion.2.refs_0_
  12.0 11.1 %collective-permute-start.1 = (bf16[256,3072]{1,0:T(8,128)(2,1)S(1)}, bf16[256,3072]{1,0:T(8,128)(2,1)}, u32[]{:S(2)}, u32[]{:S(2)}) collective-permute-start(bf16[256,3072]{1,0:T(8,128)(2,1)S(1)} %dynamic-slice_bitcast_fusion.2.refs_0_), channel_id=1, source_target_pairs={{0,1},{3,2},{4,5},{7,6},{8,9},{11,10},{12,13},{15,14},{16,17},{19,... | collective-permute-start | bytes 4718600 | tf_op jit(solution)/shard_map/ppermute | solution.py:300
  23.1 1.5 dynamic-slice_bitcast_fusion.1.refs_0_
  24.7 2.5 collective-permute-start.5
  27.1 29.7 %collective-permute-done.1.refs_1_ = bf16[256,3072]{1,0:T(8,128)(2,1)} collective-permute-done((bf16[256,3072]{1,0:T(8,128)(2,1)S(1)}, bf16[256,3072]{1,0:T(8,128)(2,1)}, u32[]{:S(2)}, u32[]{:S(2)}) %collective-permute-start.1) | collective-permute-done | bytes 1572896 | tf_op jit(solution)/shard_map/ppermute | solution.py:300
  56.8 0.6 collective-permute-done.3.refs_6_
  57.5 2.5 sum_of.6
  59.9 1.3 collective-permute-start.4
  61.2 2.1 dynamic-slice_bitcast_fusion
  63.3 6.9 %collective-permute-start = (bf16[256,3072]{1,0:T(8,128)(2,1)S(1)}, bf16[256,3072]{1,0:T(8,128)(2,1)S(1)}, u32[]{:S(2)}, u32[]{:S(2)}) collective-permute-start(bf16[256,3072]{1,0:T(8,128)(2,1)S(1)} %get-tuple-element.32), channel_id=1, source_target_pairs={{0,1},{1,0},{2,3},{3,2},{4,5},{5,4},{6,7},{7,6},{8,9},{9,8},{10,11... | collective-permute-start | bytes 4718600 | tf_op jit(solution)/shard_map/ppermute | solution.py:300
  70.2 20.3 %collective-permute-done.5.refs_1_ = bf16[256,3072]{1,0:T(8,128)(2,1)} collective-permute-done((bf16[256,3072]{1,0:T(8,128)(2,1)S(1)}, bf16[256,3072]{1,0:T(8,128)(2,1)}, u32[]{:S(2)}, u32[]{:S(2)}) %collective-permute-start.5) | collective-permute-done | bytes 1572896 | tf_op jit(solution)/shard_map/ppermute | solution.py:300
  90.5 12.1 %collective-permute-done.4.refs_2_ = bf16[256,3072]{1,0:T(8,128)(2,1)S(1)} collective-permute-done((bf16[256,3072]{1,0:T(8,128)(2,1)}, bf16[256,3072]{1,0:T(8,128)(2,1)S(1)}, u32[]{:S(2)}, u32[]{:S(2)}) %collective-permute-start.4) | collective-permute-done | bytes 1572896 | tf_op jit(solution)/shard_map/ppermute | solution.py:300
  102.6 1.6 sum_of.7
  104.2 0.8 collective-permute-start.6
  104.9 31.3 %collective-permute-done.refs_1_ = bf16[256,3072]{1,0:T(8,128)(2,1)S(1)} collective-permute-done((bf16[256,3072]{1,0:T(8,128)(2,1)S(1)}, bf16[256,3072]{1,0:T(8,128)(2,1)S(1)}, u32[]{:S(2)}, u32[]{:S(2)}) %collective-permute-start) | collective-permute-done | bytes 1572896 | tf_op jit(solution)/shard_map/ppermute | solution.py:300
  136.2 1.7 sum_of.8
  137.8 0.0 all-gather.2.cloned.1.call-update
  137.9 7.1 %collective-permute-start.9 = (bf16[512,2048]{1,0:T(8,128)(2,1)}, bf16[512,2048]{1,0:T(8,128)(2,1)}, u32[]{:S(2)}, u32[]{:S(2)}) collective-permute-start(bf16[512,2048]{1,0:T(8,128)(2,1)} %refs_1_.6), channel_id=1, source_target_pairs={{3,1},{0,2},{7,5},{4,6},{11,9},{8,10},{15,13},{12,14},{19,17},{16,... | collective-permute-start | bytes 6291464 | tf_op jit(solution)/shard_map/ppermute | solution.py:300
  145.0 1.3 collective-permute-start.8
  146.3 39.7 %collective-permute-done.9.refs_7_ = bf16[512,2048]{1,0:T(8,128)(2,1)} collective-permute-done((bf16[512,2048]{1,0:T(8,128)(2,1)}, bf16[512,2048]{1,0:T(8,128)(2,1)}, u32[]{:S(2)}, u32[]{:S(2)}) %collective-permute-start.9) | collective-permute-done | bytes 2097184 | tf_op jit(solution)/shard_map/ppermute | solution.py:300
  186.0 6.4 %collective-permute-start.10 = (bf16[512,2048]{1,0:T(8,128)(2,1)}, bf16[512,2048]{1,0:T(8,128)(2,1)}, u32[]{:S(2)}, u32[]{:S(2)}) collective-permute-start(bf16[512,2048]{1,0:T(8,128)(2,1)} %refs_1_.6), channel_id=1, source_target_pairs={{0,1},{3,2},{4,5},{7,6},{8,9},{11,10},{12,13},{15,14},{16,17},{19,... | collective-permute-start | bytes 6291464 | tf_op jit(solution)/shard_map/ppermute | solution.py:300
  192.3 1.3 collective-permute-start.11
  193.7 6.7 %back_project.2.refs_9_ = f32[512,1536]{1,0:T(8,128)S(1)} custom-call(s32[1]{0:T(128)} %bitcast.1.shards_ref, bf16[1536,8192]{1,0:T(8,128)(2,1)} %refs_1_.11, bf16[512,2048]{1,0:T(8,128)(2,1)} %refs_1_.6), custom_call_target="tpu_custom_call" | custom-call | flops 1 | bytes 1 | tf_op jit(solution)/shard_map/back_project/pallas_call | solution.py:267
  200.4 1.6 copy-done
  202.0 0.1 constant_dynamic-slice_fusion
  202.1 0.1 copy.25
  202.2 0.1 reshape.37
  202.3 0.1 copy.24
  202.3 0.1 reshape.36.own_ref
  202.4 9.1 %all-gather.2.cloned.1.call-done.refs_0_.refs_1_.refs_2_.refs_3_ = bf16[16,128,3072]{2,1,0:T(8,128)(2,1)} async-done(((bf16[2,128,3072]{2,1,0:T(8,128)(2,1)}), bf16[16,128,3072]{2,1,0:T(8,128)(2,1)}) %all-gather.2.cloned.1.call-update) | async-done | bytes 12582928 | tf_op jit(solution)/shard_map/all_gather | solution.py:444
  211.6 8.5 %attend.1.refs_0_ = bf16[512,1536]{1,0:T(8,128)(2,1)S(1)} custom-call(s32[16]{0:T(128)S(1)} %multiply_add_fusion.ids_ref, bf16[512,1536]{1,0:T(8,128)(2,1)S(1)} %copy-done.5, bf16[16,128,3072]{2,1,0:T(8,128)(2,1)} %all-gather.2.cloned.1.call-done.refs_0_.refs_1_.refs_2_.refs_3_, ...), custom_call_target="tpu_custom_call" | custom-call | flops 1 | bytes 1 | tf_op jit(solution)/shard_map/attend/pallas_call | solution.py:82
  220.0 6.9 %project.4.refs_0_ = bf16[512,2048]{1,0:T(8,128)(2,1)} custom-call(s32[1]{0:T(128)} %bitcast.shard_ref, bf16[512,1536]{1,0:T(8,128)(2,1)S(1)} %attend.1.refs_0_, bf16[1536,8192]{1,0:T(8,128)(2,1)} %refs_1_.11), custom_call_target="tpu_custom_call" | custom-call | flops 1 | bytes 1 | tf_op jit(solution)/shard_map/project/pallas_call | solution.py:225
  226.9 4.7 %collective-permute-start.7 = (bf16[512,2048]{1,0:T(8,128)(2,1)}, bf16[512,2048]{1,0:T(8,128)(2,1)}, u32[]{:S(2)}, u32[]{:S(2)}) collective-permute-start(bf16[512,2048]{1,0:T(8,128)(2,1)} %project.4.refs_0_), channel_id=1, source_target_pairs={{0,1},{3,2},{4,5},{7,6},{8,9},{11,10},{12,13},{15,14},{16,17},{19,... | collective-permute-start | bytes 6291464 | tf_op jit(solution)/shard_map/ppermute | solution.py:300
  231.7 6.0 %project.5.refs_0_ = bf16[512,2048]{1,0:T(8,128)(2,1)S(1)} custom-call(s32[1]{0:T(128)} %bitcast.7.shard_ref, bf16[512,1536]{1,0:T(8,128)(2,1)S(1)} %attend.1.refs_0_, bf16[1536,8192]{1,0:T(8,128)(2,1)} %refs_1_.11), custom_call_target="tpu_custom_call" | custom-call | flops 1 | bytes 1 | tf_op jit(solution)/shard_map/project/pallas_call | solution.py:225
  237.6 1.4 copy-done.1
  239.0 0.1 pad_add_fusion.shards_ref
  239.1 18.5 %back_project.3.g_ref = bf16[512,1536]{1,0:T(8,128)(2,1)S(1)} custom-call(s32[3]{0:T(128)S(1)} %pad_add_fusion.shards_ref, bf16[1536,8192]{1,0:T(8,128)(2,1)} %refs_1_.11, bf16[1536,8192]{1,0:T(8,128)(2,1)} %refs_1_.11, bf16[1536,8192]{1,0:T(8,128)(2,1)} %refs_1_.11, bf16[512,2048]{1,0:T(8,128)(2,1)} %collective-permute-done.2.refs_3_, ...), custom_call_target="tpu_custom_call" | custom-call | flops 1 | bytes 1 | tf_op jit(solution)/shard_map/back_project/pallas_call | solution.py:267
  257.6 19.2 %attend_grad.1 = bf16[8,128,3072]{2,1,0:T(8,128)(2,1)} custom-call(s32[16]{0:T(128)S(1)} %multiply_add_fusion.ids_ref, s32[16]{0:T(128)S(1)} %reshape.36.own_ref, bf16[512,1536]{1,0:T(8,128)(2,1)S(1)} %copy-done.5, bf16[512,1536]{1,0:T(8,128)(2,1)S(1)} %back_project.3.g_ref, ...), custom_call_target="tpu_custom_call" | custom-call | flops 1 | bytes 1 | tf_op jit(solution)/shard_map/attend_grad/pallas_call | solution.py:182
  276.8 4.7 %all-to-all-start = ((bf16[8,128,3072]{2,1,0:T(8,128)(2,1)}), bf16[8,128,3072]{2,1,0:T(8,128)(2,1)}, u32[]{:S(2)}, u32[]{:S(2)}) async-start(bf16[8,128,3072]{2,1,0:T(8,128)(2,1)} %attend_grad.1), calls=%async_computation | async-start | bytes 12582912 | tf_op jit(solution)/shard_map/all_to_all | solution.py:475
  281.6 1.4 collective-permute-start.14
  283.0 2.4 sum_of.9
  285.5 1.3 collective-permute-start.13
  286.8 7.0 %project.6 = bf16[512,2048]{1,0:T(8,128)(2,1)} custom-call(s32[1]{0:T(128)} %bitcast.10.shard_ref, bf16[512,1536]{1,0:T(8,128)(2,1)S(1)} %attend.1.refs_0_, bf16[1536,8192]{1,0:T(8,128)(2,1)} %refs_1_.11), custom_call_target="tpu_custom_call" | custom-call | flops 1 | bytes 1 | tf_op jit(solution)/shard_map/project/pallas_call | solution.py:225
  293.7 3.7 collective-permute-start.12
  297.4 6.1 %project.7.refs_0_ = bf16[512,2048]{1,0:T(8,128)(2,1)S(1)} custom-call(s32[1]{0:T(128)} %bitcast.11.shard_ref, bf16[512,1536]{1,0:T(8,128)(2,1)S(1)} %attend.1.refs_0_, bf16[1536,8192]{1,0:T(8,128)(2,1)} %refs_1_.11), custom_call_target="tpu_custom_call" | custom-call | flops 1 | bytes 1 | tf_op jit(solution)/shard_map/project/pallas_call | solution.py:225
  303.6 1.3 copy-done.3
  304.9 24.3 %collective-permute-done.14.refs_1_ = bf16[512,2048]{1,0:T(8,128)(2,1)S(1)} collective-permute-done((bf16[512,2048]{1,0:T(8,128)(2,1)}, bf16[512,2048]{1,0:T(8,128)(2,1)S(1)}, u32[]{:S(2)}, u32[]{:S(2)}) %collective-permute-start.14) | collective-permute-done | bytes 2097184 | tf_op jit(solution)/shard_map/ppermute | solution.py:300
  329.2 7.3 %collective-permute-done.13.refs_2_ = bf16[512,2048]{1,0:T(8,128)(2,1)S(1)} collective-permute-done((bf16[512,2048]{1,0:T(8,128)(2,1)S(1)}, bf16[512,2048]{1,0:T(8,128)(2,1)S(1)}, u32[]{:S(2)}, u32[]{:S(2)}) %collective-permute-start.13) | collective-permute-done | bytes 2097184 | tf_op jit(solution)/shard_map/ppermute | solution.py:300
  336.5 1.9 sum_of.10
  338.3 0.2 copy-done.6
  338.5 2.0 collective-permute-start.15
  340.5 0.1 copy.26
  340.6 0.1 copy.27
  340.7 0.1 eq.16
  340.7 0.1 broadcast_in_dim.16
  340.8 0.2 select_reduce_fusion
  341.0 0.2 dynamic-slice_reduce_fusion.slot_ref
  341.2 12.0 %all-to-all-done.returned_ref = bf16[8,128,3072]{2,1,0:T(8,128)(2,1)} async-done(((bf16[8,128,3072]{2,1,0:T(8,128)(2,1)}), bf16[8,128,3072]{2,1,0:T(8,128)(2,1)}, u32[]{:S(2)}, u32[]{:S(2)}) %all-to-all-start) | async-done | bytes 6291488 | tf_op jit(solution)/shard_map/all_to_all | solution.py:475
  353.2 6.4 %settle.1 = bf16[256,3072]{1,0:T(8,128)(2,1)} custom-call(s32[8]{0:T(128)S(1)} %dynamic-slice_reduce_fusion.slot_ref, bf16[8,128,3072]{2,1,0:T(8,128)(2,1)} %all-to-all-done.returned_ref), custom_call_target="tpu_custom_call" | custom-call | flops 1 | bytes 1 | tf_op jit(solution)/shard_map/settle/pallas_call | solution.py:378
  359.6 21.8 %collective-permute-done.12.refs_1_ = bf16[512,2048]{1,0:T(8,128)(2,1)} collective-permute-done((bf16[512,2048]{1,0:T(8,128)(2,1)}, bf16[512,2048]{1,0:T(8,128)(2,1)}, u32[]{:S(2)}, u32[]{:S(2)}) %collective-permute-start.12) | collective-permute-done | bytes 2097184 | tf_op jit(solution)/shard_map/ppermute | solution.py:300
  381.4 3.7 sum_of.11
  (24 shorter events, 0.1 us)
Async XLA Ops:
  7.2 204.4 %all-gather.2.cloned.1.call-start = ((), (), s32[]{:S(2)}) async-start(), calls=%async_computation.1 | async-start | bytes 14155776 | tf_op jit(solution)/shard_map/all_gather | solution.py:444
  7.2 50.2 %collective-permute-start.3 = (bf16[512,2048]{1,0:T(8,128)(2,1)}, bf16[512,2048]{1,0:T(8,128)(2,1)}, u32[]{:S(2)}, u32[]{:S(2)}) collective-permute-start(bf16[512,2048]{1,0:T(8,128)(2,1)} %refs_1_.6), channel_id=1, source_target_pairs={{1,0},{2,3},{5,4},{6,7},{9,8},{10,11},{13,12},{14,15},{17,16},{18,... | collective-permute-start | bytes 6291464 | tf_op jit(solution)/shard_map/ppermute | solution.py:300
  8.5 48.9 %collective-permute-start.2 = (bf16[512,2048]{1,0:T(8,128)(2,1)}, bf16[512,2048]{1,0:T(8,128)(2,1)}, u32[]{:S(2)}, u32[]{:S(2)}) collective-permute-start(bf16[512,2048]{1,0:T(8,128)(2,1)} %refs_1_.6), channel_id=1, source_target_pairs={{1,2},{2,1},{5,6},{6,5},{9,10},{10,9},{13,14},{14,13},{17,18},{18,... | collective-permute-start | bytes 6291464 | tf_op jit(solution)/shard_map/ppermute | solution.py:300
  12.0 44.8 %collective-permute-start.1 = (bf16[256,3072]{1,0:T(8,128)(2,1)S(1)}, bf16[256,3072]{1,0:T(8,128)(2,1)}, u32[]{:S(2)}, u32[]{:S(2)}) collective-permute-start(bf16[256,3072]{1,0:T(8,128)(2,1)S(1)} %dynamic-slice_bitcast_fusion.2.refs_0_), channel_id=1, source_target_pairs={{0,1},{3,2},{4,5},{7,6},{8,9},{11,10},{12,13},{15,14},{16,17},{19,... | collective-permute-start | bytes 4718600 | tf_op jit(solution)/shard_map/ppermute | solution.py:300
  24.7 65.8 %collective-permute-start.5 = (bf16[256,3072]{1,0:T(8,128)(2,1)S(1)}, bf16[256,3072]{1,0:T(8,128)(2,1)}, u32[]{:S(2)}, u32[]{:S(2)}) collective-permute-start(bf16[256,3072]{1,0:T(8,128)(2,1)S(1)} %dynamic-slice_bitcast_fusion.1.refs_0_), channel_id=1, source_target_pairs={{0,1},{3,2},{4,5},{7,6},{8,9},{11,10},{12,13},{15,14},{16,17},{19,... | collective-permute-start | bytes 4718600 | tf_op jit(solution)/shard_map/ppermute | solution.py:300
  59.9 42.7 %collective-permute-start.4 = (bf16[256,3072]{1,0:T(8,128)(2,1)}, bf16[256,3072]{1,0:T(8,128)(2,1)S(1)}, u32[]{:S(2)}, u32[]{:S(2)}) collective-permute-start(bf16[256,3072]{1,0:T(8,128)(2,1)} %sum_of.6), channel_id=1, source_target_pairs={{1,3},{2,0},{5,7},{6,4},{9,11},{10,8},{13,15},{14,12},{17,19},{18,... | collective-permute-start | bytes 4718600 | tf_op jit(solution)/shard_map/ppermute | solution.py:300
  63.3 72.9 %collective-permute-start = (bf16[256,3072]{1,0:T(8,128)(2,1)S(1)}, bf16[256,3072]{1,0:T(8,128)(2,1)S(1)}, u32[]{:S(2)}, u32[]{:S(2)}) collective-permute-start(bf16[256,3072]{1,0:T(8,128)(2,1)S(1)} %get-tuple-element.32), channel_id=1, source_target_pairs={{0,1},{1,0},{2,3},{3,2},{4,5},{5,4},{6,7},{7,6},{8,9},{9,8},{10,11... | collective-permute-start | bytes 4718600 | tf_op jit(solution)/shard_map/ppermute | solution.py:300
  104.2 32.0 %collective-permute-start.6 = (bf16[256,3072]{1,0:T(8,128)(2,1)S(1)}, bf16[256,3072]{1,0:T(8,128)(2,1)S(1)}, u32[]{:S(2)}, u32[]{:S(2)}) collective-permute-start(bf16[256,3072]{1,0:T(8,128)(2,1)S(1)} %sum_of.7), channel_id=1, source_target_pairs={{1,2},{2,1},{5,6},{6,5},{9,10},{10,9},{13,14},{14,13},{17,18},{18,... | collective-permute-start | bytes 4718600 | tf_op jit(solution)/shard_map/ppermute | solution.py:300
  137.9 48.1 %collective-permute-start.9 = (bf16[512,2048]{1,0:T(8,128)(2,1)}, bf16[512,2048]{1,0:T(8,128)(2,1)}, u32[]{:S(2)}, u32[]{:S(2)}) collective-permute-start(bf16[512,2048]{1,0:T(8,128)(2,1)} %refs_1_.6), channel_id=1, source_target_pairs={{3,1},{0,2},{7,5},{4,6},{11,9},{8,10},{15,13},{12,14},{19,17},{16,... | collective-permute-start | bytes 6291464 | tf_op jit(solution)/shard_map/ppermute | solution.py:300
  145.0 94.1 %collective-permute-start.8 = (bf16[512,2048]{1,0:T(8,128)(2,1)}, bf16[512,2048]{1,0:T(8,128)(2,1)}, u32[]{:S(2)}, u32[]{:S(2)}) collective-permute-start(bf16[512,2048]{1,0:T(8,128)(2,1)} %collective-permute-done.2.refs_3_), channel_id=1, source_target_pairs={{1,0},{2,3},{5,4},{6,7},{9,8},{10,11},{13,12},{14,15},{17,16},{18,... | collective-permute-start | bytes 6291464 | tf_op jit(solution)/shard_map/ppermute | solution.py:300
  186.0 53.1 %collective-permute-start.10 = (bf16[512,2048]{1,0:T(8,128)(2,1)}, bf16[512,2048]{1,0:T(8,128)(2,1)}, u32[]{:S(2)}, u32[]{:S(2)}) collective-permute-start(bf16[512,2048]{1,0:T(8,128)(2,1)} %refs_1_.6), channel_id=1, source_target_pairs={{0,1},{3,2},{4,5},{7,6},{8,9},{11,10},{12,13},{15,14},{16,17},{19,... | collective-permute-start | bytes 6291464 | tf_op jit(solution)/shard_map/ppermute | solution.py:300
  192.3 46.7 %collective-permute-start.11 = (bf16[512,2048]{1,0:T(8,128)(2,1)}, bf16[512,2048]{1,0:T(8,128)(2,1)}, u32[]{:S(2)}, u32[]{:S(2)}) collective-permute-start(bf16[512,2048]{1,0:T(8,128)(2,1)} %collective-permute-done.9.refs_7_), channel_id=1, source_target_pairs={{1,0},{2,3},{5,4},{6,7},{9,8},{10,11},{13,12},{14,15},{17,16},{18,... | collective-permute-start | bytes 6291464 | tf_op jit(solution)/shard_map/ppermute | solution.py:300
  193.6 8.4 %copy-start.8 = (s32[64,2]{0,1:T(2,128)S(1)}, s32[64,2]{0,1:T(2,128)}, u32[]{:S(2)}) copy-start(s32[64,2]{0,1:T(2,128)} %param.10) | copy-start | bytes 1540
  193.6 8.4 %copy-start.9 = (s32[64,2]{0,1:T(2,128)S(1)}, s32[64,2]{0,1:T(2,128)}, u32[]{:S(2)}) copy-start(s32[64,2]{0,1:T(2,128)} %param.11) | copy-start | bytes 1540
  193.7 17.9 %copy-start.5 = (bf16[512,1536]{1,0:T(8,128)(2,1)S(1)}, bf16[512,1536]{1,0:T(8,128)(2,1)}, u32[]{:S(2)}) copy-start(bf16[512,1536]{1,0:T(8,128)(2,1)} %q_ref.3) | copy-start | bytes 4718596
  200.4 1.7 copy-start
  226.9 56.1 %collective-permute-start.7 = (bf16[512,2048]{1,0:T(8,128)(2,1)}, bf16[512,2048]{1,0:T(8,128)(2,1)}, u32[]{:S(2)}, u32[]{:S(2)}) collective-permute-start(bf16[512,2048]{1,0:T(8,128)(2,1)} %project.4.refs_0_), channel_id=1, source_target_pairs={{0,1},{3,2},{4,5},{7,6},{8,9},{11,10},{12,13},{15,14},{16,17},{19,... | collective-permute-start | bytes 6291464 | tf_op jit(solution)/shard_map/ppermute | solution.py:300
  237.6 1.4 copy-start.1
  276.8 76.3 %all-to-all-start = ((bf16[8,128,3072]{2,1,0:T(8,128)(2,1)}), bf16[8,128,3072]{2,1,0:T(8,128)(2,1)}, u32[]{:S(2)}, u32[]{:S(2)}) async-start(bf16[8,128,3072]{2,1,0:T(8,128)(2,1)} %attend_grad.1), calls=%async_computation | async-start | bytes 12582912 | tf_op jit(solution)/shard_map/all_to_all | solution.py:475
  281.6 47.6 %collective-permute-start.14 = (bf16[512,2048]{1,0:T(8,128)(2,1)}, bf16[512,2048]{1,0:T(8,128)(2,1)S(1)}, u32[]{:S(2)}, u32[]{:S(2)}) collective-permute-start(bf16[512,2048]{1,0:T(8,128)(2,1)} %copy-done.1), channel_id=1, source_target_pairs={{0,1},{3,2},{4,5},{7,6},{8,9},{11,10},{12,13},{15,14},{16,17},{19,... | collective-permute-start | bytes 6291464 | tf_op jit(solution)/shard_map/ppermute | solution.py:300
  285.5 51.0 %collective-permute-start.13 = (bf16[512,2048]{1,0:T(8,128)(2,1)S(1)}, bf16[512,2048]{1,0:T(8,128)(2,1)S(1)}, u32[]{:S(2)}, u32[]{:S(2)}) collective-permute-start(bf16[512,2048]{1,0:T(8,128)(2,1)S(1)} %sum_of.9), channel_id=1, source_target_pairs={{1,3},{2,0},{5,7},{6,4},{9,11},{10,8},{13,15},{14,12},{17,19},{18,... | collective-permute-start | bytes 6291464 | tf_op jit(solution)/shard_map/ppermute | solution.py:300
  293.7 87.7 %collective-permute-start.12 = (bf16[512,2048]{1,0:T(8,128)(2,1)}, bf16[512,2048]{1,0:T(8,128)(2,1)}, u32[]{:S(2)}, u32[]{:S(2)}) collective-permute-start(bf16[512,2048]{1,0:T(8,128)(2,1)} %project.6), channel_id=1, source_target_pairs={{0,1},{1,0},{2,3},{3,2},{4,5},{5,4},{6,7},{7,6},{8,9},{9,8},{10,11... | collective-permute-start | bytes 6291464 | tf_op jit(solution)/shard_map/ppermute | solution.py:300
  297.4 39.0 %copy-start.2 = (bf16[512,2048]{1,0:T(8,128)(2,1)S(1)}, bf16[512,2048]{1,0:T(8,128)(2,1)}, u32[]{:S(2)}) copy-start(bf16[512,2048]{1,0:T(8,128)(2,1)} %copy-done.1) | copy-start | bytes 6291460
  303.6 1.3 copy-start.3
  336.5 2.0 copy-start.6
  338.5 42.9 %collective-permute-start.15 = (bf16[512,2048]{1,0:T(8,128)(2,1)}, bf16[512,2048]{1,0:T(8,128)(2,1)}, u32[]{:S(2)}, u32[]{:S(2)}) collective-permute-start(bf16[512,2048]{1,0:T(8,128)(2,1)} %sum_of.10), channel_id=1, source_target_pairs={{1,2},{2,1},{5,6},{6,5},{9,10},{10,9},{13,14},{14,13},{17,18},{18,... | collective-permute-start | bytes 6291464 | tf_op jit(solution)/shard_map/ppermute | solution.py:300
  341.2 40.2 %copy-start.4 = (bf16[512,2048]{1,0:T(8,128)(2,1)S(1)}, bf16[512,2048]{1,0:T(8,128)(2,1)}, u32[]{:S(2)}) copy-start(bf16[512,2048]{1,0:T(8,128)(2,1)} %copy-done.3) | copy-start | bytes 6291460
  353.2 28.2 %copy-start.7 = (bf16[512,2048]{1,0:T(8,128)(2,1)S(1)}, bf16[512,2048]{1,0:T(8,128)(2,1)}, u32[]{:S(2)}) copy-start(bf16[512,2048]{1,0:T(8,128)(2,1)} %copy-done.6) | copy-start | bytes 6291460
Sparse Core Ops, SparseCore 0:
  138.0 73.5 all-gather.1

commit v4 on v3

--- a/solution.py
+++ b/solution.py
@@ -64,10 +64,10 @@
         out_ref[r, h * HD : (h + 1) * HD] = out.astype(jnp.bfloat16)
 
 
-def neighbour_specs(group, share):
+def neighbour_specs(group, share, part):
     def spec(place):
         return pl.BlockSpec(
-            (1, NBR_LEN, share), lambda c, ids, *_: (ids[2 * group * c + place], 0, 0)
+            (1, NBR_LEN, share), lambda c, ids, *_: (ids[2 * group * c + place], 0, part)
         )
 
     return [spec(place) for place in range(2 * group)]
@@ -85,7 +85,7 @@
             num_scalar_prefetch=1,
             grid=(spans // group,),
             in_specs=[pl.BlockSpec((group * SPAN, width), lambda c, ids: (c, part))]
-            + neighbour_specs(group, share),
+            + neighbour_specs(group, share, 0),
             out_specs=pl.BlockSpec((group * SPAN, width), lambda c, ids: (c, 0)),
         ),
         out_shape=jax.ShapeDtypeStruct((tokens, width), jnp.bfloat16),
@@ -95,7 +95,7 @@
     )(ids, queries, *([blocks] * (2 * group)))
 
 
-def attend_grad_kernel(group, parts, ids_ref, own_ref, q_ref, g_ref, *refs):
+def attend_grad_kernel(group, ids_ref, own_ref, q_ref, g_ref, *refs):
     del ids_ref
     out_ref, total_ref = refs[-2:]
     step = pl.program_id(0)
@@ -106,59 +106,57 @@
 
     factor = HD**-0.5
     heads = q_ref.shape[1] // HD
-    part_heads = heads // parts
     for c in range(group):
         tokens = slice(c * SPAN, (c + 1) * SPAN)
         places = (
             (own_ref[2 * (group * step + c)], slice(0, NBR_LEN)),
             (own_ref[2 * (group * step + c) + 1], slice(NBR_LEN, 2 * NBR_LEN)),
         )
-        for part in range(parts):
-            first_ref, second_ref = refs[2 * (group * part + c) : 2 * (group * part + c) + 2]
-            pairs = range(0, part_heads, 2)
-            query = [block_diagonal(q_ref, tokens, part * part_heads + h) for h in pairs]
-            grad = [block_diagonal(g_ref, tokens, part * part_heads + h) for h in pairs]
-            scores = [
-                lax.dot_general(
-                    two_heads_of(first_ref, second_ref, h, 0),
-                    x,
-                    NT,
-                    preferred_element_type=jnp.float32,
-                )
-                for h, x in zip(pairs, query)
-            ]
-            grad_probs = [
-                lax.dot_general(
-                    two_heads_of(first_ref, second_ref, h, HD),
-                    x,
-                    NT,
-                    preferred_element_type=jnp.float32,
-                )
-                for h, x in zip(pairs, grad)
-            ]
-            highest = [jnp.max(s, axis=0, keepdims=True) for s in scores]
-            expo = [jnp.exp((s - m) * factor) for s, m in zip(scores, highest)]
-            inverse = [1.0 / jnp.sum(e, axis=0, keepdims=True) for e in expo]
-            probs = [e * r for e, r in zip(expo, inverse)]
-            inner = [jnp.sum(p * d, axis=0, keepdims=True) for p, d in zip(probs, grad_probs)]
-            grad_scores = [
-                (p * (d - i)).astype(jnp.bfloat16) for p, d, i in zip(probs, grad_probs, inner)
-            ]
-            grad_keys = [
-                jnp.dot(d, x, preferred_element_type=jnp.float32)
-                for d, x in zip(grad_scores, query)
-            ]
-            grad_values = [
-                jnp.dot(p.astype(jnp.bfloat16), x, preferred_element_type=jnp.float32)
-                for p, x in zip(probs, grad)
-            ]
-            for h, keys, values in zip(pairs, grad_keys, grad_values):
-                for i in range(2):
-                    at = 2 * (part * part_heads + h + i) * HD
-                    lanes = slice(i * HD, (i + 1) * HD)
-                    for owner, rows in places:
-                        total_ref[owner, :, at : at + HD] += keys[rows, lanes]
-                        total_ref[owner, :, at + HD : at + 2 * HD] += values[rows, lanes]
+        first_ref, second_ref = refs[2 * c : 2 * c + 2]
+        pairs = range(0, heads, 2)
+        query = [block_diagonal(q_ref, tokens, h) for h in pairs]
+        grad = [block_diagonal(g_ref, tokens, h) for h in pairs]
+        scores = [
+            lax.dot_general(
+                two_heads_of(first_ref, second_ref, h, 0),
+                x,
+                NT,
+                preferred_element_type=jnp.float32,
+            )
+            for h, x in zip(pairs, query)
+        ]
+        grad_probs = [
+            lax.dot_general(
+                two_heads_of(first_ref, second_ref, h, HD),
+                x,
+                NT,
+                preferred_element_type=jnp.float32,
+            )
+            for h, x in zip(pairs, grad)
+        ]
+        highest = [jnp.max(s, axis=0, keepdims=True) for s in scores]
+        expo = [jnp.exp((s - m) * factor) for s, m in zip(scores, highest)]
+        inverse = [1.0 / jnp.sum(e, axis=0, keepdims=True) for e in expo]
+        probs = [e * r for e, r in zip(expo, inverse)]
+        inner = [jnp.sum(p * d, axis=0, keepdims=True) for p, d in zip(probs, grad_probs)]
+        grad_scores = [
+            (p * (d - i)).astype(jnp.bfloat16) for p, d, i in zip(probs, grad_probs, inner)
+        ]
+        grad_keys = [
+            jnp.dot(d, x, preferred_element_type=jnp.float32)
+            for d, x in zip(grad_scores, query)
+        ]
+        grad_values = [
+            jnp.dot(p.astype(jnp.bfloat16), x, preferred_element_type=jnp.float32)
+            for p, x in zip(probs, grad)
+        ]
+        for h, keys, values in zip(pairs, grad_keys, grad_values):
+            for i in range(2):
+                at = 2 * (h + i) * HD
+                lanes = slice(i * HD, (i + 1) * HD)
+                for owner, rows in places:
+                    total_ref[owner, :, at : at + HD] += keys[rows, lanes]
+                    total_ref[owner, :, at + HD : at + 2 * HD] += values[rows, lanes]
 
     @pl.when(step == pl.num_programs(0) - 1)
     def _():
@@ -172,30 +170,28 @@
             ].astype(jnp.bfloat16)
 
 
-def attend_grad(ids, owners, owner_count, queries, grads, blocks):
-    tokens, width = queries.shape
+def attend_grad(ids, owners, owner_count, queries, grads, blocks, part, parts):
+    tokens = queries.shape[0]
     spans = tokens // SPAN
-    parts = len(blocks)
-    part_share = blocks[0].shape[2]
-    share = parts * part_share
+    width, share = queries.shape[1] // parts, blocks.shape[2] // parts
     group = 2 if spans % 2 == 0 else 1
     return pl.pallas_call(
-        functools.partial(attend_grad_kernel, group, parts),
+        functools.partial(attend_grad_kernel, group),
         grid_spec=pltpu.PrefetchScalarGridSpec(
             num_scalar_prefetch=2,
             grid=(spans // group,),
-            in_specs=[pl.BlockSpec((group * SPAN, width), lambda c, ids, own: (c, 0))] * 2
-            + neighbour_specs(group, part_share) * parts,
+            in_specs=[pl.BlockSpec((group * SPAN, width), lambda c, ids, own: (c, part))] * 2
+            + neighbour_specs(group, share, part),
             out_specs=pl.BlockSpec(
                 (owner_count, NBR_LEN, share), lambda c, ids, own: (0, 0, 0)
             ),
             scratch_shapes=[pltpu.VMEM((owner_count, NBR_LEN, share), jnp.float32)],
         ),
         out_shape=jax.ShapeDtypeStruct((owner_count, NBR_LEN, share), jnp.bfloat16),
-        compiler_params=pltpu.CompilerParams(vmem_limit_bytes=50 * MIB),
+        compiler_params=pltpu.CompilerParams(vmem_limit_bytes=48 * MIB),
         cost_estimate=SMALL,
         name="attend_grad",
-    )(ids, owners, queries, grads, *[b for b in blocks for _ in range(2 * group)])
+    )(ids, owners, queries, grads, *([blocks] * (2 * group)))
 
 
 def tile_of(width):
@@ -345,7 +341,9 @@
 
     def add_beside(self, *others):
         self.beside = self.term(after(beside_of(self.me), self.near, *others), [])
-        self.beside_in = send(self.beside, SWAP)
+
+    def swap_beside(self, *others):
+        self.beside_in = send(after(self.beside, *others), SWAP)
 
     def add_far(self, *others):
         self.far_sum = sum_of([self.far, after(self.far_in, *others)])
@@ -362,32 +360,45 @@
         return self.term(after(self.me, *others), self.received())
 
 
-def settle_kernel(slot_ref, returned_ref, out_ref):
-    totals = [jnp.zeros(returned_ref.shape[1:], jnp.float32) for _ in range(NB_DEV)]
-    for r in range(returned_ref.shape[0]):
-        block = returned_ref[r].astype(jnp.float32)
-        for slot in range(NB_DEV):
-            totals[slot] = totals[slot] + jnp.where(slot_ref[r] == slot, block, 0.0)
-    for slot in range(NB_DEV):
-        out_ref[slot * NBR_LEN : (slot + 1) * NBR_LEN] = totals[slot].astype(jnp.bfloat16)
+def settle_kernel(steps, slot_ref, *refs):
+    for part, returned_ref in enumerate(refs[:-1]):
+
+        @pl.when(pl.program_id(0) // steps == part)
+        def _(returned_ref=returned_ref):
+            totals = [jnp.zeros(returned_ref.shape[1:], jnp.float32) for _ in range(NB_DEV)]
+            for r in range(returned_ref.shape[0]):
+                block = returned_ref[r].astype(jnp.float32)
+                for slot in range(NB_DEV):
+                    totals[slot] = totals[slot] + jnp.where(slot_ref[r] == slot, block, 0.0)
+            for slot in range(NB_DEV):
+                rows = slice(slot * NBR_LEN, (slot + 1) * NBR_LEN)
+                refs[-1][rows] = totals[slot].astype(jnp.bfloat16)
 
 
 def settle(slots, returned):
-    readers, _, width = returned.shape
-    tile = next(tile for tile in (1024, 768, 512, 256, HD) if width % tile == 0)
+    readers, _, width = returned[0].shape
+    tile = next(tile for tile in (768, 512, 256, HD) if width % tile == 0)
+    steps = width // tile
+
+    def spec(part):
+        return pl.BlockSpec(
+            (readers, NBR_LEN, tile),
+            lambda j, s: (0, 0, jnp.clip(j - part * steps, 0, steps - 1)),
+        )
+
     return pl.pallas_call(
-        settle_kernel,
+        functools.partial(settle_kernel, steps),
         grid_spec=pltpu.PrefetchScalarGridSpec(
             num_scalar_prefetch=1,
-            grid=(width // tile,),
-            in_specs=[pl.BlockSpec((readers, NBR_LEN, tile), lambda j, s: (0, 0, j))],
+            grid=(len(returned) * steps,),
+            in_specs=[spec(part) for part in range(len(returned))],
             out_specs=pl.BlockSpec((NB_DEV * NBR_LEN, tile), lambda j, s: (0, j)),
         ),
-        out_shape=jax.ShapeDtypeStruct((NB_DEV * NBR_LEN, width), jnp.bfloat16),
+        out_shape=jax.ShapeDtypeStruct((NB_DEV * NBR_LEN, len(returned) * width), jnp.bfloat16),
         compiler_params=pltpu.CompilerParams(vmem_limit_bytes=42 * MIB),
         cost_estimate=SMALL,
         name="settle",
-    )(slots, returned)
+    )(slots, *returned)
 
 
 def local(kv_part, queries, w_out, d_out, nbr_owner, nbr_slot):
@@ -426,11 +437,13 @@
         outwards = send(d_out, OUTWARDS)
         line = LineSum(kv_term, me)
         line.add_beside()
+        line.swap_beside()
         line.add_far(across, outwards)
         line.add_near(line.far_in)
         share = line.finish()
         two_in = send(after(d_out, line.near_sum), TWO_IN)
-        inwards = send(after(d_out, two_in), INWARDS)
+        grads = back_project([(after(me, share), [d_out])], w_out, None, jnp.float32)
+        inwards = send(after(d_out, grads), INWARDS)
         groups = [
             (me, [d_out]),
             (near_of(me), [across, send(after(across, line.near_sum), OUTWARDS)]),
@@ -445,19 +458,28 @@
         share.reshape(NB_DEV, NBR_LEN, share_width), "dp", axis=0, tiled=True
     )
 
+    parts = 2 if (head_width // HD) % 4 == 0 else 1
+
+    def grad_part(ids, part):
+        return attend_grad(ids, owners, dp_count, queries, grads, blocks, part, parts)
+
     def mixed_term(shard, received):
         return project(shard, [attended], w_out, out_width, received)
 
     if count == 4:
-        grads = back_project(groups[:1], w_out, None, jnp.float32)
+        near = (after(groups[1][0], two_in), groups[1][1])
+        grads = back_project([near], w_out, grads, jnp.float32)
         attended = attend(after(ids, grads), queries, blocks, 0)
         line = LineSum(mixed_term, me)
-        first = (after(groups[1][0], line.near), groups[1][1])
-        grads = back_project([first] + groups[2:], w_out, grads, jnp.bfloat16)
-        own_sums = attend_grad(ids, owners, dp_count, queries, grads, [blocks])
-        line.add_far(own_sums)
-        line.add_beside(line.far_sum)
+        first = (after(groups[2][0], line.near), groups[2][1])
+        grads = back_project([first] + groups[3:], w_out, grads, jnp.bfloat16)
+        own_sums = [grad_part(ids, 0)]
+        line.add_far(own_sums[0])
+        own_sums.append(grad_part(after(ids, line.far_sum), 1))
+        line.add_beside(own_sums[1])
+        line.swap_beside(line.near_in)
         mine = mixed_term(after(me, line.beside), [])
+        own_sums[1] = after(own_sums[1], mine)
         line.add_near(line.far_in, mine)
     else:
         attended = attend(ids, queries, blocks, 0)
@@ -471,11 +493,14 @@
             grads = back_project(
                 groups[at : at + 1], w_out, grads, jnp.bfloat16 if last else jnp.float32
             )
-        own_sums = attend_grad(ids, owners, dp_count, queries, grads, [blocks])
-    returned = lax.all_to_all(own_sums, "dp", split_axis=0, concat_axis=0, tiled=True)
+        own_sums = [grad_part(ids, part) for part in range(parts)]
+    returned = [
+        lax.all_to_all(part, "dp", split_axis=0, concat_axis=0, tiled=True) for part in own_sums
+    ]
     d_kv = settle(serving_slot, returned)
     if count == 4:
-        mixed = sum_of([after(mine, d_kv), *line.received()])
+        mine = sum_of([after(mine, d_kv), line.beside_in, line.far_in])
+        mixed = sum_of([mine, line.near_in])
     return (mixed, d_kv)
 
 

time: 396 us -> 391 us (0.987)
  waiting for transfers between devices: 208 us -> 189 us
  Pallas kernels: 98.9 us -> 108 us
  local copies, waits for them, and re-layouts: 10.6 us -> 17.3 us
    ppermute x16, waiting for transfers between devices: 187 us -> 172 us  [send(): return lax.ppermute(x, 'tensor', hops)]
    unnamed x22 -> x28, local copies, waits for them, and re-layouts: 4.73 us -> 11.4 us
    ppermute x16, starting transfers between devices: 54.9 us -> 50.4 us  [send(): return lax.ppermute(x, 'tensor', hops)]
    pallas_call x2 -> x3, Pallas kernels: 25.2 us -> 29.3 us  [back_project(): pl.pallas_call(functools.partial(back_project_kernel, [len(sources) for _...]
    pallas_call x6 -> x7, Pallas kernels: 13.6 us -> 17.3 us  [sum_of(): pl.pallas_call(sum_kernel, grid=(steps,), in_specs=[block] * len(arrays),...]
    all_to_all x1 -> x2, starting transfers between devices: 4.75 us -> 8.11 us  [local(): lax.all_to_all(part, 'dp', split_axis=0, concat_axis=0, tiled=True)]
    pallas_call x2 -> x3, Pallas kernels: 25.6 us -> 27.6 us  [the longest x2 22.1 us: attend_grad(): pl.pallas_call(functools.partial(attend_grad_kernel, group), grid_spec=pl...]
    all_to_all x1 -> x2, waiting for transfers between devices: 12 us -> 11.6 us  [local(): lax.all_to_all(part, 'dp', split_axis=0, concat_axis=0, tiled=True)]
  transfers between devices with their start and end apart: 18 -> 19, of which waited for: 11 -> 13; matrix products, arithmetic and copies ran while one was open for 2% -> 2% of each run, Pallas kernels for 24% -> 27%
where the time goes in v4:
time: 391 us; the launch traced here: 387 us
  waiting for transfers between devices  189 us (48%)
  Pallas kernels  108 us (28%)
  starting transfers between devices  58.6 us (15%)
  local copies, waits for them, and re-layouts  17.3 us (4%)
  between operations  14.3 us (4%)
    ppermute x16, waiting for transfers between devices, send(): return lax.ppermute(x, 'tensor', hops)  172 us
    ppermute x16, starting transfers between devices, send(): return lax.ppermute(x, 'tensor', hops)  50.4 us
    pallas_call x3, Pallas kernels, back_project(): pl.pallas_call(functools.partial(back_project_kernel, [len(sources) for _...  29.3 us
    pallas_call x4, Pallas kernels, project(): pl.pallas_call(functools.partial(project_kernel, parts, len(received)), g...  24.8 us
    pallas_call x2, Pallas kernels, attend_grad(): pl.pallas_call(functools.partial(attend_grad_kernel, group), grid_spec=pl...  22.1 us
    pallas_call x7, Pallas kernels, sum_of(): pl.pallas_call(sum_kernel, grid=(steps,), in_specs=[block] * len(arrays),...  17.3 us
    all_to_all x2, waiting for transfers between devices, local(): lax.all_to_all(part, 'dp', split_axis=0, concat_axis=0, tiled=True)  11.6 us
    unnamed x28, local copies, waits for them, and re-layouts  11.4 us
  transfers between devices with their start and end apart: 19, of which 13 were waited for; matrix products, arithmetic and copies ran while one was open for 2% of the time, Pallas kernels for 27%

profile of v4, /device:TPU:0, one launch (start us, length us, event | category | flops | bytes accessed | tf_op | source)
XLA Modules:
  0.0 386.9 jit_solution(5183350285225285623)
XLA Ops:
  7.2 2.0 collective-permute-start.2
  9.2 1.3 collective-permute-start.3
  10.5 1.5 dynamic-slice_bitcast_fusion.3.refs_0_
  12.0 8.9 %collective-permute-start.1 = (bf16[256,3072]{1,0:T(8,128)(2,1)S(1)}, bf16[256,3072]{1,0:T(8,128)(2,1)}, u32[]{:S(2)}, u32[]{:S(2)}) collective-permute-start(bf16[256,3072]{1,0:T(8,128)(2,1)S(1)} %dynamic-slice_bitcast_fusion.3.refs_0_), channel_id=1, source_target_pairs={{0,1},{3,2},{4,5},{7,6},{8,9},{11,10},{12,13},{15,14},{16,17},{19,... | collective-permute-start | bytes 4718600 | tf_op jit(solution)/shard_map/ppermute | solution.py:296
  20.9 1.5 dynamic-slice_bitcast_fusion.2.refs_0_
  22.5 2.4 collective-permute-start
  24.9 29.7 %collective-permute-done.1.refs_1_ = bf16[256,3072]{1,0:T(8,128)(2,1)} collective-permute-done((bf16[256,3072]{1,0:T(8,128)(2,1)S(1)}, bf16[256,3072]{1,0:T(8,128)(2,1)}, u32[]{:S(2)}, u32[]{:S(2)}) %collective-permute-start.1) | collective-permute-done | bytes 1572896 | tf_op jit(solution)/shard_map/ppermute | solution.py:296
  54.6 6.1 %collective-permute-done.3.refs_3_ = bf16[512,2048]{1,0:T(8,128)(2,1)} collective-permute-done((bf16[512,2048]{1,0:T(8,128)(2,1)}, bf16[512,2048]{1,0:T(8,128)(2,1)}, u32[]{:S(2)}, u32[]{:S(2)}) %collective-permute-start.3) | collective-permute-done | bytes 2097184 | tf_op jit(solution)/shard_map/ppermute | solution.py:296
  60.7 2.5 sum_of.7
  63.1 1.3 collective-permute-start.4
  64.4 2.1 dynamic-slice_bitcast_fusion
  66.5 4.5 %collective-permute-start.7 = (bf16[256,3072]{1,0:T(8,128)(2,1)S(1)}, bf16[256,3072]{1,0:T(8,128)(2,1)S(1)}, u32[]{:S(2)}, u32[]{:S(2)}) collective-permute-start(bf16[256,3072]{1,0:T(8,128)(2,1)S(1)} %get-tuple-element.42), channel_id=1, source_target_pairs={{0,1},{1,0},{2,3},{3,2},{4,5},{5,4},{6,7},{7,6},{8,9},{9,8},{10,11... | collective-permute-start | bytes 4718600 | tf_op jit(solution)/shard_map/ppermute | solution.py:296
  71.0 17.3 %collective-permute-done.refs_1_ = bf16[256,3072]{1,0:T(8,128)(2,1)} collective-permute-done((bf16[256,3072]{1,0:T(8,128)(2,1)S(1)}, bf16[256,3072]{1,0:T(8,128)(2,1)}, u32[]{:S(2)}, u32[]{:S(2)}) %collective-permute-start) | collective-permute-done | bytes 1572896 | tf_op jit(solution)/shard_map/ppermute | solution.py:296
  88.3 13.2 %collective-permute-done.4.refs_2_ = bf16[256,3072]{1,0:T(8,128)(2,1)S(1)} collective-permute-done((bf16[256,3072]{1,0:T(8,128)(2,1)}, bf16[256,3072]{1,0:T(8,128)(2,1)S(1)}, u32[]{:S(2)}, u32[]{:S(2)}) %collective-permute-start.4) | collective-permute-done | bytes 1572896 | tf_op jit(solution)/shard_map/ppermute | solution.py:296
  101.5 1.6 sum_of.8
  103.1 0.8 collective-permute-start.8
  103.8 31.3 %collective-permute-done.7.refs_1_ = bf16[256,3072]{1,0:T(8,128)(2,1)S(1)} collective-permute-done((bf16[256,3072]{1,0:T(8,128)(2,1)S(1)}, bf16[256,3072]{1,0:T(8,128)(2,1)S(1)}, u32[]{:S(2)}, u32[]{:S(2)}) %collective-permute-start.7) | collective-permute-done | bytes 1572896 | tf_op jit(solution)/shard_map/ppermute | solution.py:296
  135.1 1.7 sum_of.9
  136.8 7.6 %collective-permute-start.5 = (bf16[512,2048]{1,0:T(8,128)(2,1)}, bf16[512,2048]{1,0:T(8,128)(2,1)}, u32[]{:S(2)}, u32[]{:S(2)}) collective-permute-start(bf16[512,2048]{1,0:T(8,128)(2,1)} %refs_1_.6), channel_id=1, source_target_pairs={{3,1},{0,2},{7,5},{4,6},{11,9},{8,10},{15,13},{12,14},{19,17},{16,... | collective-permute-start | bytes 6291464 | tf_op jit(solution)/shard_map/ppermute | solution.py:296
  144.3 1.3 collective-permute-start.6
  145.7 7.2 %back_project.3.refs_3_ = f32[512,1536]{1,0:T(8,128)S(1)} custom-call(s32[1]{0:T(128)} %bitcast.6.shards_ref, bf16[1536,8192]{1,0:T(8,128)(2,1)} %refs_1_.11, bf16[512,2048]{1,0:T(8,128)(2,1)} %refs_1_.6), custom_call_target="tpu_custom_call" | custom-call | flops 1 | bytes 1 | tf_op jit(solution)/shard_map/back_project/pallas_call | solution.py:263
  152.9 1.6 copy-done.3
  154.5 5.8 %collective-permute-start.10 = (bf16[512,2048]{1,0:T(8,128)(2,1)}, bf16[512,2048]{1,0:T(8,128)(2,1)}, u32[]{:S(2)}, u32[]{:S(2)}) collective-permute-start(bf16[512,2048]{1,0:T(8,128)(2,1)} %refs_1_.6), channel_id=1, source_target_pairs={{0,1},{3,2},{4,5},{7,6},{8,9},{11,10},{12,13},{15,14},{16,17},{19,... | collective-permute-start | bytes 6291464 | tf_op jit(solution)/shard_map/ppermute | solution.py:296
  160.4 29.0 %collective-permute-done.5.refs_4_ = bf16[512,2048]{1,0:T(8,128)(2,1)} collective-permute-done((bf16[512,2048]{1,0:T(8,128)(2,1)}, bf16[512,2048]{1,0:T(8,128)(2,1)}, u32[]{:S(2)}, u32[]{:S(2)}) %collective-permute-start.5) | collective-permute-done | bytes 2097184 | tf_op jit(solution)/shard_map/ppermute | solution.py:296
  189.4 1.3 collective-permute-start.11
  191.1 3.4 collective-permute-done.6.refs_2_
  194.5 1.3 copy-done.8
  195.8 1.6 copy-done.9
  197.4 8.6 %back_project.4.refs_6_ = f32[512,1536]{1,0:T(8,128)} custom-call(s32[1]{0:T(128)} %bitcast.3.shards_ref, bf16[1536,8192]{1,0:T(8,128)(2,1)} %refs_1_.11, bf16[512,2048]{1,0:T(8,128)(2,1)} %collective-permute-done.2.refs_1_, bf16[512,2048]{1,0:T(8,128)(2,1)S(1)} %copy-done.9, f32[512,1536]{1,0:T(8,128)} %copy-done.3), custom_call_target="tpu_custom_call" | custom-call | flops 1 | bytes 1 | tf_op jit(solution)/shard_map/back_project/pallas_call | solution.py:263
  206.0 5.3 %all-gather.2.cloned.1.call-done.refs_0_.refs_1_.refs_2_.refs_3_ = bf16[16,128,3072]{2,1,0:T(8,128)(2,1)} async-done(((bf16[2,128,3072]{2,1,0:T(8,128)(2,1)}), bf16[16,128,3072]{2,1,0:T(8,128)(2,1)}) %all-gather.2.cloned.1.call-update) | async-done | bytes 12582928 | tf_op jit(solution)/shard_map/all_gather | solution.py:457
  211.3 8.9 %attend.1.refs_0_ = bf16[512,1536]{1,0:T(8,128)(2,1)S(1)} custom-call(s32[16]{0:T(128)S(1)} %multiply_add_fusion.ids_ref, bf16[512,1536]{1,0:T(8,128)(2,1)S(1)} %copy-done, bf16[16,128,3072]{2,1,0:T(8,128)(2,1)} %all-gather.2.cloned.1.call-done.refs_0_.refs_1_.refs_2_.refs_3_, ...), custom_call_target="tpu_custom_call" | custom-call | flops 1 | bytes 1 | tf_op jit(solution)/shard_map/attend/pallas_call | solution.py:82
  220.2 6.9 %project.4.refs_0_ = bf16[512,2048]{1,0:T(8,128)(2,1)} custom-call(s32[1]{0:T(128)} %bitcast.shard_ref, bf16[512,1536]{1,0:T(8,128)(2,1)S(1)} %attend.1.refs_0_, bf16[1536,8192]{1,0:T(8,128)(2,1)} %refs_1_.11), custom_call_target="tpu_custom_call" | custom-call | flops 1 | bytes 1 | tf_op jit(solution)/shard_map/project/pallas_call | solution.py:221
  227.1 4.7 %collective-permute-start.9 = (bf16[512,2048]{1,0:T(8,128)(2,1)}, bf16[512,2048]{1,0:T(8,128)(2,1)}, u32[]{:S(2)}, u32[]{:S(2)}) collective-permute-start(bf16[512,2048]{1,0:T(8,128)(2,1)} %project.4.refs_0_), channel_id=1, source_target_pairs={{0,1},{3,2},{4,5},{7,6},{8,9},{11,10},{12,13},{15,14},{16,17},{19,... | collective-permute-start | bytes 6291464 | tf_op jit(solution)/shard_map/ppermute | solution.py:296
  231.8 6.0 %project.5.refs_0_ = bf16[512,2048]{1,0:T(8,128)(2,1)S(1)} custom-call(s32[1]{0:T(128)} %bitcast.8.shard_ref, bf16[512,1536]{1,0:T(8,128)(2,1)S(1)} %attend.1.refs_0_, bf16[1536,8192]{1,0:T(8,128)(2,1)} %refs_1_.11), custom_call_target="tpu_custom_call" | custom-call | flops 1 | bytes 1 | tf_op jit(solution)/shard_map/project/pallas_call | solution.py:221
  237.8 1.3 copy-done.4
  239.2 13.5 %back_project.5.g_ref = bf16[512,1536]{1,0:T(8,128)(2,1)S(1)} custom-call(s32[2]{0:T(128)S(1)} %pad_add_fusion.shards_ref, bf16[1536,8192]{1,0:T(8,128)(2,1)} %refs_1_.11, bf16[1536,8192]{1,0:T(8,128)(2,1)} %refs_1_.11, bf16[512,2048]{1,0:T(8,128)(2,1)} %collective-permute-done.10.refs_2_, bf16[512,2048]{1,0:T(8,128)(2,1)} %collective-permute-done.3.refs_3_, ...), custom_call_target="tpu_custom_call" | custom-call | flops 1 | bytes 1 | tf_op jit(solution)/shard_map/back_project/pallas_call | solution.py:263
  252.7 11.0 %attend_grad.2 = bf16[8,128,1536]{2,1,0:T(8,128)(2,1)} custom-call(s32[16]{0:T(128)S(1)} %multiply_add_fusion.ids_ref, s32[16]{0:T(128)S(1)} %reshape.36.own_ref, bf16[512,1536]{1,0:T(8,128)(2,1)S(1)} %copy-done, bf16[512,1536]{1,0:T(8,128)(2,1)S(1)} %back_project.5.g_ref, ...), custom_call_target="tpu_custom_call" | custom-call | flops 1 | bytes 1 | tf_op jit(solution)/shard_map/attend_grad/pallas_call | solution.py:178
  263.7 1.1 copy-done.1
  264.8 4.5 %all-to-all-start = ((bf16[8,128,1536]{2,1,0:T(8,128)(2,1)}), bf16[8,128,1536]{2,1,0:T(8,128)(2,1)}, u32[]{:S(2)}, u32[]{:S(2)}) async-start(bf16[8,128,1536]{2,1,0:T(8,128)(2,1)} %attend_grad.2), calls=%async_computation | async-start | bytes 6291456 | tf_op jit(solution)/shard_map/all_to_all | solution.py:498
  269.3 2.8 collective-permute-start.12
  272.1 4.7 %collective-permute-done.9.refs_1_ = bf16[512,2048]{1,0:T(8,128)(2,1)} collective-permute-done((bf16[512,2048]{1,0:T(8,128)(2,1)}, bf16[512,2048]{1,0:T(8,128)(2,1)}, u32[]{:S(2)}, u32[]{:S(2)}) %collective-permute-start.9) | collective-permute-done | bytes 2097184 | tf_op jit(solution)/shard_map/ppermute | solution.py:296
  276.8 3.4 sum_of.10
  280.2 1.3 collective-permute-start.14
  281.5 11.1 %attend_grad.3 = bf16[8,128,1536]{2,1,0:T(8,128)(2,1)} custom-call(s32[16]{0:T(128)S(1)} %multiply_add_fusion.ids_ref, s32[16]{0:T(128)S(1)} %reshape.36.own_ref, bf16[512,1536]{1,0:T(8,128)(2,1)S(1)} %copy-done, bf16[512,1536]{1,0:T(8,128)(2,1)S(1)} %copy-done.2, bf16[16,128,3072]{2,1,0:T(8,128)(2,1)} %all-gather.2.cloned.1.call-done.refs_0_.refs_1_.refs_2_.refs_3_, ...), custom_call_target="tpu_custom_call" | custom-call | flops 1 | bytes 1 | tf_op jit(solution)/shard_map/attend_grad/pallas_call | solution.py:178
  292.5 6.0 %project.6 = bf16[512,2048]{1,0:T(8,128)(2,1)S(1)} custom-call(s32[1]{0:T(128)} %bitcast.10.shard_ref, bf16[512,1536]{1,0:T(8,128)(2,1)S(1)} %attend.1.refs_0_, bf16[1536,8192]{1,0:T(8,128)(2,1)} %refs_1_.11), custom_call_target="tpu_custom_call" | custom-call | flops 1 | bytes 1 | tf_op jit(solution)/shard_map/project/pallas_call | solution.py:221
  298.5 1.3 copy-done.10
  299.9 6.0 %project.7.refs_0_ = bf16[512,2048]{1,0:T(8,128)(2,1)S(1)} custom-call(s32[1]{0:T(128)} %bitcast.11.shard_ref, bf16[512,1536]{1,0:T(8,128)(2,1)S(1)} %attend.1.refs_0_, bf16[1536,8192]{1,0:T(8,128)(2,1)} %refs_1_.11), custom_call_target="tpu_custom_call" | custom-call | flops 1 | bytes 1 | tf_op jit(solution)/shard_map/project/pallas_call | solution.py:221
  305.8 1.3 copy-done.6
  307.2 3.6 all-to-all-start.1
  310.8 10.2 %collective-permute-done.12.refs_1_ = bf16[512,2048]{1,0:T(8,128)(2,1)} collective-permute-done((bf16[512,2048]{1,0:T(8,128)(2,1)}, bf16[512,2048]{1,0:T(8,128)(2,1)}, u32[]{:S(2)}, u32[]{:S(2)}) %collective-permute-start.12) | collective-permute-done | bytes 2097184 | tf_op jit(solution)/shard_map/ppermute | solution.py:296
  321.0 2.5 collective-permute-start.13
  323.5 6.3 %collective-permute-done.14.refs_2_ = bf16[512,2048]{1,0:T(8,128)(2,1)} collective-permute-done((bf16[512,2048]{1,0:T(8,128)(2,1)}, bf16[512,2048]{1,0:T(8,128)(2,1)}, u32[]{:S(2)}, u32[]{:S(2)}) %collective-permute-start.14) | collective-permute-done | bytes 2097184 | tf_op jit(solution)/shard_map/ppermute | solution.py:296
  329.8 1.6 copy-done.5
  331.4 2.8 sum_of.12
  334.3 2.0 collective-permute-start.15
  336.3 0.1 copy.27
  336.4 0.1 copy.26
  336.6 0.2 select_reduce_fusion
  336.8 0.2 dynamic-slice_reduce_fusion.slot_ref
  337.0 11.6 %all-to-all-done.1.refs_1_ = bf16[8,128,1536]{2,1,0:T(8,128)(2,1)S(1)} async-done(((bf16[8,128,1536]{2,1,0:T(8,128)(2,1)}), bf16[8,128,1536]{2,1,0:T(8,128)(2,1)S(1)}, u32[]{:S(2)}, u32[]{:S(2)}) %all-to-all-start.1) | async-done | bytes 3145760 | tf_op jit(solution)/shard_map/all_to_all | solution.py:498
  348.6 5.5 %settle.1 = bf16[256,3072]{1,0:T(8,128)(2,1)} custom-call(s32[8]{0:T(128)S(1)} %dynamic-slice_reduce_fusion.slot_ref, bf16[8,128,1536]{2,1,0:T(8,128)(2,1)} %all-to-all-done.refs_0_, bf16[8,128,1536]{2,1,0:T(8,128)(2,1)S(1)} %all-to-all-done.1.refs_1_), custom_call_target="tpu_custom_call" | custom-call | flops 1 | bytes 1 | tf_op jit(solution)/shard_map/settle/pallas_call | solution.py:389
  354.1 20.5 %collective-permute-done.13.refs_1_ = bf16[512,2048]{1,0:T(8,128)(2,1)} collective-permute-done((bf16[512,2048]{1,0:T(8,128)(2,1)}, bf16[512,2048]{1,0:T(8,128)(2,1)}, u32[]{:S(2)}, u32[]{:S(2)}) %collective-permute-start.13) | collective-permute-done | bytes 2097184 | tf_op jit(solution)/shard_map/ppermute | solution.py:296
  374.7 2.6 sum_of.11.refs_0_
  377.3 2.8 sum_of.13
  (35 shorter events, 0.8 us)
Async XLA Ops:
  7.2 204.1 %all-gather.2.cloned.1.call-start = ((), (), s32[]{:S(2)}) async-start(), calls=%async_computation.2 | async-start | bytes 14155776 | tf_op jit(solution)/shard_map/all_gather | solution.py:457
  7.2 47.4 %collective-permute-start.2 = (bf16[512,2048]{1,0:T(8,128)(2,1)}, bf16[512,2048]{1,0:T(8,128)(2,1)}, u32[]{:S(2)}, u32[]{:S(2)}) collective-permute-start(bf16[512,2048]{1,0:T(8,128)(2,1)} %refs_1_.6), channel_id=1, source_target_pairs={{1,2},{2,1},{5,6},{6,5},{9,10},{10,9},{13,14},{14,13},{17,18},{18,... | collective-permute-start | bytes 6291464 | tf_op jit(solution)/shard_map/ppermute | solution.py:296
  9.2 51.5 %collective-permute-start.3 = (bf16[512,2048]{1,0:T(8,128)(2,1)}, bf16[512,2048]{1,0:T(8,128)(2,1)}, u32[]{:S(2)}, u32[]{:S(2)}) collective-permute-start(bf16[512,2048]{1,0:T(8,128)(2,1)} %refs_1_.6), channel_id=1, source_target_pairs={{1,0},{2,3},{5,4},{6,7},{9,8},{10,11},{13,12},{14,15},{17,16},{18,... | collective-permute-start | bytes 6291464 | tf_op jit(solution)/shard_map/ppermute | solution.py:296
  12.0 42.6 %collective-permute-start.1 = (bf16[256,3072]{1,0:T(8,128)(2,1)S(1)}, bf16[256,3072]{1,0:T(8,128)(2,1)}, u32[]{:S(2)}, u32[]{:S(2)}) collective-permute-start(bf16[256,3072]{1,0:T(8,128)(2,1)S(1)} %dynamic-slice_bitcast_fusion.3.refs_0_), channel_id=1, source_target_pairs={{0,1},{3,2},{4,5},{7,6},{8,9},{11,10},{12,13},{15,14},{16,17},{19,... | collective-permute-start | bytes 4718600 | tf_op jit(solution)/shard_map/ppermute | solution.py:296
  22.5 65.8 %collective-permute-start = (bf16[256,3072]{1,0:T(8,128)(2,1)S(1)}, bf16[256,3072]{1,0:T(8,128)(2,1)}, u32[]{:S(2)}, u32[]{:S(2)}) collective-permute-start(bf16[256,3072]{1,0:T(8,128)(2,1)S(1)} %dynamic-slice_bitcast_fusion.2.refs_0_), channel_id=1, source_target_pairs={{0,1},{3,2},{4,5},{7,6},{8,9},{11,10},{12,13},{15,14},{16,17},{19,... | collective-permute-start | bytes 4718600 | tf_op jit(solution)/shard_map/ppermute | solution.py:296
  63.1 38.4 %collective-permute-start.4 = (bf16[256,3072]{1,0:T(8,128)(2,1)}, bf16[256,3072]{1,0:T(8,128)(2,1)S(1)}, u32[]{:S(2)}, u32[]{:S(2)}) collective-permute-start(bf16[256,3072]{1,0:T(8,128)(2,1)} %sum_of.7), channel_id=1, source_target_pairs={{1,3},{2,0},{5,7},{6,4},{9,11},{10,8},{13,15},{14,12},{17,19},{18,... | collective-permute-start | bytes 4718600 | tf_op jit(solution)/shard_map/ppermute | solution.py:296
  66.5 68.6 %collective-permute-start.7 = (bf16[256,3072]{1,0:T(8,128)(2,1)S(1)}, bf16[256,3072]{1,0:T(8,128)(2,1)S(1)}, u32[]{:S(2)}, u32[]{:S(2)}) collective-permute-start(bf16[256,3072]{1,0:T(8,128)(2,1)S(1)} %get-tuple-element.42), channel_id=1, source_target_pairs={{0,1},{1,0},{2,3},{3,2},{4,5},{5,4},{6,7},{7,6},{8,9},{9,8},{10,11... | collective-permute-start | bytes 4718600 | tf_op jit(solution)/shard_map/ppermute | solution.py:296
  103.1 32.0 %collective-permute-start.8 = (bf16[256,3072]{1,0:T(8,128)(2,1)S(1)}, bf16[256,3072]{1,0:T(8,128)(2,1)S(1)}, u32[]{:S(2)}, u32[]{:S(2)}) collective-permute-start(bf16[256,3072]{1,0:T(8,128)(2,1)S(1)} %sum_of.8), channel_id=1, source_target_pairs={{1,2},{2,1},{5,6},{6,5},{9,10},{10,9},{13,14},{14,13},{17,18},{18,... | collective-permute-start | bytes 4718600 | tf_op jit(solution)/shard_map/ppermute | solution.py:296
  136.8 52.6 %collective-permute-start.5 = (bf16[512,2048]{1,0:T(8,128)(2,1)}, bf16[512,2048]{1,0:T(8,128)(2,1)}, u32[]{:S(2)}, u32[]{:S(2)}) collective-permute-start(bf16[512,2048]{1,0:T(8,128)(2,1)} %refs_1_.6), channel_id=1, source_target_pairs={{3,1},{0,2},{7,5},{4,6},{11,9},{8,10},{15,13},{12,14},{19,17},{16,... | collective-permute-start | bytes 6291464 | tf_op jit(solution)/shard_map/ppermute | solution.py:296
  144.3 50.1 %collective-permute-start.6 = (bf16[512,2048]{1,0:T(8,128)(2,1)}, bf16[512,2048]{1,0:T(8,128)(2,1)S(1)}, u32[]{:S(2)}, u32[]{:S(2)}) collective-permute-start(bf16[512,2048]{1,0:T(8,128)(2,1)} %collective-permute-done.2.refs_1_), channel_id=1, source_target_pairs={{1,0},{2,3},{5,4},{6,7},{9,8},{10,11},{13,12},{14,15},{17,16},{18,... | collective-permute-start | bytes 6291464 | tf_op jit(solution)/shard_map/ppermute | solution.py:296
  145.6 45.0 %copy-start.11 = (s32[64,2]{0,1:T(2,128)S(1)}, s32[64,2]{0,1:T(2,128)}, u32[]{:S(2)}) copy-start(s32[64,2]{0,1:T(2,128)} %param.11) | copy-start | bytes 1540
  145.6 45.0 %copy-start.12 = (s32[64,2]{0,1:T(2,128)S(1)}, s32[64,2]{0,1:T(2,128)}, u32[]{:S(2)}) copy-start(s32[64,2]{0,1:T(2,128)} %param.10) | copy-start | bytes 1540
  152.9 1.6 copy-start.3
  154.5 84.6 %collective-permute-start.10 = (bf16[512,2048]{1,0:T(8,128)(2,1)}, bf16[512,2048]{1,0:T(8,128)(2,1)}, u32[]{:S(2)}, u32[]{:S(2)}) collective-permute-start(bf16[512,2048]{1,0:T(8,128)(2,1)} %refs_1_.6), channel_id=1, source_target_pairs={{0,1},{3,2},{4,5},{7,6},{8,9},{11,10},{12,13},{15,14},{16,17},{19,... | collective-permute-start | bytes 6291464 | tf_op jit(solution)/shard_map/ppermute | solution.py:296
  189.4 49.8 %collective-permute-start.11 = (bf16[512,2048]{1,0:T(8,128)(2,1)}, bf16[512,2048]{1,0:T(8,128)(2,1)}, u32[]{:S(2)}, u32[]{:S(2)}) collective-permute-start(bf16[512,2048]{1,0:T(8,128)(2,1)} %collective-permute-done.5.refs_4_), channel_id=1, source_target_pairs={{1,0},{2,3},{5,4},{6,7},{9,8},{10,11},{13,12},{14,15},{17,16},{18,... | collective-permute-start | bytes 6291464 | tf_op jit(solution)/shard_map/ppermute | solution.py:296
  194.5 1.3 copy-start.8
  195.8 1.6 copy-start.9
  197.4 13.9 %copy-start = (bf16[512,1536]{1,0:T(8,128)(2,1)S(1)}, bf16[512,1536]{1,0:T(8,128)(2,1)}, u32[]{:S(2)}) copy-start(bf16[512,1536]{1,0:T(8,128)(2,1)} %q_ref.5) | copy-start | bytes 4718596
  227.1 49.7 %collective-permute-start.9 = (bf16[512,2048]{1,0:T(8,128)(2,1)}, bf16[512,2048]{1,0:T(8,128)(2,1)}, u32[]{:S(2)}, u32[]{:S(2)}) collective-permute-start(bf16[512,2048]{1,0:T(8,128)(2,1)} %project.4.refs_0_), channel_id=1, source_target_pairs={{0,1},{3,2},{4,5},{7,6},{8,9},{11,10},{12,13},{15,14},{16,17},{19,... | collective-permute-start | bytes 6291464 | tf_op jit(solution)/shard_map/ppermute | solution.py:296
  237.8 1.3 copy-start.4
  263.7 1.1 copy-start.1
  264.8 42.4 %all-to-all-start = ((bf16[8,128,1536]{2,1,0:T(8,128)(2,1)}), bf16[8,128,1536]{2,1,0:T(8,128)(2,1)}, u32[]{:S(2)}, u32[]{:S(2)}) async-start(bf16[8,128,1536]{2,1,0:T(8,128)(2,1)} %attend_grad.2), calls=%async_computation | async-start | bytes 6291456 | tf_op jit(solution)/shard_map/all_to_all | solution.py:498
  269.3 12.2 %copy-start.2 = (bf16[512,1536]{1,0:T(8,128)(2,1)S(1)}, bf16[512,1536]{1,0:T(8,128)(2,1)}, u32[]{:S(2)}) copy-start(bf16[512,1536]{1,0:T(8,128)(2,1)} %copy-done.1) | copy-start | bytes 4718596
  269.3 51.7 %collective-permute-start.12 = (bf16[512,2048]{1,0:T(8,128)(2,1)}, bf16[512,2048]{1,0:T(8,128)(2,1)}, u32[]{:S(2)}, u32[]{:S(2)}) collective-permute-start(bf16[512,2048]{1,0:T(8,128)(2,1)} %copy-done.4), channel_id=1, source_target_pairs={{0,1},{3,2},{4,5},{7,6},{8,9},{11,10},{12,13},{15,14},{16,17},{19,... | collective-permute-start | bytes 6291464 | tf_op jit(solution)/shard_map/ppermute | solution.py:296
  280.2 49.7 %collective-permute-start.14 = (bf16[512,2048]{1,0:T(8,128)(2,1)}, bf16[512,2048]{1,0:T(8,128)(2,1)}, u32[]{:S(2)}, u32[]{:S(2)}) collective-permute-start(bf16[512,2048]{1,0:T(8,128)(2,1)} %sum_of.10), channel_id=1, source_target_pairs={{1,3},{2,0},{5,7},{6,4},{9,11},{10,8},{13,15},{14,12},{17,19},{18,... | collective-permute-start | bytes 6291464 | tf_op jit(solution)/shard_map/ppermute | solution.py:296
  298.5 1.4 copy-start.10
  305.8 1.3 copy-start.6
  307.2 41.5 %all-to-all-start.1 = ((bf16[8,128,1536]{2,1,0:T(8,128)(2,1)}), bf16[8,128,1536]{2,1,0:T(8,128)(2,1)S(1)}, u32[]{:S(2)}, u32[]{:S(2)}) async-start(bf16[8,128,1536]{2,1,0:T(8,128)(2,1)} %attend_grad.3), calls=%async_computation.1 | async-start | bytes 6291456 | tf_op jit(solution)/shard_map/all_to_all | solution.py:498
  321.0 53.6 %collective-permute-start.13 = (bf16[512,2048]{1,0:T(8,128)(2,1)}, bf16[512,2048]{1,0:T(8,128)(2,1)}, u32[]{:S(2)}, u32[]{:S(2)}) collective-permute-start(bf16[512,2048]{1,0:T(8,128)(2,1)} %copy-done.10), channel_id=1, source_target_pairs={{0,1},{1,0},{2,3},{3,2},{4,5},{5,4},{6,7},{7,6},{8,9},{9,8},{10,11... | collective-permute-start | bytes 6291464 | tf_op jit(solution)/shard_map/ppermute | solution.py:296
  329.8 1.6 copy-start.5
  334.3 43.0 %collective-permute-start.15 = (bf16[512,2048]{1,0:T(8,128)(2,1)}, bf16[512,2048]{1,0:T(8,128)(2,1)}, u32[]{:S(2)}, u32[]{:S(2)}) collective-permute-start(bf16[512,2048]{1,0:T(8,128)(2,1)} %sum_of.12), channel_id=1, source_target_pairs={{1,2},{2,1},{5,6},{6,5},{9,10},{10,9},{13,14},{14,13},{17,18},{18,... | collective-permute-start | bytes 6291464 | tf_op jit(solution)/shard_map/ppermute | solution.py:296
  348.6 26.0 %copy-start.7 = (bf16[512,2048]{1,0:T(8,128)(2,1)S(1)}, bf16[512,2048]{1,0:T(8,128)(2,1)}, u32[]{:S(2)}) copy-start(bf16[512,2048]{1,0:T(8,128)(2,1)} %copy-done.6) | copy-start | bytes 6291460
Sparse Core Ops, SparseCore 0:
  136.9 74.3 all-gather.1

commit v5 on v4

--- a/solution.py
+++ b/solution.py
@@ -428,17 +428,20 @@
     ids = owners * NB_DEV + slots
     serving_slot = lax.dynamic_index_in_dim(slot_from, reader, 1, False)
 
+    parts = 2 if (head_width // HD) % 4 == 0 else 1
+    by_line = count == 4 and parts == 2
+
     def kv_term(shard, received):
         term = lax.dynamic_slice_in_dim(kv_part[0], shard * share_width, share_width, 1)
         return sum_of([term, *received]) if received else term
 
-    if count == 4:
-        across = send(d_out, ACROSS)
+    if by_line:
         outwards = send(d_out, OUTWARDS)
         line = LineSum(kv_term, me)
-        line.add_beside()
+        across = send(after(d_out, line.far), ACROSS)
+        line.add_far(outwards)
+        line.add_beside(across)
         line.swap_beside()
-        line.add_far(across, outwards)
         line.add_near(line.far_in)
         share = line.finish()
         two_in = send(after(d_out, line.near_sum), TWO_IN)
@@ -458,15 +461,13 @@
         share.reshape(NB_DEV, NBR_LEN, share_width), "dp", axis=0, tiled=True
     )
 
-    parts = 2 if (head_width // HD) % 4 == 0 else 1
-
     def grad_part(ids, part):
         return attend_grad(ids, owners, dp_count, queries, grads, blocks, part, parts)
 
     def mixed_term(shard, received):
         return project(shard, [attended], w_out, out_width, received)
 
-    if count == 4:
+    if by_line:
         near = (after(groups[1][0], two_in), groups[1][1])
         grads = back_project([near], w_out, grads, jnp.float32)
         attended = attend(after(ids, grads), queries, blocks, 0)
@@ -498,7 +499,7 @@
         lax.all_to_all(part, "dp", split_axis=0, concat_axis=0, tiled=True) for part in own_sums
     ]
     d_kv = settle(serving_slot, returned)
-    if count == 4:
+    if by_line:
         mine = sum_of([after(mine, d_kv), line.beside_in, line.far_in])
         mixed = sum_of([mine, line.near_in])
     return (mixed, d_kv)

time: 391 us -> 388 us (level)
  waiting for transfers between devices: 189 us -> 182 us
  starting transfers between devices: 58.6 us -> 63.5 us
    ppermute x16, waiting for transfers between devices: 172 us -> 164 us  [send(): return lax.ppermute(x, 'tensor', hops)]
    ppermute x16, starting transfers between devices: 50.4 us -> 54.3 us  [send(): return lax.ppermute(x, 'tensor', hops)]
  transfers between devices with their start and end apart: 19 -> 19, of which waited for: 13 -> 14; matrix products, arithmetic and copies ran while one was open for 2% -> 2% of each run, Pallas kernels for 27% -> 27%
where the time goes in v5:
time: 388 us; the launch traced here: 386 us
  waiting for transfers between devices  182 us (47%)
  Pallas kernels  108 us (28%)
  starting transfers between devices  63.5 us (16%)
  local copies, waits for them, and re-layouts  17.4 us (4%)
  between operations  14.3 us (4%)
    ppermute x16, waiting for transfers between devices, send(): return lax.ppermute(x, 'tensor', hops)  164 us
    ppermute x16, starting transfers between devices, send(): return lax.ppermute(x, 'tensor', hops)  54.3 us
    pallas_call x3, Pallas kernels, back_project(): pl.pallas_call(functools.partial(back_project_kernel, [len(sources) for _...  29.2 us
    pallas_call x4, Pallas kernels, project(): pl.pallas_call(functools.partial(project_kernel, parts, len(received)), g...  24.8 us
    pallas_call x2, Pallas kernels, attend_grad(): pl.pallas_call(functools.partial(attend_grad_kernel, group), grid_spec=pl...  22.1 us
    pallas_call x7, Pallas kernels, sum_of(): pl.pallas_call(sum_kernel, grid=(steps,), in_specs=[block] * len(arrays),...  17.3 us
    all_to_all x2, waiting for transfers between devices, local(): lax.all_to_all(part, 'dp', split_axis=0, concat_axis=0, tiled=True)  13.4 us
    unnamed x28, local copies, waits for them, and re-layouts  11.5 us
  transfers between devices with their start and end apart: 19, of which 14 were waited for; matrix products, arithmetic and copies ran while one was open for 2% of the time, Pallas kernels for 27%

profile of v5, /device:TPU:0, one launch (start us, length us, event | category | flops | bytes accessed | tf_op | source)
XLA Modules:
  0.0 385.8 jit_solution(14638088096036454763)
XLA Ops:
  7.2 1.3 collective-permute-start.2
  8.5 1.5 dynamic-slice_bitcast_fusion.3.refs_0_
  10.0 7.4 %collective-permute-start.1 = (bf16[256,3072]{1,0:T(8,128)(2,1)S(1)}, bf16[256,3072]{1,0:T(8,128)(2,1)}, u32[]{:S(2)}, u32[]{:S(2)}) collective-permute-start(bf16[256,3072]{1,0:T(8,128)(2,1)S(1)} %dynamic-slice_bitcast_fusion.3.refs_0_), channel_id=1, source_target_pairs={{0,1},{3,2},{4,5},{7,6},{8,9},{11,10},{12,13},{15,14},{16,17},{19,... | collective-permute-start | bytes 4718600 | tf_op jit(solution)/shard_map/ppermute | solution.py:296
  17.5 2.0 collective-permute-start.5
  19.5 1.5 dynamic-slice_bitcast_fusion.2.refs_0_
  21.0 4.9 %collective-permute-start = (bf16[256,3072]{1,0:T(8,128)(2,1)S(1)}, bf16[256,3072]{1,0:T(8,128)(2,1)}, u32[]{:S(2)}, u32[]{:S(2)}) collective-permute-start(bf16[256,3072]{1,0:T(8,128)(2,1)S(1)} %dynamic-slice_bitcast_fusion.2.refs_0_), channel_id=1, source_target_pairs={{0,1},{3,2},{4,5},{7,6},{8,9},{11,10},{12,13},{15,14},{16,17},{19,... | collective-permute-start | bytes 4718600 | tf_op jit(solution)/shard_map/ppermute | solution.py:296
  25.9 25.1 %collective-permute-done.1.refs_1_ = bf16[256,3072]{1,0:T(8,128)(2,1)} collective-permute-done((bf16[256,3072]{1,0:T(8,128)(2,1)S(1)}, bf16[256,3072]{1,0:T(8,128)(2,1)}, u32[]{:S(2)}, u32[]{:S(2)}) %collective-permute-start.1) | collective-permute-done | bytes 1572896 | tf_op jit(solution)/shard_map/ppermute | solution.py:296
  51.1 6.4 %collective-permute-done.2.refs_3_ = bf16[512,2048]{1,0:T(8,128)(2,1)} collective-permute-done((bf16[512,2048]{1,0:T(8,128)(2,1)}, bf16[512,2048]{1,0:T(8,128)(2,1)}, u32[]{:S(2)}, u32[]{:S(2)}) %collective-permute-start.2) | collective-permute-done | bytes 2097184 | tf_op jit(solution)/shard_map/ppermute | solution.py:296
  57.5 2.5 sum_of.7
  59.9 1.3 collective-permute-start.3
  61.2 2.1 dynamic-slice_bitcast_fusion
  63.3 7.0 %collective-permute-start.7 = (bf16[256,3072]{1,0:T(8,128)(2,1)S(1)}, bf16[256,3072]{1,0:T(8,128)(2,1)S(1)}, u32[]{:S(2)}, u32[]{:S(2)}) collective-permute-start(bf16[256,3072]{1,0:T(8,128)(2,1)S(1)} %get-tuple-element.44), channel_id=1, source_target_pairs={{0,1},{1,0},{2,3},{3,2},{4,5},{5,4},{6,7},{7,6},{8,9},{9,8},{10,11... | collective-permute-start | bytes 4718600 | tf_op jit(solution)/shard_map/ppermute | solution.py:296
  70.3 14.5 %collective-permute-done.refs_1_ = bf16[256,3072]{1,0:T(8,128)(2,1)} collective-permute-done((bf16[256,3072]{1,0:T(8,128)(2,1)S(1)}, bf16[256,3072]{1,0:T(8,128)(2,1)}, u32[]{:S(2)}, u32[]{:S(2)}) %collective-permute-start) | collective-permute-done | bytes 1572896 | tf_op jit(solution)/shard_map/ppermute | solution.py:296
  84.8 15.4 %collective-permute-done.3.refs_2_ = bf16[256,3072]{1,0:T(8,128)(2,1)S(1)} collective-permute-done((bf16[256,3072]{1,0:T(8,128)(2,1)}, bf16[256,3072]{1,0:T(8,128)(2,1)S(1)}, u32[]{:S(2)}, u32[]{:S(2)}) %collective-permute-start.3) | collective-permute-done | bytes 1572896 | tf_op jit(solution)/shard_map/ppermute | solution.py:296
  100.1 1.6 sum_of.8
  101.7 0.8 collective-permute-start.8
  102.5 31.3 %collective-permute-done.7.refs_1_ = bf16[256,3072]{1,0:T(8,128)(2,1)S(1)} collective-permute-done((bf16[256,3072]{1,0:T(8,128)(2,1)S(1)}, bf16[256,3072]{1,0:T(8,128)(2,1)S(1)}, u32[]{:S(2)}, u32[]{:S(2)}) %collective-permute-start.7) | collective-permute-done | bytes 1572896 | tf_op jit(solution)/shard_map/ppermute | solution.py:296
  133.8 1.7 sum_of.9
  135.4 8.0 %collective-permute-start.4 = (bf16[512,2048]{1,0:T(8,128)(2,1)}, bf16[512,2048]{1,0:T(8,128)(2,1)}, u32[]{:S(2)}, u32[]{:S(2)}) collective-permute-start(bf16[512,2048]{1,0:T(8,128)(2,1)} %refs_1_.6), channel_id=1, source_target_pairs={{3,1},{0,2},{7,5},{4,6},{11,9},{8,10},{15,13},{12,14},{19,17},{16,... | collective-permute-start | bytes 6291464 | tf_op jit(solution)/shard_map/ppermute | solution.py:296
  143.4 1.3 collective-permute-start.6
  144.7 7.2 %back_project.3.refs_3_ = f32[512,1536]{1,0:T(8,128)S(1)} custom-call(s32[1]{0:T(128)} %bitcast.6.shards_ref, bf16[1536,8192]{1,0:T(8,128)(2,1)} %refs_1_.11, bf16[512,2048]{1,0:T(8,128)(2,1)} %refs_1_.6), custom_call_target="tpu_custom_call" | custom-call | flops 1 | bytes 1 | tf_op jit(solution)/shard_map/back_project/pallas_call | solution.py:263
  151.9 1.7 copy-done.3
  153.6 5.8 %collective-permute-start.10 = (bf16[512,2048]{1,0:T(8,128)(2,1)}, bf16[512,2048]{1,0:T(8,128)(2,1)}, u32[]{:S(2)}, u32[]{:S(2)}) collective-permute-start(bf16[512,2048]{1,0:T(8,128)(2,1)} %refs_1_.6), channel_id=1, source_target_pairs={{0,1},{3,2},{4,5},{7,6},{8,9},{11,10},{12,13},{15,14},{16,17},{19,... | collective-permute-start | bytes 6291464 | tf_op jit(solution)/shard_map/ppermute | solution.py:296
  159.4 29.0 %collective-permute-done.4.refs_4_ = bf16[512,2048]{1,0:T(8,128)(2,1)} collective-permute-done((bf16[512,2048]{1,0:T(8,128)(2,1)}, bf16[512,2048]{1,0:T(8,128)(2,1)}, u32[]{:S(2)}, u32[]{:S(2)}) %collective-permute-start.4) | collective-permute-done | bytes 2097184 | tf_op jit(solution)/shard_map/ppermute | solution.py:296
  188.5 1.3 collective-permute-start.11
  190.2 3.9 %collective-permute-done.6.refs_2_ = bf16[512,2048]{1,0:T(8,128)(2,1)S(1)} collective-permute-done((bf16[512,2048]{1,0:T(8,128)(2,1)}, bf16[512,2048]{1,0:T(8,128)(2,1)S(1)}, u32[]{:S(2)}, u32[]{:S(2)}) %collective-permute-start.6) | collective-permute-done | bytes 2097184 | tf_op jit(solution)/shard_map/ppermute | solution.py:296
  194.1 1.3 copy-done.8
  195.4 1.6 copy-done.9
  197.0 8.5 %back_project.4.refs_6_ = f32[512,1536]{1,0:T(8,128)} custom-call(s32[1]{0:T(128)} %bitcast.3.shards_ref, bf16[1536,8192]{1,0:T(8,128)(2,1)} %refs_1_.11, bf16[512,2048]{1,0:T(8,128)(2,1)} %collective-permute-done.5.refs_1_, bf16[512,2048]{1,0:T(8,128)(2,1)S(1)} %copy-done.9, f32[512,1536]{1,0:T(8,128)} %copy-done.3), custom_call_target="tpu_custom_call" | custom-call | flops 1 | bytes 1 | tf_op jit(solution)/shard_map/back_project/pallas_call | solution.py:263
  205.5 4.7 %all-gather.2.cloned.1.call-done.refs_0_.refs_1_.refs_2_.refs_3_ = bf16[16,128,3072]{2,1,0:T(8,128)(2,1)} async-done(((bf16[2,128,3072]{2,1,0:T(8,128)(2,1)}), bf16[16,128,3072]{2,1,0:T(8,128)(2,1)}) %all-gather.2.cloned.1.call-update) | async-done | bytes 12582928 | tf_op jit(solution)/shard_map/all_gather | solution.py:460
  210.2 9.4 %attend.1.refs_0_ = bf16[512,1536]{1,0:T(8,128)(2,1)S(1)} custom-call(s32[16]{0:T(128)S(1)} %multiply_add_fusion.ids_ref, bf16[512,1536]{1,0:T(8,128)(2,1)S(1)} %copy-done, bf16[16,128,3072]{2,1,0:T(8,128)(2,1)} %all-gather.2.cloned.1.call-done.refs_0_.refs_1_.refs_2_.refs_3_, ...), custom_call_target="tpu_custom_call" | custom-call | flops 1 | bytes 1 | tf_op jit(solution)/shard_map/attend/pallas_call | solution.py:82
  219.6 6.9 %project.4.refs_0_ = bf16[512,2048]{1,0:T(8,128)(2,1)} custom-call(s32[1]{0:T(128)} %bitcast.shard_ref, bf16[512,1536]{1,0:T(8,128)(2,1)S(1)} %attend.1.refs_0_, bf16[1536,8192]{1,0:T(8,128)(2,1)} %refs_1_.11), custom_call_target="tpu_custom_call" | custom-call | flops 1 | bytes 1 | tf_op jit(solution)/shard_map/project/pallas_call | solution.py:221
  226.5 4.8 %collective-permute-start.9 = (bf16[512,2048]{1,0:T(8,128)(2,1)}, bf16[512,2048]{1,0:T(8,128)(2,1)}, u32[]{:S(2)}, u32[]{:S(2)}) collective-permute-start(bf16[512,2048]{1,0:T(8,128)(2,1)} %project.4.refs_0_), channel_id=1, source_target_pairs={{0,1},{3,2},{4,5},{7,6},{8,9},{11,10},{12,13},{15,14},{16,17},{19,... | collective-permute-start | bytes 6291464 | tf_op jit(solution)/shard_map/ppermute | solution.py:296
  231.2 6.0 %project.5.refs_0_ = bf16[512,2048]{1,0:T(8,128)(2,1)S(1)} custom-call(s32[1]{0:T(128)} %bitcast.8.shard_ref, bf16[512,1536]{1,0:T(8,128)(2,1)S(1)} %attend.1.refs_0_, bf16[1536,8192]{1,0:T(8,128)(2,1)} %refs_1_.11), custom_call_target="tpu_custom_call" | custom-call | flops 1 | bytes 1 | tf_op jit(solution)/shard_map/project/pallas_call | solution.py:221
  237.2 1.3 copy-done.4
  238.6 13.5 %back_project.5.g_ref = bf16[512,1536]{1,0:T(8,128)(2,1)S(1)} custom-call(s32[2]{0:T(128)S(1)} %pad_add_fusion.shards_ref, bf16[1536,8192]{1,0:T(8,128)(2,1)} %refs_1_.11, bf16[1536,8192]{1,0:T(8,128)(2,1)} %refs_1_.11, bf16[512,2048]{1,0:T(8,128)(2,1)} %collective-permute-done.10.refs_2_, bf16[512,2048]{1,0:T(8,128)(2,1)} %collective-permute-done.2.refs_3_, ...), custom_call_target="tpu_custom_call" | custom-call | flops 1 | bytes 1 | tf_op jit(solution)/shard_map/back_project/pallas_call | solution.py:263
  252.1 11.1 %attend_grad.2 = bf16[8,128,1536]{2,1,0:T(8,128)(2,1)} custom-call(s32[16]{0:T(128)S(1)} %multiply_add_fusion.ids_ref, s32[16]{0:T(128)S(1)} %reshape.36.own_ref, bf16[512,1536]{1,0:T(8,128)(2,1)S(1)} %copy-done, bf16[512,1536]{1,0:T(8,128)(2,1)S(1)} %back_project.5.g_ref, ...), custom_call_target="tpu_custom_call" | custom-call | flops 1 | bytes 1 | tf_op jit(solution)/shard_map/attend_grad/pallas_call | solution.py:178
  263.2 1.1 copy-done.1
  264.3 4.5 %all-to-all-start = ((bf16[8,128,1536]{2,1,0:T(8,128)(2,1)}), bf16[8,128,1536]{2,1,0:T(8,128)(2,1)}, u32[]{:S(2)}, u32[]{:S(2)}) async-start(bf16[8,128,1536]{2,1,0:T(8,128)(2,1)} %attend_grad.2), calls=%async_computation | async-start | bytes 6291456 | tf_op jit(solution)/shard_map/all_to_all | solution.py:499
  268.8 2.8 collective-permute-start.12
  271.5 4.7 %collective-permute-done.9.refs_1_ = bf16[512,2048]{1,0:T(8,128)(2,1)} collective-permute-done((bf16[512,2048]{1,0:T(8,128)(2,1)}, bf16[512,2048]{1,0:T(8,128)(2,1)}, u32[]{:S(2)}, u32[]{:S(2)}) %collective-permute-start.9) | collective-permute-done | bytes 2097184 | tf_op jit(solution)/shard_map/ppermute | solution.py:296
  276.2 3.4 sum_of.10
  279.6 1.3 collective-permute-start.14
  280.9 11.0 %attend_grad.3 = bf16[8,128,1536]{2,1,0:T(8,128)(2,1)} custom-call(s32[16]{0:T(128)S(1)} %multiply_add_fusion.ids_ref, s32[16]{0:T(128)S(1)} %reshape.36.own_ref, bf16[512,1536]{1,0:T(8,128)(2,1)S(1)} %copy-done, bf16[512,1536]{1,0:T(8,128)(2,1)S(1)} %copy-done.2, bf16[16,128,3072]{2,1,0:T(8,128)(2,1)} %all-gather.2.cloned.1.call-done.refs_0_.refs_1_.refs_2_.refs_3_, ...), custom_call_target="tpu_custom_call" | custom-call | flops 1 | bytes 1 | tf_op jit(solution)/shard_map/attend_grad/pallas_call | solution.py:178
  292.0 6.0 %project.6 = bf16[512,2048]{1,0:T(8,128)(2,1)S(1)} custom-call(s32[1]{0:T(128)} %bitcast.10.shard_ref, bf16[512,1536]{1,0:T(8,128)(2,1)S(1)} %attend.1.refs_0_, bf16[1536,8192]{1,0:T(8,128)(2,1)} %refs_1_.11), custom_call_target="tpu_custom_call" | custom-call | flops 1 | bytes 1 | tf_op jit(solution)/shard_map/project/pallas_call | solution.py:221
  298.0 1.4 copy-done.10
  299.3 6.0 %project.7.refs_0_ = bf16[512,2048]{1,0:T(8,128)(2,1)S(1)} custom-call(s32[1]{0:T(128)} %bitcast.11.shard_ref, bf16[512,1536]{1,0:T(8,128)(2,1)S(1)} %attend.1.refs_0_, bf16[1536,8192]{1,0:T(8,128)(2,1)} %refs_1_.11), custom_call_target="tpu_custom_call" | custom-call | flops 1 | bytes 1 | tf_op jit(solution)/shard_map/project/pallas_call | solution.py:221
  305.3 1.3 copy-done.6
  306.7 4.6 %all-to-all-start.1 = ((bf16[8,128,1536]{2,1,0:T(8,128)(2,1)}), bf16[8,128,1536]{2,1,0:T(8,128)(2,1)S(1)}, u32[]{:S(2)}, u32[]{:S(2)}) async-start(bf16[8,128,1536]{2,1,0:T(8,128)(2,1)} %attend_grad.3), calls=%async_computation.1 | async-start | bytes 6291456 | tf_op jit(solution)/shard_map/all_to_all | solution.py:499
  311.3 9.0 %collective-permute-done.12.refs_1_ = bf16[512,2048]{1,0:T(8,128)(2,1)} collective-permute-done((bf16[512,2048]{1,0:T(8,128)(2,1)}, bf16[512,2048]{1,0:T(8,128)(2,1)}, u32[]{:S(2)}, u32[]{:S(2)}) %collective-permute-start.12) | collective-permute-done | bytes 2097184 | tf_op jit(solution)/shard_map/ppermute | solution.py:296
  320.3 2.5 collective-permute-start.13
  322.8 5.9 %collective-permute-done.14.refs_2_ = bf16[512,2048]{1,0:T(8,128)(2,1)} collective-permute-done((bf16[512,2048]{1,0:T(8,128)(2,1)}, bf16[512,2048]{1,0:T(8,128)(2,1)}, u32[]{:S(2)}, u32[]{:S(2)}) %collective-permute-start.14) | collective-permute-done | bytes 2097184 | tf_op jit(solution)/shard_map/ppermute | solution.py:296
  328.7 1.6 copy-done.5
  330.3 2.8 sum_of.12
  333.1 2.0 collective-permute-start.15
  335.1 0.1 copy.27
  335.2 0.1 copy.26
  335.5 0.2 select_reduce_fusion
  335.7 0.2 dynamic-slice_reduce_fusion.slot_ref
  335.9 13.3 %all-to-all-done.1.refs_1_ = bf16[8,128,1536]{2,1,0:T(8,128)(2,1)S(1)} async-done(((bf16[8,128,1536]{2,1,0:T(8,128)(2,1)}), bf16[8,128,1536]{2,1,0:T(8,128)(2,1)S(1)}, u32[]{:S(2)}, u32[]{:S(2)}) %all-to-all-start.1) | async-done | bytes 3145760 | tf_op jit(solution)/shard_map/all_to_all | solution.py:499
  349.2 5.5 %settle.1 = bf16[256,3072]{1,0:T(8,128)(2,1)} custom-call(s32[8]{0:T(128)S(1)} %dynamic-slice_reduce_fusion.slot_ref, bf16[8,128,1536]{2,1,0:T(8,128)(2,1)} %all-to-all-done.refs_0_, bf16[8,128,1536]{2,1,0:T(8,128)(2,1)S(1)} %all-to-all-done.1.refs_1_), custom_call_target="tpu_custom_call" | custom-call | flops 1 | bytes 1 | tf_op jit(solution)/shard_map/settle/pallas_call | solution.py:389
  354.7 18.9 %collective-permute-done.13.refs_1_ = bf16[512,2048]{1,0:T(8,128)(2,1)} collective-permute-done((bf16[512,2048]{1,0:T(8,128)(2,1)}, bf16[512,2048]{1,0:T(8,128)(2,1)}, u32[]{:S(2)}, u32[]{:S(2)}) %collective-permute-start.13) | collective-permute-done | bytes 2097184 | tf_op jit(solution)/shard_map/ppermute | solution.py:296
  373.6 2.6 sum_of.11.refs_0_
  376.1 2.8 sum_of.13
  (35 shorter events, 0.8 us)
Async XLA Ops:
  7.2 203.0 %all-gather.2.cloned.1.call-start = ((), (), s32[]{:S(2)}) async-start(), calls=%async_computation.2 | async-start | bytes 14155776 | tf_op jit(solution)/shard_map/all_gather | solution.py:460
  7.2 50.2 %collective-permute-start.2 = (bf16[512,2048]{1,0:T(8,128)(2,1)}, bf16[512,2048]{1,0:T(8,128)(2,1)}, u32[]{:S(2)}, u32[]{:S(2)}) collective-permute-start(bf16[512,2048]{1,0:T(8,128)(2,1)} %refs_1_.6), channel_id=1, source_target_pairs={{1,0},{2,3},{5,4},{6,7},{9,8},{10,11},{13,12},{14,15},{17,16},{18,... | collective-permute-start | bytes 6291464 | tf_op jit(solution)/shard_map/ppermute | solution.py:296
  10.0 41.0 %collective-permute-start.1 = (bf16[256,3072]{1,0:T(8,128)(2,1)S(1)}, bf16[256,3072]{1,0:T(8,128)(2,1)}, u32[]{:S(2)}, u32[]{:S(2)}) collective-permute-start(bf16[256,3072]{1,0:T(8,128)(2,1)S(1)} %dynamic-slice_bitcast_fusion.3.refs_0_), channel_id=1, source_target_pairs={{0,1},{3,2},{4,5},{7,6},{8,9},{11,10},{12,13},{15,14},{16,17},{19,... | collective-permute-start | bytes 4718600 | tf_op jit(solution)/shard_map/ppermute | solution.py:296
  17.5 43.7 %collective-permute-start.5 = (bf16[512,2048]{1,0:T(8,128)(2,1)}, bf16[512,2048]{1,0:T(8,128)(2,1)}, u32[]{:S(2)}, u32[]{:S(2)}) collective-permute-start(bf16[512,2048]{1,0:T(8,128)(2,1)} %refs_1_.6), channel_id=1, source_target_pairs={{1,2},{2,1},{5,6},{6,5},{9,10},{10,9},{13,14},{14,13},{17,18},{18,... | collective-permute-start | bytes 6291464 | tf_op jit(solution)/shard_map/ppermute | solution.py:296
  21.0 63.8 %collective-permute-start = (bf16[256,3072]{1,0:T(8,128)(2,1)S(1)}, bf16[256,3072]{1,0:T(8,128)(2,1)}, u32[]{:S(2)}, u32[]{:S(2)}) collective-permute-start(bf16[256,3072]{1,0:T(8,128)(2,1)S(1)} %dynamic-slice_bitcast_fusion.2.refs_0_), channel_id=1, source_target_pairs={{0,1},{3,2},{4,5},{7,6},{8,9},{11,10},{12,13},{15,14},{16,17},{19,... | collective-permute-start | bytes 4718600 | tf_op jit(solution)/shard_map/ppermute | solution.py:296
  59.9 40.2 %collective-permute-start.3 = (bf16[256,3072]{1,0:T(8,128)(2,1)}, bf16[256,3072]{1,0:T(8,128)(2,1)S(1)}, u32[]{:S(2)}, u32[]{:S(2)}) collective-permute-start(bf16[256,3072]{1,0:T(8,128)(2,1)} %sum_of.7), channel_id=1, source_target_pairs={{1,3},{2,0},{5,7},{6,4},{9,11},{10,8},{13,15},{14,12},{17,19},{18,... | collective-permute-start | bytes 4718600 | tf_op jit(solution)/shard_map/ppermute | solution.py:296
  63.3 70.4 %collective-permute-start.7 = (bf16[256,3072]{1,0:T(8,128)(2,1)S(1)}, bf16[256,3072]{1,0:T(8,128)(2,1)S(1)}, u32[]{:S(2)}, u32[]{:S(2)}) collective-permute-start(bf16[256,3072]{1,0:T(8,128)(2,1)S(1)} %get-tuple-element.44), channel_id=1, source_target_pairs={{0,1},{1,0},{2,3},{3,2},{4,5},{5,4},{6,7},{7,6},{8,9},{9,8},{10,11... | collective-permute-start | bytes 4718600 | tf_op jit(solution)/shard_map/ppermute | solution.py:296
  101.7 32.0 %collective-permute-start.8 = (bf16[256,3072]{1,0:T(8,128)(2,1)S(1)}, bf16[256,3072]{1,0:T(8,128)(2,1)S(1)}, u32[]{:S(2)}, u32[]{:S(2)}) collective-permute-start(bf16[256,3072]{1,0:T(8,128)(2,1)S(1)} %sum_of.8), channel_id=1, source_target_pairs={{1,2},{2,1},{5,6},{6,5},{9,10},{10,9},{13,14},{14,13},{17,18},{18,... | collective-permute-start | bytes 4718600 | tf_op jit(solution)/shard_map/ppermute | solution.py:296
  135.4 53.0 %collective-permute-start.4 = (bf16[512,2048]{1,0:T(8,128)(2,1)}, bf16[512,2048]{1,0:T(8,128)(2,1)}, u32[]{:S(2)}, u32[]{:S(2)}) collective-permute-start(bf16[512,2048]{1,0:T(8,128)(2,1)} %refs_1_.6), channel_id=1, source_target_pairs={{3,1},{0,2},{7,5},{4,6},{11,9},{8,10},{15,13},{12,14},{19,17},{16,... | collective-permute-start | bytes 6291464 | tf_op jit(solution)/shard_map/ppermute | solution.py:296
  143.4 50.7 %collective-permute-start.6 = (bf16[512,2048]{1,0:T(8,128)(2,1)}, bf16[512,2048]{1,0:T(8,128)(2,1)S(1)}, u32[]{:S(2)}, u32[]{:S(2)}) collective-permute-start(bf16[512,2048]{1,0:T(8,128)(2,1)} %collective-permute-done.5.refs_1_), channel_id=1, source_target_pairs={{1,0},{2,3},{5,4},{6,7},{9,8},{10,11},{13,12},{14,15},{17,16},{18,... | collective-permute-start | bytes 6291464 | tf_op jit(solution)/shard_map/ppermute | solution.py:296
  144.7 45.1 %copy-start.11 = (s32[64,2]{0,1:T(2,128)S(1)}, s32[64,2]{0,1:T(2,128)}, u32[]{:S(2)}) copy-start(s32[64,2]{0,1:T(2,128)} %param.11) | copy-start | bytes 1540
  144.7 45.1 %copy-start.12 = (s32[64,2]{0,1:T(2,128)S(1)}, s32[64,2]{0,1:T(2,128)}, u32[]{:S(2)}) copy-start(s32[64,2]{0,1:T(2,128)} %param.10) | copy-start | bytes 1540
  151.9 1.7 copy-start.3
  153.6 85.0 %collective-permute-start.10 = (bf16[512,2048]{1,0:T(8,128)(2,1)}, bf16[512,2048]{1,0:T(8,128)(2,1)}, u32[]{:S(2)}, u32[]{:S(2)}) collective-permute-start(bf16[512,2048]{1,0:T(8,128)(2,1)} %refs_1_.6), channel_id=1, source_target_pairs={{0,1},{3,2},{4,5},{7,6},{8,9},{11,10},{12,13},{15,14},{16,17},{19,... | collective-permute-start | bytes 6291464 | tf_op jit(solution)/shard_map/ppermute | solution.py:296
  188.5 50.1 %collective-permute-start.11 = (bf16[512,2048]{1,0:T(8,128)(2,1)}, bf16[512,2048]{1,0:T(8,128)(2,1)}, u32[]{:S(2)}, u32[]{:S(2)}) collective-permute-start(bf16[512,2048]{1,0:T(8,128)(2,1)} %collective-permute-done.4.refs_4_), channel_id=1, source_target_pairs={{1,0},{2,3},{5,4},{6,7},{9,8},{10,11},{13,12},{14,15},{17,16},{18,... | collective-permute-start | bytes 6291464 | tf_op jit(solution)/shard_map/ppermute | solution.py:296
  194.0 1.3 copy-start.8
  195.4 1.6 copy-start.9
  197.0 13.2 %copy-start = (bf16[512,1536]{1,0:T(8,128)(2,1)S(1)}, bf16[512,1536]{1,0:T(8,128)(2,1)}, u32[]{:S(2)}) copy-start(bf16[512,1536]{1,0:T(8,128)(2,1)} %q_ref.5) | copy-start | bytes 4718596
  226.5 49.8 %collective-permute-start.9 = (bf16[512,2048]{1,0:T(8,128)(2,1)}, bf16[512,2048]{1,0:T(8,128)(2,1)}, u32[]{:S(2)}, u32[]{:S(2)}) collective-permute-start(bf16[512,2048]{1,0:T(8,128)(2,1)} %project.4.refs_0_), channel_id=1, source_target_pairs={{0,1},{3,2},{4,5},{7,6},{8,9},{11,10},{12,13},{15,14},{16,17},{19,... | collective-permute-start | bytes 6291464 | tf_op jit(solution)/shard_map/ppermute | solution.py:296
  237.2 1.3 copy-start.4
  263.2 1.1 copy-start.1
  264.3 42.4 %all-to-all-start = ((bf16[8,128,1536]{2,1,0:T(8,128)(2,1)}), bf16[8,128,1536]{2,1,0:T(8,128)(2,1)}, u32[]{:S(2)}, u32[]{:S(2)}) async-start(bf16[8,128,1536]{2,1,0:T(8,128)(2,1)} %attend_grad.2), calls=%async_computation | async-start | bytes 6291456 | tf_op jit(solution)/shard_map/all_to_all | solution.py:499
  268.8 12.1 %copy-start.2 = (bf16[512,1536]{1,0:T(8,128)(2,1)S(1)}, bf16[512,1536]{1,0:T(8,128)(2,1)}, u32[]{:S(2)}) copy-start(bf16[512,1536]{1,0:T(8,128)(2,1)} %copy-done.1) | copy-start | bytes 4718596
  268.8 51.5 %collective-permute-start.12 = (bf16[512,2048]{1,0:T(8,128)(2,1)}, bf16[512,2048]{1,0:T(8,128)(2,1)}, u32[]{:S(2)}, u32[]{:S(2)}) collective-permute-start(bf16[512,2048]{1,0:T(8,128)(2,1)} %copy-done.4), channel_id=1, source_target_pairs={{0,1},{3,2},{4,5},{7,6},{8,9},{11,10},{12,13},{15,14},{16,17},{19,... | collective-permute-start | bytes 6291464 | tf_op jit(solution)/shard_map/ppermute | solution.py:296
  279.6 49.1 %collective-permute-start.14 = (bf16[512,2048]{1,0:T(8,128)(2,1)}, bf16[512,2048]{1,0:T(8,128)(2,1)}, u32[]{:S(2)}, u32[]{:S(2)}) collective-permute-start(bf16[512,2048]{1,0:T(8,128)(2,1)} %sum_of.10), channel_id=1, source_target_pairs={{1,3},{2,0},{5,7},{6,4},{9,11},{10,8},{13,15},{14,12},{17,19},{18,... | collective-permute-start | bytes 6291464 | tf_op jit(solution)/shard_map/ppermute | solution.py:296
  297.9 1.4 copy-start.10
  305.3 1.3 copy-start.6
  306.7 42.5 %all-to-all-start.1 = ((bf16[8,128,1536]{2,1,0:T(8,128)(2,1)}), bf16[8,128,1536]{2,1,0:T(8,128)(2,1)S(1)}, u32[]{:S(2)}, u32[]{:S(2)}) async-start(bf16[8,128,1536]{2,1,0:T(8,128)(2,1)} %attend_grad.3), calls=%async_computation.1 | async-start | bytes 6291456 | tf_op jit(solution)/shard_map/all_to_all | solution.py:499
  320.3 53.3 %collective-permute-start.13 = (bf16[512,2048]{1,0:T(8,128)(2,1)}, bf16[512,2048]{1,0:T(8,128)(2,1)}, u32[]{:S(2)}, u32[]{:S(2)}) collective-permute-start(bf16[512,2048]{1,0:T(8,128)(2,1)} %copy-done.10), channel_id=1, source_target_pairs={{0,1},{1,0},{2,3},{3,2},{4,5},{5,4},{6,7},{7,6},{8,9},{9,8},{10,11... | collective-permute-start | bytes 6291464 | tf_op jit(solution)/shard_map/ppermute | solution.py:296
  328.7 1.6 copy-start.5
  333.1 43.0 %collective-permute-start.15 = (bf16[512,2048]{1,0:T(8,128)(2,1)}, bf16[512,2048]{1,0:T(8,128)(2,1)}, u32[]{:S(2)}, u32[]{:S(2)}) collective-permute-start(bf16[512,2048]{1,0:T(8,128)(2,1)} %sum_of.12), channel_id=1, source_target_pairs={{1,2},{2,1},{5,6},{6,5},{9,10},{10,9},{13,14},{14,13},{17,18},{18,... | collective-permute-start | bytes 6291464 | tf_op jit(solution)/shard_map/ppermute | solution.py:296
  349.2 24.4 %copy-start.7 = (bf16[512,2048]{1,0:T(8,128)(2,1)S(1)}, bf16[512,2048]{1,0:T(8,128)(2,1)}, u32[]{:S(2)}) copy-start(bf16[512,2048]{1,0:T(8,128)(2,1)} %copy-done.6) | copy-start | bytes 6291460
Sparse Core Ops, SparseCore 0:
  135.6 74.5 all-gather.1

commit v6 on v5

--- a/solution.py
+++ b/solution.py
@@ -195,7 +195,7 @@
 
 
 def tile_of(width):
-    return next(tile for tile in (512, 384, 256, HD) if width % tile == 0)
+    return next(tile for tile in (1024, 768, 512, 384, 256, HD) if width % tile == 0)
 
 
 def project_kernel(parts, received, shard_ref, *refs):

time: 388 us -> 389 us (level)
  transfers between devices with their start and end apart: 19 -> 19, of which waited for: 14 -> 14; matrix products, arithmetic and copies ran while one was open for 2% -> 2% of each run, Pallas kernels for 27% -> 26%
where the time goes in v6:
time: 389 us; the launch traced here: 386 us
  waiting for transfers between devices  184 us (47%)
  Pallas kernels  107 us (28%)
  starting transfers between devices  63.5 us (16%)
  local copies, waits for them, and re-layouts  17.4 us (4%)
  between operations  14.3 us (4%)
    ppermute x16, waiting for transfers between devices, send(): return lax.ppermute(x, 'tensor', hops)  166 us
    ppermute x16, starting transfers between devices, send(): return lax.ppermute(x, 'tensor', hops)  54.4 us
    pallas_call x3, Pallas kernels, back_project(): pl.pallas_call(functools.partial(back_project_kernel, [len(sources) for _...  29.5 us
    pallas_call x4, Pallas kernels, project(): pl.pallas_call(functools.partial(project_kernel, parts, len(received)), g...  23.3 us
    pallas_call x2, Pallas kernels, attend_grad(): pl.pallas_call(functools.partial(attend_grad_kernel, group), grid_spec=pl...  22.1 us
    pallas_call x7, Pallas kernels, sum_of(): pl.pallas_call(sum_kernel, grid=(steps,), in_specs=[block] * len(arrays),...  17.3 us
    all_to_all x2, waiting for transfers between devices, local(): lax.all_to_all(part, 'dp', split_axis=0, concat_axis=0, tiled=True)  13 us
    unnamed x28, local copies, waits for them, and re-layouts  11.5 us
  transfers between devices with their start and end apart: 19, of which 14 were waited for; matrix products, arithmetic and copies ran while one was open for 2% of the time, Pallas kernels for 26%

profile of v6, /device:TPU:0, one launch (start us, length us, event | category | flops | bytes accessed | tf_op | source)
XLA Modules:
  0.0 386.5 jit_solution(17252912505351304179)
XLA Ops:
  7.2 1.3 collective-permute-start.2
  8.5 1.5 dynamic-slice_bitcast_fusion.3.refs_0_
  10.0 7.4 %collective-permute-start.1 = (bf16[256,3072]{1,0:T(8,128)(2,1)S(1)}, bf16[256,3072]{1,0:T(8,128)(2,1)}, u32[]{:S(2)}, u32[]{:S(2)}) collective-permute-start(bf16[256,3072]{1,0:T(8,128)(2,1)S(1)} %dynamic-slice_bitcast_fusion.3.refs_0_), channel_id=1, source_target_pairs={{0,1},{3,2},{4,5},{7,6},{8,9},{11,10},{12,13},{15,14},{16,17},{19,... | collective-permute-start | bytes 4718600 | tf_op jit(solution)/shard_map/ppermute | solution.py:296
  17.5 2.0 collective-permute-start.5
  19.5 1.5 dynamic-slice_bitcast_fusion.2.refs_0_
  21.0 4.9 %collective-permute-start = (bf16[256,3072]{1,0:T(8,128)(2,1)S(1)}, bf16[256,3072]{1,0:T(8,128)(2,1)}, u32[]{:S(2)}, u32[]{:S(2)}) collective-permute-start(bf16[256,3072]{1,0:T(8,128)(2,1)S(1)} %dynamic-slice_bitcast_fusion.2.refs_0_), channel_id=1, source_target_pairs={{0,1},{3,2},{4,5},{7,6},{8,9},{11,10},{12,13},{15,14},{16,17},{19,... | collective-permute-start | bytes 4718600 | tf_op jit(solution)/shard_map/ppermute | solution.py:296
  25.9 25.1 %collective-permute-done.1.refs_1_ = bf16[256,3072]{1,0:T(8,128)(2,1)} collective-permute-done((bf16[256,3072]{1,0:T(8,128)(2,1)S(1)}, bf16[256,3072]{1,0:T(8,128)(2,1)}, u32[]{:S(2)}, u32[]{:S(2)}) %collective-permute-start.1) | collective-permute-done | bytes 1572896 | tf_op jit(solution)/shard_map/ppermute | solution.py:296
  51.1 6.4 %collective-permute-done.2.refs_3_ = bf16[512,2048]{1,0:T(8,128)(2,1)} collective-permute-done((bf16[512,2048]{1,0:T(8,128)(2,1)}, bf16[512,2048]{1,0:T(8,128)(2,1)}, u32[]{:S(2)}, u32[]{:S(2)}) %collective-permute-start.2) | collective-permute-done | bytes 2097184 | tf_op jit(solution)/shard_map/ppermute | solution.py:296
  57.5 2.5 sum_of.7
  59.9 1.3 collective-permute-start.3
  61.2 2.1 dynamic-slice_bitcast_fusion
  63.3 7.0 %collective-permute-start.7 = (bf16[256,3072]{1,0:T(8,128)(2,1)S(1)}, bf16[256,3072]{1,0:T(8,128)(2,1)S(1)}, u32[]{:S(2)}, u32[]{:S(2)}) collective-permute-start(bf16[256,3072]{1,0:T(8,128)(2,1)S(1)} %get-tuple-element.44), channel_id=1, source_target_pairs={{0,1},{1,0},{2,3},{3,2},{4,5},{5,4},{6,7},{7,6},{8,9},{9,8},{10,11... | collective-permute-start | bytes 4718600 | tf_op jit(solution)/shard_map/ppermute | solution.py:296
  70.3 14.5 %collective-permute-done.refs_1_ = bf16[256,3072]{1,0:T(8,128)(2,1)} collective-permute-done((bf16[256,3072]{1,0:T(8,128)(2,1)S(1)}, bf16[256,3072]{1,0:T(8,128)(2,1)}, u32[]{:S(2)}, u32[]{:S(2)}) %collective-permute-start) | collective-permute-done | bytes 1572896 | tf_op jit(solution)/shard_map/ppermute | solution.py:296
  84.8 15.4 %collective-permute-done.3.refs_2_ = bf16[256,3072]{1,0:T(8,128)(2,1)S(1)} collective-permute-done((bf16[256,3072]{1,0:T(8,128)(2,1)}, bf16[256,3072]{1,0:T(8,128)(2,1)S(1)}, u32[]{:S(2)}, u32[]{:S(2)}) %collective-permute-start.3) | collective-permute-done | bytes 1572896 | tf_op jit(solution)/shard_map/ppermute | solution.py:296
  100.1 1.6 sum_of.8
  101.7 0.8 collective-permute-start.8
  102.5 31.3 %collective-permute-done.7.refs_1_ = bf16[256,3072]{1,0:T(8,128)(2,1)S(1)} collective-permute-done((bf16[256,3072]{1,0:T(8,128)(2,1)S(1)}, bf16[256,3072]{1,0:T(8,128)(2,1)S(1)}, u32[]{:S(2)}, u32[]{:S(2)}) %collective-permute-start.7) | collective-permute-done | bytes 1572896 | tf_op jit(solution)/shard_map/ppermute | solution.py:296
  133.8 1.7 sum_of.9
  135.4 8.0 %collective-permute-start.4 = (bf16[512,2048]{1,0:T(8,128)(2,1)}, bf16[512,2048]{1,0:T(8,128)(2,1)}, u32[]{:S(2)}, u32[]{:S(2)}) collective-permute-start(bf16[512,2048]{1,0:T(8,128)(2,1)} %refs_1_.6), channel_id=1, source_target_pairs={{3,1},{0,2},{7,5},{4,6},{11,9},{8,10},{15,13},{12,14},{19,17},{16,... | collective-permute-start | bytes 6291464 | tf_op jit(solution)/shard_map/ppermute | solution.py:296
  143.4 1.3 collective-permute-start.6
  144.7 7.2 %back_project.3.refs_3_ = f32[512,1536]{1,0:T(8,128)S(1)} custom-call(s32[1]{0:T(128)} %bitcast.6.shards_ref, bf16[1536,8192]{1,0:T(8,128)(2,1)} %refs_1_.11, bf16[512,2048]{1,0:T(8,128)(2,1)} %refs_1_.6), custom_call_target="tpu_custom_call" | custom-call | flops 1 | bytes 1 | tf_op jit(solution)/shard_map/back_project/pallas_call | solution.py:263
  151.9 1.7 copy-done.3
  153.5 6.0 %collective-permute-start.10 = (bf16[512,2048]{1,0:T(8,128)(2,1)}, bf16[512,2048]{1,0:T(8,128)(2,1)}, u32[]{:S(2)}, u32[]{:S(2)}) collective-permute-start(bf16[512,2048]{1,0:T(8,128)(2,1)} %refs_1_.6), channel_id=1, source_target_pairs={{0,1},{3,2},{4,5},{7,6},{8,9},{11,10},{12,13},{15,14},{16,17},{19,... | collective-permute-start | bytes 6291464 | tf_op jit(solution)/shard_map/ppermute | solution.py:296
  159.5 28.9 %collective-permute-done.4.refs_4_ = bf16[512,2048]{1,0:T(8,128)(2,1)} collective-permute-done((bf16[512,2048]{1,0:T(8,128)(2,1)}, bf16[512,2048]{1,0:T(8,128)(2,1)}, u32[]{:S(2)}, u32[]{:S(2)}) %collective-permute-start.4) | collective-permute-done | bytes 2097184 | tf_op jit(solution)/shard_map/ppermute | solution.py:296
  188.5 1.3 collective-permute-start.11
  190.2 3.9 %collective-permute-done.6.refs_2_ = bf16[512,2048]{1,0:T(8,128)(2,1)S(1)} collective-permute-done((bf16[512,2048]{1,0:T(8,128)(2,1)}, bf16[512,2048]{1,0:T(8,128)(2,1)S(1)}, u32[]{:S(2)}, u32[]{:S(2)}) %collective-permute-start.6) | collective-permute-done | bytes 2097184 | tf_op jit(solution)/shard_map/ppermute | solution.py:296
  194.1 1.3 copy-done.8
  195.4 1.6 copy-done.9
  197.0 8.0 %back_project.4.refs_6_ = f32[512,1536]{1,0:T(8,128)} custom-call(s32[1]{0:T(128)} %bitcast.3.shards_ref, bf16[1536,8192]{1,0:T(8,128)(2,1)} %refs_1_.11, bf16[512,2048]{1,0:T(8,128)(2,1)} %collective-permute-done.5.refs_1_, bf16[512,2048]{1,0:T(8,128)(2,1)S(1)} %copy-done.9, f32[512,1536]{1,0:T(8,128)} %copy-done.3), custom_call_target="tpu_custom_call" | custom-call | flops 1 | bytes 1 | tf_op jit(solution)/shard_map/back_project/pallas_call | solution.py:263
  205.0 5.2 %all-gather.2.cloned.1.call-done.refs_0_.refs_1_.refs_2_.refs_3_ = bf16[16,128,3072]{2,1,0:T(8,128)(2,1)} async-done(((bf16[2,128,3072]{2,1,0:T(8,128)(2,1)}), bf16[16,128,3072]{2,1,0:T(8,128)(2,1)}) %all-gather.2.cloned.1.call-update) | async-done | bytes 12582928 | tf_op jit(solution)/shard_map/all_gather | solution.py:460
  210.2 8.9 %attend.1.refs_0_ = bf16[512,1536]{1,0:T(8,128)(2,1)S(1)} custom-call(s32[16]{0:T(128)S(1)} %multiply_add_fusion.ids_ref, bf16[512,1536]{1,0:T(8,128)(2,1)S(1)} %copy-done, bf16[16,128,3072]{2,1,0:T(8,128)(2,1)} %all-gather.2.cloned.1.call-done.refs_0_.refs_1_.refs_2_.refs_3_, ...), custom_call_target="tpu_custom_call" | custom-call | flops 1 | bytes 1 | tf_op jit(solution)/shard_map/attend/pallas_call | solution.py:82
  219.1 6.5 %project.4.refs_0_ = bf16[512,2048]{1,0:T(8,128)(2,1)} custom-call(s32[1]{0:T(128)} %bitcast.shard_ref, bf16[512,1536]{1,0:T(8,128)(2,1)S(1)} %attend.1.refs_0_, bf16[1536,8192]{1,0:T(8,128)(2,1)} %refs_1_.11), custom_call_target="tpu_custom_call" | custom-call | flops 1 | bytes 1 | tf_op jit(solution)/shard_map/project/pallas_call | solution.py:221
  225.6 4.8 %collective-permute-start.9 = (bf16[512,2048]{1,0:T(8,128)(2,1)}, bf16[512,2048]{1,0:T(8,128)(2,1)}, u32[]{:S(2)}, u32[]{:S(2)}) collective-permute-start(bf16[512,2048]{1,0:T(8,128)(2,1)} %project.4.refs_0_), channel_id=1, source_target_pairs={{0,1},{3,2},{4,5},{7,6},{8,9},{11,10},{12,13},{15,14},{16,17},{19,... | collective-permute-start | bytes 6291464 | tf_op jit(solution)/shard_map/ppermute | solution.py:296
  230.3 5.6 %project.5.refs_0_ = bf16[512,2048]{1,0:T(8,128)(2,1)S(1)} custom-call(s32[1]{0:T(128)} %bitcast.8.shard_ref, bf16[512,1536]{1,0:T(8,128)(2,1)S(1)} %attend.1.refs_0_, bf16[1536,8192]{1,0:T(8,128)(2,1)} %refs_1_.11), custom_call_target="tpu_custom_call" | custom-call | flops 1 | bytes 1 | tf_op jit(solution)/shard_map/project/pallas_call | solution.py:221
  236.0 1.3 copy-done.4
  237.4 14.3 %back_project.5.g_ref = bf16[512,1536]{1,0:T(8,128)(2,1)S(1)} custom-call(s32[2]{0:T(128)S(1)} %pad_add_fusion.shards_ref, bf16[1536,8192]{1,0:T(8,128)(2,1)} %refs_1_.11, bf16[1536,8192]{1,0:T(8,128)(2,1)} %refs_1_.11, bf16[512,2048]{1,0:T(8,128)(2,1)} %collective-permute-done.10.refs_2_, bf16[512,2048]{1,0:T(8,128)(2,1)} %collective-permute-done.2.refs_3_, ...), custom_call_target="tpu_custom_call" | custom-call | flops 1 | bytes 1 | tf_op jit(solution)/shard_map/back_project/pallas_call | solution.py:263
  251.6 11.1 %attend_grad.2 = bf16[8,128,1536]{2,1,0:T(8,128)(2,1)} custom-call(s32[16]{0:T(128)S(1)} %multiply_add_fusion.ids_ref, s32[16]{0:T(128)S(1)} %reshape.36.own_ref, bf16[512,1536]{1,0:T(8,128)(2,1)S(1)} %copy-done, bf16[512,1536]{1,0:T(8,128)(2,1)S(1)} %back_project.5.g_ref, ...), custom_call_target="tpu_custom_call" | custom-call | flops 1 | bytes 1 | tf_op jit(solution)/shard_map/attend_grad/pallas_call | solution.py:178
  262.7 1.1 copy-done.1
  263.8 4.5 %all-to-all-start = ((bf16[8,128,1536]{2,1,0:T(8,128)(2,1)}), bf16[8,128,1536]{2,1,0:T(8,128)(2,1)}, u32[]{:S(2)}, u32[]{:S(2)}) async-start(bf16[8,128,1536]{2,1,0:T(8,128)(2,1)} %attend_grad.2), calls=%async_computation | async-start | bytes 6291456 | tf_op jit(solution)/shard_map/all_to_all | solution.py:499
  268.3 2.8 collective-permute-start.12
  271.1 4.4 %collective-permute-done.9.refs_1_ = bf16[512,2048]{1,0:T(8,128)(2,1)} collective-permute-done((bf16[512,2048]{1,0:T(8,128)(2,1)}, bf16[512,2048]{1,0:T(8,128)(2,1)}, u32[]{:S(2)}, u32[]{:S(2)}) %collective-permute-start.9) | collective-permute-done | bytes 2097184 | tf_op jit(solution)/shard_map/ppermute | solution.py:296
  275.5 3.4 sum_of.10
  278.9 1.3 collective-permute-start.14
  280.2 11.1 %attend_grad.3 = bf16[8,128,1536]{2,1,0:T(8,128)(2,1)} custom-call(s32[16]{0:T(128)S(1)} %multiply_add_fusion.ids_ref, s32[16]{0:T(128)S(1)} %reshape.36.own_ref, bf16[512,1536]{1,0:T(8,128)(2,1)S(1)} %copy-done, bf16[512,1536]{1,0:T(8,128)(2,1)S(1)} %copy-done.2, bf16[16,128,3072]{2,1,0:T(8,128)(2,1)} %all-gather.2.cloned.1.call-done.refs_0_.refs_1_.refs_2_.refs_3_, ...), custom_call_target="tpu_custom_call" | custom-call | flops 1 | bytes 1 | tf_op jit(solution)/shard_map/attend_grad/pallas_call | solution.py:178
  291.3 5.6 %project.6 = bf16[512,2048]{1,0:T(8,128)(2,1)S(1)} custom-call(s32[1]{0:T(128)} %bitcast.10.shard_ref, bf16[512,1536]{1,0:T(8,128)(2,1)S(1)} %attend.1.refs_0_, bf16[1536,8192]{1,0:T(8,128)(2,1)} %refs_1_.11), custom_call_target="tpu_custom_call" | custom-call | flops 1 | bytes 1 | tf_op jit(solution)/shard_map/project/pallas_call | solution.py:221
  296.9 1.4 copy-done.10
  298.3 5.6 %project.7.refs_0_ = bf16[512,2048]{1,0:T(8,128)(2,1)S(1)} custom-call(s32[1]{0:T(128)} %bitcast.11.shard_ref, bf16[512,1536]{1,0:T(8,128)(2,1)S(1)} %attend.1.refs_0_, bf16[1536,8192]{1,0:T(8,128)(2,1)} %refs_1_.11), custom_call_target="tpu_custom_call" | custom-call | flops 1 | bytes 1 | tf_op jit(solution)/shard_map/project/pallas_call | solution.py:221
  303.9 1.3 copy-done.6
  305.2 1.0 all-to-all-done.refs_0_
  306.2 4.5 %all-to-all-start.1 = ((bf16[8,128,1536]{2,1,0:T(8,128)(2,1)}), bf16[8,128,1536]{2,1,0:T(8,128)(2,1)S(1)}, u32[]{:S(2)}, u32[]{:S(2)}) async-start(bf16[8,128,1536]{2,1,0:T(8,128)(2,1)} %attend_grad.3), calls=%async_computation.1 | async-start | bytes 6291456 | tf_op jit(solution)/shard_map/all_to_all | solution.py:499
  310.7 9.6 %collective-permute-done.12.refs_1_ = bf16[512,2048]{1,0:T(8,128)(2,1)} collective-permute-done((bf16[512,2048]{1,0:T(8,128)(2,1)}, bf16[512,2048]{1,0:T(8,128)(2,1)}, u32[]{:S(2)}, u32[]{:S(2)}) %collective-permute-start.12) | collective-permute-done | bytes 2097184 | tf_op jit(solution)/shard_map/ppermute | solution.py:296
  320.3 2.5 collective-permute-start.13
  322.8 6.6 %collective-permute-done.14.refs_2_ = bf16[512,2048]{1,0:T(8,128)(2,1)} collective-permute-done((bf16[512,2048]{1,0:T(8,128)(2,1)}, bf16[512,2048]{1,0:T(8,128)(2,1)}, u32[]{:S(2)}, u32[]{:S(2)}) %collective-permute-start.14) | collective-permute-done | bytes 2097184 | tf_op jit(solution)/shard_map/ppermute | solution.py:296
  329.4 1.6 copy-done.5
  331.0 2.8 sum_of.12
  333.8 2.0 collective-permute-start.15
  335.8 0.1 copy.27
  336.2 0.2 select_reduce_fusion
  336.4 0.2 dynamic-slice_reduce_fusion.slot_ref
  336.6 12.0 %all-to-all-done.1.refs_1_ = bf16[8,128,1536]{2,1,0:T(8,128)(2,1)S(1)} async-done(((bf16[8,128,1536]{2,1,0:T(8,128)(2,1)}), bf16[8,128,1536]{2,1,0:T(8,128)(2,1)S(1)}, u32[]{:S(2)}, u32[]{:S(2)}) %all-to-all-start.1) | async-done | bytes 3145760 | tf_op jit(solution)/shard_map/all_to_all | solution.py:499
  348.6 5.5 %settle.1 = bf16[256,3072]{1,0:T(8,128)(2,1)} custom-call(s32[8]{0:T(128)S(1)} %dynamic-slice_reduce_fusion.slot_ref, bf16[8,128,1536]{2,1,0:T(8,128)(2,1)} %all-to-all-done.refs_0_, bf16[8,128,1536]{2,1,0:T(8,128)(2,1)S(1)} %all-to-all-done.1.refs_1_), custom_call_target="tpu_custom_call" | custom-call | flops 1 | bytes 1 | tf_op jit(solution)/shard_map/settle/pallas_call | solution.py:389
  354.1 20.1 %collective-permute-done.13.refs_1_ = bf16[512,2048]{1,0:T(8,128)(2,1)} collective-permute-done((bf16[512,2048]{1,0:T(8,128)(2,1)}, bf16[512,2048]{1,0:T(8,128)(2,1)}, u32[]{:S(2)}, u32[]{:S(2)}) %collective-permute-start.13) | collective-permute-done | bytes 2097184 | tf_op jit(solution)/shard_map/ppermute | solution.py:296
  374.3 2.6 sum_of.11.refs_0_
  376.8 2.8 sum_of.13
  (35 shorter events, 0.8 us)
Async XLA Ops:
  7.2 203.0 %all-gather.2.cloned.1.call-start = ((), (), s32[]{:S(2)}) async-start(), calls=%async_computation.2 | async-start | bytes 14155776 | tf_op jit(solution)/shard_map/all_gather | solution.py:460
  7.2 50.2 %collective-permute-start.2 = (bf16[512,2048]{1,0:T(8,128)(2,1)}, bf16[512,2048]{1,0:T(8,128)(2,1)}, u32[]{:S(2)}, u32[]{:S(2)}) collective-permute-start(bf16[512,2048]{1,0:T(8,128)(2,1)} %refs_1_.6), channel_id=1, source_target_pairs={{1,0},{2,3},{5,4},{6,7},{9,8},{10,11},{13,12},{14,15},{17,16},{18,... | collective-permute-start | bytes 6291464 | tf_op jit(solution)/shard_map/ppermute | solution.py:296
  10.0 41.0 %collective-permute-start.1 = (bf16[256,3072]{1,0:T(8,128)(2,1)S(1)}, bf16[256,3072]{1,0:T(8,128)(2,1)}, u32[]{:S(2)}, u32[]{:S(2)}) collective-permute-start(bf16[256,3072]{1,0:T(8,128)(2,1)S(1)} %dynamic-slice_bitcast_fusion.3.refs_0_), channel_id=1, source_target_pairs={{0,1},{3,2},{4,5},{7,6},{8,9},{11,10},{12,13},{15,14},{16,17},{19,... | collective-permute-start | bytes 4718600 | tf_op jit(solution)/shard_map/ppermute | solution.py:296
  17.5 43.7 %collective-permute-start.5 = (bf16[512,2048]{1,0:T(8,128)(2,1)}, bf16[512,2048]{1,0:T(8,128)(2,1)}, u32[]{:S(2)}, u32[]{:S(2)}) collective-permute-start(bf16[512,2048]{1,0:T(8,128)(2,1)} %refs_1_.6), channel_id=1, source_target_pairs={{1,2},{2,1},{5,6},{6,5},{9,10},{10,9},{13,14},{14,13},{17,18},{18,... | collective-permute-start | bytes 6291464 | tf_op jit(solution)/shard_map/ppermute | solution.py:296
  21.0 63.8 %collective-permute-start = (bf16[256,3072]{1,0:T(8,128)(2,1)S(1)}, bf16[256,3072]{1,0:T(8,128)(2,1)}, u32[]{:S(2)}, u32[]{:S(2)}) collective-permute-start(bf16[256,3072]{1,0:T(8,128)(2,1)S(1)} %dynamic-slice_bitcast_fusion.2.refs_0_), channel_id=1, source_target_pairs={{0,1},{3,2},{4,5},{7,6},{8,9},{11,10},{12,13},{15,14},{16,17},{19,... | collective-permute-start | bytes 4718600 | tf_op jit(solution)/shard_map/ppermute | solution.py:296
  59.9 40.2 %collective-permute-start.3 = (bf16[256,3072]{1,0:T(8,128)(2,1)}, bf16[256,3072]{1,0:T(8,128)(2,1)S(1)}, u32[]{:S(2)}, u32[]{:S(2)}) collective-permute-start(bf16[256,3072]{1,0:T(8,128)(2,1)} %sum_of.7), channel_id=1, source_target_pairs={{1,3},{2,0},{5,7},{6,4},{9,11},{10,8},{13,15},{14,12},{17,19},{18,... | collective-permute-start | bytes 4718600 | tf_op jit(solution)/shard_map/ppermute | solution.py:296
  63.3 70.4 %collective-permute-start.7 = (bf16[256,3072]{1,0:T(8,128)(2,1)S(1)}, bf16[256,3072]{1,0:T(8,128)(2,1)S(1)}, u32[]{:S(2)}, u32[]{:S(2)}) collective-permute-start(bf16[256,3072]{1,0:T(8,128)(2,1)S(1)} %get-tuple-element.44), channel_id=1, source_target_pairs={{0,1},{1,0},{2,3},{3,2},{4,5},{5,4},{6,7},{7,6},{8,9},{9,8},{10,11... | collective-permute-start | bytes 4718600 | tf_op jit(solution)/shard_map/ppermute | solution.py:296
  101.7 32.0 %collective-permute-start.8 = (bf16[256,3072]{1,0:T(8,128)(2,1)S(1)}, bf16[256,3072]{1,0:T(8,128)(2,1)S(1)}, u32[]{:S(2)}, u32[]{:S(2)}) collective-permute-start(bf16[256,3072]{1,0:T(8,128)(2,1)S(1)} %sum_of.8), channel_id=1, source_target_pairs={{1,2},{2,1},{5,6},{6,5},{9,10},{10,9},{13,14},{14,13},{17,18},{18,... | collective-permute-start | bytes 4718600 | tf_op jit(solution)/shard_map/ppermute | solution.py:296
  135.4 53.0 %collective-permute-start.4 = (bf16[512,2048]{1,0:T(8,128)(2,1)}, bf16[512,2048]{1,0:T(8,128)(2,1)}, u32[]{:S(2)}, u32[]{:S(2)}) collective-permute-start(bf16[512,2048]{1,0:T(8,128)(2,1)} %refs_1_.6), channel_id=1, source_target_pairs={{3,1},{0,2},{7,5},{4,6},{11,9},{8,10},{15,13},{12,14},{19,17},{16,... | collective-permute-start | bytes 6291464 | tf_op jit(solution)/shard_map/ppermute | solution.py:296
  143.4 50.7 %collective-permute-start.6 = (bf16[512,2048]{1,0:T(8,128)(2,1)}, bf16[512,2048]{1,0:T(8,128)(2,1)S(1)}, u32[]{:S(2)}, u32[]{:S(2)}) collective-permute-start(bf16[512,2048]{1,0:T(8,128)(2,1)} %collective-permute-done.5.refs_1_), channel_id=1, source_target_pairs={{1,0},{2,3},{5,4},{6,7},{9,8},{10,11},{13,12},{14,15},{17,16},{18,... | collective-permute-start | bytes 6291464 | tf_op jit(solution)/shard_map/ppermute | solution.py:296
  144.7 45.1 %copy-start.11 = (s32[64,2]{0,1:T(2,128)S(1)}, s32[64,2]{0,1:T(2,128)}, u32[]{:S(2)}) copy-start(s32[64,2]{0,1:T(2,128)} %param.11) | copy-start | bytes 1540
  144.7 45.1 %copy-start.12 = (s32[64,2]{0,1:T(2,128)S(1)}, s32[64,2]{0,1:T(2,128)}, u32[]{:S(2)}) copy-start(s32[64,2]{0,1:T(2,128)} %param.10) | copy-start | bytes 1540
  151.9 1.7 copy-start.3
  153.5 83.8 %collective-permute-start.10 = (bf16[512,2048]{1,0:T(8,128)(2,1)}, bf16[512,2048]{1,0:T(8,128)(2,1)}, u32[]{:S(2)}, u32[]{:S(2)}) collective-permute-start(bf16[512,2048]{1,0:T(8,128)(2,1)} %refs_1_.6), channel_id=1, source_target_pairs={{0,1},{3,2},{4,5},{7,6},{8,9},{11,10},{12,13},{15,14},{16,17},{19,... | collective-permute-start | bytes 6291464 | tf_op jit(solution)/shard_map/ppermute | solution.py:296
  188.5 48.9 %collective-permute-start.11 = (bf16[512,2048]{1,0:T(8,128)(2,1)}, bf16[512,2048]{1,0:T(8,128)(2,1)}, u32[]{:S(2)}, u32[]{:S(2)}) collective-permute-start(bf16[512,2048]{1,0:T(8,128)(2,1)} %collective-permute-done.4.refs_4_), channel_id=1, source_target_pairs={{1,0},{2,3},{5,4},{6,7},{9,8},{10,11},{13,12},{14,15},{17,16},{18,... | collective-permute-start | bytes 6291464 | tf_op jit(solution)/shard_map/ppermute | solution.py:296
  194.0 1.3 copy-start.8
  195.4 1.6 copy-start.9
  197.0 13.2 %copy-start = (bf16[512,1536]{1,0:T(8,128)(2,1)S(1)}, bf16[512,1536]{1,0:T(8,128)(2,1)}, u32[]{:S(2)}) copy-start(bf16[512,1536]{1,0:T(8,128)(2,1)} %q_ref.5) | copy-start | bytes 4718596
  225.6 50.0 %collective-permute-start.9 = (bf16[512,2048]{1,0:T(8,128)(2,1)}, bf16[512,2048]{1,0:T(8,128)(2,1)}, u32[]{:S(2)}, u32[]{:S(2)}) collective-permute-start(bf16[512,2048]{1,0:T(8,128)(2,1)} %project.4.refs_0_), channel_id=1, source_target_pairs={{0,1},{3,2},{4,5},{7,6},{8,9},{11,10},{12,13},{15,14},{16,17},{19,... | collective-permute-start | bytes 6291464 | tf_op jit(solution)/shard_map/ppermute | solution.py:296
  236.0 1.3 copy-start.4
  262.7 1.1 copy-start.1
  263.8 42.4 %all-to-all-start = ((bf16[8,128,1536]{2,1,0:T(8,128)(2,1)}), bf16[8,128,1536]{2,1,0:T(8,128)(2,1)}, u32[]{:S(2)}, u32[]{:S(2)}) async-start(bf16[8,128,1536]{2,1,0:T(8,128)(2,1)} %attend_grad.2), calls=%async_computation | async-start | bytes 6291456 | tf_op jit(solution)/shard_map/all_to_all | solution.py:499
  268.3 11.9 %copy-start.2 = (bf16[512,1536]{1,0:T(8,128)(2,1)S(1)}, bf16[512,1536]{1,0:T(8,128)(2,1)}, u32[]{:S(2)}) copy-start(bf16[512,1536]{1,0:T(8,128)(2,1)} %copy-done.1) | copy-start | bytes 4718596
  268.3 51.9 %collective-permute-start.12 = (bf16[512,2048]{1,0:T(8,128)(2,1)}, bf16[512,2048]{1,0:T(8,128)(2,1)}, u32[]{:S(2)}, u32[]{:S(2)}) collective-permute-start(bf16[512,2048]{1,0:T(8,128)(2,1)} %copy-done.4), channel_id=1, source_target_pairs={{0,1},{3,2},{4,5},{7,6},{8,9},{11,10},{12,13},{15,14},{16,17},{19,... | collective-permute-start | bytes 6291464 | tf_op jit(solution)/shard_map/ppermute | solution.py:296
  278.9 50.5 %collective-permute-start.14 = (bf16[512,2048]{1,0:T(8,128)(2,1)}, bf16[512,2048]{1,0:T(8,128)(2,1)}, u32[]{:S(2)}, u32[]{:S(2)}) collective-permute-start(bf16[512,2048]{1,0:T(8,128)(2,1)} %sum_of.10), channel_id=1, source_target_pairs={{1,3},{2,0},{5,7},{6,4},{9,11},{10,8},{13,15},{14,12},{17,19},{18,... | collective-permute-start | bytes 6291464 | tf_op jit(solution)/shard_map/ppermute | solution.py:296
  296.9 1.4 copy-start.10
  303.9 1.3 copy-start.6
  306.2 42.4 %all-to-all-start.1 = ((bf16[8,128,1536]{2,1,0:T(8,128)(2,1)}), bf16[8,128,1536]{2,1,0:T(8,128)(2,1)S(1)}, u32[]{:S(2)}, u32[]{:S(2)}) async-start(bf16[8,128,1536]{2,1,0:T(8,128)(2,1)} %attend_grad.3), calls=%async_computation.1 | async-start | bytes 6291456 | tf_op jit(solution)/shard_map/all_to_all | solution.py:499
  320.3 54.0 %collective-permute-start.13 = (bf16[512,2048]{1,0:T(8,128)(2,1)}, bf16[512,2048]{1,0:T(8,128)(2,1)}, u32[]{:S(2)}, u32[]{:S(2)}) collective-permute-start(bf16[512,2048]{1,0:T(8,128)(2,1)} %copy-done.10), channel_id=1, source_target_pairs={{0,1},{1,0},{2,3},{3,2},{4,5},{5,4},{6,7},{7,6},{8,9},{9,8},{10,11... | collective-permute-start | bytes 6291464 | tf_op jit(solution)/shard_map/ppermute | solution.py:296
  329.4 1.6 copy-start.5
  333.8 43.0 %collective-permute-start.15 = (bf16[512,2048]{1,0:T(8,128)(2,1)}, bf16[512,2048]{1,0:T(8,128)(2,1)}, u32[]{:S(2)}, u32[]{:S(2)}) collective-permute-start(bf16[512,2048]{1,0:T(8,128)(2,1)} %sum_of.12), channel_id=1, source_target_pairs={{1,2},{2,1},{5,6},{6,5},{9,10},{10,9},{13,14},{14,13},{17,18},{18,... | collective-permute-start | bytes 6291464 | tf_op jit(solution)/shard_map/ppermute | solution.py:296
  348.6 25.6 %copy-start.7 = (bf16[512,2048]{1,0:T(8,128)(2,1)S(1)}, bf16[512,2048]{1,0:T(8,128)(2,1)}, u32[]{:S(2)}) copy-start(bf16[512,2048]{1,0:T(8,128)(2,1)} %copy-done.6) | copy-start | bytes 6291460
Sparse Core Ops, SparseCore 0:
  135.6 74.5 all-gather.1
